TPU v7x, 32 devices: a whole 2x2x4 slice. The times are simulated.
32 devices in a mesh: dp: 4 (over x, core), seq: 8 (over z, y).
Axes of the slice: x: 2, y: 2, z: 4, core: 2. Of those that a mesh axis runs over, the one named last changes fastest.
Arguments:
- hidden_in: bfloat16 [32, 2048, 576], P('dp', 'seq'), may hold values from -6 to 6
- span_order: int32 [16], replicated, may hold values from 0 to 15, each once
- attn_gain: bfloat16 [576], replicated, may hold values from 0.099609375 to 1.8984375
- q_weight: bfloat16 [576, 576], P('dp', 'seq'), may hold values from -0.25 to 0.25
- k_weight: bfloat16 [576, 192], P('dp', 'seq'), may hold values from -0.25 to 0.25
- v_weight: bfloat16 [576, 192], P('dp', 'seq'), may hold values from -0.25 to 0.25
- o_weight: bfloat16 [576, 576], P('dp', 'seq'), may hold values from -1.5 to 1.5
- mlp_gain: bfloat16 [576], replicated, may hold values from 0.099609375 to 1.8984375
- gate_weight: bfloat16 [576, 1536], P('dp', 'seq'), may hold values from -0.25 to 0.25
- up_weight: bfloat16 [576, 1536], P('dp', 'seq'), may hold values from -0.25 to 0.25
- down_weight: bfloat16 [1536, 576], P('dp', 'seq'), may hold values from -0.15625 to 0.15625
- out_grad: bfloat16 [32, 2048, 576], P('dp', 'seq'), may hold values from -6 to 6
Outputs:
- hidden_out: bfloat16 [32, 2048, 576], P('dp', 'seq')
- grad_in: float32 [32, 2048, 576], P('dp', 'seq')
- attn_gain_grad: float32 [576], replicated
- q_weight_grad: float32 [576, 576], P('dp', 'seq')
- k_weight_grad: float32 [576, 192], P('dp', 'seq')
- v_weight_grad: float32 [576, 192], P('dp', 'seq')
- o_weight_grad: float32 [576, 576], P('dp', 'seq')
- mlp_gain_grad: float32 [576], replicated
- gate_weight_grad: float32 [576, 1536], P('dp', 'seq')
- up_weight_grad: float32 [576, 1536], P('dp', 'seq')
- down_weight_grad: float32 [1536, 576], P('dp', 'seq')
Inputs may be any that keep to these rules, and one draw needn't show every extreme that they name: `span_order`: every span number appears exactly once; the same order holds for every sequence.
All inputs are finite; a program needn't handle non-finite values.
Results may differ from a plain program's by a relative error of at most 0.02.
Values may be sent and summed in bfloat16 or wider, within the bound.
A program may use at most 256 MiB of HBM per device.

v0:
```python
import jax
import jax.numpy as jnp
from jax import lax
from jax.sharding import PartitionSpec as P

HD = 64
MICRO = 2


eps_norm = 1e-05
rope_base = 100000.0
neg_big = -1e30


def slot_positions(slot_ids, span_order, span_len):
    span_ids = slot_ids // span_len
    span_hits = span_ids[:, None] == jnp.arange(span_order.shape[0], dtype=jnp.int32)[None, :]
    starts = jnp.sum(jnp.where(span_hits, span_order[None, :], 0), axis=1)
    return starts * span_len + slot_ids % span_len


def rope_tables(slot_pos):
    half_width = HD // 2
    inv_freq = rope_base ** (-(jnp.arange(half_width, dtype=jnp.float32) * 2.0) / HD)
    angles = slot_pos.astype(jnp.float32)[:, None] * inv_freq[None, :]
    cosine = jnp.concatenate([jnp.cos(angles), jnp.cos(angles)], axis=1)
    sine_tab = jnp.concatenate([jnp.sin(angles), jnp.sin(angles)], axis=1)
    return (cosine[:, None, :], sine_tab[:, None, :])


def rotate(vector, cosine, sine_tab):
    half_width = vector.shape[-1] // 2
    turned = jnp.concatenate([-vector[..., half_width:], vector[..., :half_width]], axis=-1)
    return vector * cosine + turned * sine_tab


def rotate_back(grad_out, cosine, sine_tab):
    half_width = grad_out.shape[-1] // 2
    scaled = grad_out * sine_tab
    turned = jnp.concatenate([scaled[..., half_width:], -scaled[..., :half_width]], axis=-1)
    return grad_out * cosine + turned


def norm_back(vector, rstd_vec, gain_vec, grad_n):
    scaled = grad_n * gain_vec
    gain_term = jnp.sum(grad_n * vector * rstd_vec, axis=0)
    grad_vec = rstd_vec * scaled - vector * rstd_vec**3 * jnp.mean(
        scaled * vector, axis=-1, keepdims=True
    )
    return (grad_vec, gain_term)


def add_tuples(old_sums, new_terms):
    if old_sums is None:
        return tuple(new_terms)
    return tuple((old_sum + new_term for old_sum, new_term in zip(old_sums, new_terms)))


def shards(
    hidden_in,
    span_order,
    attn_gain,
    q_weight,
    k_weight,
    v_weight,
    o_weight,
    mlp_gain,
    gate_weight,
    up_weight,
    down_weight,
    out_grad,
):
    local_seqs, row_count, model_width = hidden_in.shape
    seq_parts = lax.axis_size("seq")
    full_length = row_count * seq_parts
    span_len = full_length // (2 * seq_parts)
    per_micro = local_seqs // MICRO
    kv_width = k_weight.shape[1] * seq_parts
    kv_heads = kv_width // HD
    head_count = model_width // HD
    group_size = head_count // kv_heads
    tok_count = per_micro * row_count
    score_scale = HD ** (-0.5)
    own_slots = lax.axis_index("seq") * row_count + jnp.arange(row_count, dtype=jnp.int32)
    own_pos = slot_positions(own_slots, span_order, span_len)
    all_pos = slot_positions(jnp.arange(full_length, dtype=jnp.int32), span_order, span_len)
    allowed = own_pos[:, None] >= all_pos[None, :]
    cos_own, sin_own = rope_tables(own_pos)
    gain_attn = attn_gain.astype(jnp.float32)
    gain_mlp = mlp_gain.astype(jnp.float32)

    def attend(inputs):
        queries, key_rows, value_rows = inputs
        query_grp = queries.reshape(row_count, kv_heads, group_size, HD)
        key_grp = key_rows.reshape(full_length, kv_heads, HD)
        value_grp = value_rows.reshape(full_length, kv_heads, HD)
        scores = (
            jnp.einsum("rkgd,lkd->kgrl", query_grp, key_grp, preferred_element_type=jnp.float32)
            * score_scale
        )
        scores = jnp.where(allowed, scores, neg_big)
        row_peak = jnp.max(scores, axis=-1, keepdims=True)
        exp_scores = jnp.exp(scores - row_peak)
        row_total = jnp.sum(exp_scores, axis=-1, keepdims=True)
        attn_probs = exp_scores / row_total
        log_total = row_peak + jnp.log(row_total)
        mixed = jnp.einsum(
            "kgrl,lkd->rkgd",
            attn_probs.astype(jnp.bfloat16),
            value_grp,
            preferred_element_type=jnp.float32,
        )
        return (mixed.astype(jnp.bfloat16).reshape(row_count, model_width), log_total)

    def attend_back(inputs):
        queries, key_rows, value_rows, grad_mix, log_total = inputs
        query_grp = queries.reshape(row_count, kv_heads, group_size, HD)
        key_grp = key_rows.reshape(full_length, kv_heads, HD)
        value_grp = value_rows.reshape(full_length, kv_heads, HD)
        grad_grp = grad_mix.reshape(row_count, kv_heads, group_size, HD)
        scores = (
            jnp.einsum("rkgd,lkd->kgrl", query_grp, key_grp, preferred_element_type=jnp.float32)
            * score_scale
        )
        scores = jnp.where(allowed, scores, neg_big)
        attn_probs = jnp.exp(scores - log_total)
        probs_low = attn_probs.astype(jnp.bfloat16)
        grad_probs = jnp.einsum(
            "rkgd,lkd->kgrl", grad_grp, value_grp, preferred_element_type=jnp.float32
        )
        row_delta = jnp.sum(attn_probs * grad_probs, axis=-1, keepdims=True)
        grad_scores = (attn_probs * (grad_probs - row_delta)).astype(jnp.bfloat16)
        grad_query_rot = (
            jnp.einsum("kgrl,lkd->rkgd", grad_scores, key_grp, preferred_element_type=jnp.float32)
            * score_scale
        )
        key_term = (
            jnp.einsum("kgrl,rkgd->lkd", grad_scores, query_grp, preferred_element_type=jnp.float32)
            * score_scale
        )
        value_term = jnp.einsum(
            "kgrl,rkgd->lkd", probs_low, grad_grp, preferred_element_type=jnp.float32
        )
        return (
            grad_query_rot.reshape(row_count, head_count, HD),
            key_term.reshape(full_length, kv_width),
            value_term.reshape(full_length, kv_width),
        )

    outputs = []
    in_grads = []
    totals = None
    for micro_idx in range(MICRO):
        first_seq = micro_idx * per_micro
        block_in = hidden_in[first_seq : first_seq + per_micro]
        block_grad = out_grad[first_seq : first_seq + per_micro]
        col_parts = (
            lax.all_gather(q_weight, "seq", axis=1, tiled=True),
            lax.all_gather(k_weight, "seq", axis=1, tiled=True),
            lax.all_gather(v_weight, "seq", axis=1, tiled=True),
            lax.all_gather(o_weight, "seq", axis=1, tiled=True),
            lax.all_gather(gate_weight, "seq", axis=1, tiled=True),
            lax.all_gather(up_weight, "seq", axis=1, tiled=True),
            lax.all_gather(down_weight, "seq", axis=1, tiled=True),
        )
        query_mat, key_mat, value_mat, out_mat, gate_mat, up_mat, down_mat = (
            lax.all_gather(col_parts[0], "dp", axis=0, tiled=True),
            lax.all_gather(col_parts[1], "dp", axis=0, tiled=True),
            lax.all_gather(col_parts[2], "dp", axis=0, tiled=True),
            lax.all_gather(col_parts[3], "dp", axis=0, tiled=True),
            lax.all_gather(col_parts[4], "dp", axis=0, tiled=True),
            lax.all_gather(col_parts[5], "dp", axis=0, tiled=True),
            lax.all_gather(col_parts[6], "dp", axis=0, tiled=True),
        )
        resid_in = block_in.astype(jnp.float32).reshape(tok_count, model_width)
        rstd_one = lax.rsqrt(jnp.mean(resid_in * resid_in, axis=-1, keepdims=True) + eps_norm)
        normed_one = (resid_in * rstd_one * gain_attn).astype(jnp.bfloat16)
        query_lin = jnp.dot(normed_one, query_mat, preferred_element_type=jnp.float32)
        key_lin = jnp.dot(normed_one, key_mat, preferred_element_type=jnp.float32)
        value_lin = jnp.dot(normed_one, value_mat, preferred_element_type=jnp.float32)
        query_rot = rotate(
            query_lin.reshape(per_micro, row_count, head_count, HD), cos_own, sin_own
        ).astype(jnp.bfloat16)
        key_rot = (
            rotate(key_lin.reshape(per_micro, row_count, kv_heads, HD), cos_own, sin_own)
            .astype(jnp.bfloat16)
            .reshape(per_micro, row_count, kv_width)
        )
        value_low = value_lin.astype(jnp.bfloat16).reshape(per_micro, row_count, kv_width)
        key_all, value_all = (
            lax.all_gather(key_rot, "seq", axis=1, tiled=True),
            lax.all_gather(value_low, "seq", axis=1, tiled=True),
        )
        mixed_seq, log_total = lax.map(attend, (query_rot, key_all, value_all))
        mixed_low = mixed_seq.reshape(tok_count, model_width)
        hidden_mid = resid_in + jnp.dot(mixed_low, out_mat, preferred_element_type=jnp.float32)
        rstd_two = lax.rsqrt(jnp.mean(hidden_mid * hidden_mid, axis=-1, keepdims=True) + eps_norm)
        normed_two = (hidden_mid * rstd_two * gain_mlp).astype(jnp.bfloat16)
        gate_lin = jnp.dot(normed_two, gate_mat, preferred_element_type=jnp.float32)
        up_lin = jnp.dot(normed_two, up_mat, preferred_element_type=jnp.float32)
        gate_sig = jax.nn.sigmoid(gate_lin)
        inner_low = (gate_lin * gate_sig * up_lin).astype(jnp.bfloat16)
        mlp_out = jnp.dot(inner_low, down_mat, preferred_element_type=jnp.float32)
        outputs.append(
            (hidden_mid + mlp_out).astype(jnp.bfloat16).reshape(per_micro, row_count, model_width)
        )
        col_again = (
            lax.all_gather(q_weight, "seq", axis=1, tiled=True),
            lax.all_gather(k_weight, "seq", axis=1, tiled=True),
            lax.all_gather(v_weight, "seq", axis=1, tiled=True),
            lax.all_gather(o_weight, "seq", axis=1, tiled=True),
            lax.all_gather(gate_weight, "seq", axis=1, tiled=True),
            lax.all_gather(up_weight, "seq", axis=1, tiled=True),
            lax.all_gather(down_weight, "seq", axis=1, tiled=True),
        )
        query_mat, key_mat, value_mat, out_mat, gate_mat, up_mat, down_mat = (
            lax.all_gather(col_again[0], "dp", axis=0, tiled=True),
            lax.all_gather(col_again[1], "dp", axis=0, tiled=True),
            lax.all_gather(col_again[2], "dp", axis=0, tiled=True),
            lax.all_gather(col_again[3], "dp", axis=0, tiled=True),
            lax.all_gather(col_again[4], "dp", axis=0, tiled=True),
            lax.all_gather(col_again[5], "dp", axis=0, tiled=True),
            lax.all_gather(col_again[6], "dp", axis=0, tiled=True),
        )
        key_all, value_all = (
            lax.all_gather(key_rot, "seq", axis=1, tiled=True),
            lax.all_gather(value_low, "seq", axis=1, tiled=True),
        )
        grad_top = block_grad.astype(jnp.float32).reshape(tok_count, model_width)
        grad_top_low = grad_top.astype(jnp.bfloat16)
        down_term = jnp.einsum(
            "tf,td->fd", inner_low, grad_top_low, preferred_element_type=jnp.float32
        )
        grad_inner = jnp.einsum(
            "td,fd->tf", grad_top_low, down_mat, preferred_element_type=jnp.float32
        )
        grad_gate = (grad_inner * up_lin * gate_sig * (1.0 + gate_lin * (1.0 - gate_sig))).astype(
            jnp.bfloat16
        )
        grad_up = (grad_inner * gate_lin * gate_sig).astype(jnp.bfloat16)
        gate_term = jnp.einsum(
            "td,tf->df", normed_two, grad_gate, preferred_element_type=jnp.float32
        )
        up_term = jnp.einsum("td,tf->df", normed_two, grad_up, preferred_element_type=jnp.float32)
        grad_normed_two = jnp.einsum(
            "tf,df->td", grad_gate, gate_mat, preferred_element_type=jnp.float32
        ) + jnp.einsum("tf,df->td", grad_up, up_mat, preferred_element_type=jnp.float32)
        grad_mid_norm, gain_mlp_term = norm_back(hidden_mid, rstd_two, gain_mlp, grad_normed_two)
        grad_mid = grad_top + grad_mid_norm
        grad_mid_low = grad_mid.astype(jnp.bfloat16)
        out_term = jnp.einsum(
            "td,te->de", mixed_low, grad_mid_low, preferred_element_type=jnp.float32
        )
        grad_mixed = jnp.einsum(
            "te,de->td", grad_mid_low, out_mat, preferred_element_type=jnp.float32
        ).astype(jnp.bfloat16)
        grad_query_rot, key_terms, value_terms = lax.map(
            attend_back,
            (
                query_rot,
                key_all,
                value_all,
                grad_mixed.reshape(per_micro, row_count, model_width),
                log_total,
            ),
        )
        key_share, value_share = (
            lax.psum_scatter(key_terms, "seq", scatter_dimension=1, tiled=True),
            lax.psum_scatter(value_terms, "seq", scatter_dimension=1, tiled=True),
        )
        grad_query = (
            rotate_back(grad_query_rot, cos_own, sin_own)
            .astype(jnp.bfloat16)
            .reshape(tok_count, model_width)
        )
        grad_key = (
            rotate_back(key_share.reshape(per_micro, row_count, kv_heads, HD), cos_own, sin_own)
            .astype(jnp.bfloat16)
            .reshape(tok_count, kv_width)
        )
        grad_value = value_share.astype(jnp.bfloat16).reshape(tok_count, kv_width)
        query_term = jnp.einsum(
            "td,te->de", normed_one, grad_query, preferred_element_type=jnp.float32
        )
        key_term = jnp.einsum("td,te->de", normed_one, grad_key, preferred_element_type=jnp.float32)
        value_term = jnp.einsum(
            "td,te->de", normed_one, grad_value, preferred_element_type=jnp.float32
        )
        grad_normed_one = (
            jnp.einsum("te,de->td", grad_query, query_mat, preferred_element_type=jnp.float32)
            + jnp.einsum("te,de->td", grad_key, key_mat, preferred_element_type=jnp.float32)
            + jnp.einsum("te,de->td", grad_value, value_mat, preferred_element_type=jnp.float32)
        )
        grad_in_norm, gain_attn_term = norm_back(resid_in, rstd_one, gain_attn, grad_normed_one)
        in_grads.append((grad_mid + grad_in_norm).reshape(per_micro, row_count, model_width))
        totals = add_tuples(
            totals,
            (
                query_term,
                key_term,
                value_term,
                out_term,
                gate_term,
                up_term,
                down_term,
                gain_attn_term,
                gain_mlp_term,
            ),
        )
    col_sums = (
        lax.psum_scatter(
            totals[0].astype(jnp.bfloat16), "seq", scatter_dimension=1, tiled=True
        ).astype(jnp.float32),
        lax.psum_scatter(
            totals[1].astype(jnp.bfloat16), "seq", scatter_dimension=1, tiled=True
        ).astype(jnp.float32),
        lax.psum_scatter(
            totals[2].astype(jnp.bfloat16), "seq", scatter_dimension=1, tiled=True
        ).astype(jnp.float32),
        lax.psum_scatter(
            totals[3].astype(jnp.bfloat16), "seq", scatter_dimension=1, tiled=True
        ).astype(jnp.float32),
        lax.psum_scatter(
            totals[4].astype(jnp.bfloat16), "seq", scatter_dimension=1, tiled=True
        ).astype(jnp.float32),
        lax.psum_scatter(
            totals[5].astype(jnp.bfloat16), "seq", scatter_dimension=1, tiled=True
        ).astype(jnp.float32),
        lax.psum_scatter(
            totals[6].astype(jnp.bfloat16), "seq", scatter_dimension=1, tiled=True
        ).astype(jnp.float32),
    )
    owned = (
        lax.psum_scatter(
            col_sums[0].astype(jnp.bfloat16), "dp", scatter_dimension=0, tiled=True
        ).astype(jnp.float32),
        lax.psum_scatter(
            col_sums[1].astype(jnp.bfloat16), "dp", scatter_dimension=0, tiled=True
        ).astype(jnp.float32),
        lax.psum_scatter(
            col_sums[2].astype(jnp.bfloat16), "dp", scatter_dimension=0, tiled=True
        ).astype(jnp.float32),
        lax.psum_scatter(
            col_sums[3].astype(jnp.bfloat16), "dp", scatter_dimension=0, tiled=True
        ).astype(jnp.float32),
        lax.psum_scatter(
            col_sums[4].astype(jnp.bfloat16), "dp", scatter_dimension=0, tiled=True
        ).astype(jnp.float32),
        lax.psum_scatter(
            col_sums[5].astype(jnp.bfloat16), "dp", scatter_dimension=0, tiled=True
        ).astype(jnp.float32),
        lax.psum_scatter(
            col_sums[6].astype(jnp.bfloat16), "dp", scatter_dimension=0, tiled=True
        ).astype(jnp.float32),
    )
    gain_sums = lax.psum((totals[7], totals[8]), ("dp", "seq"))
    return (
        jnp.concatenate(outputs, axis=0),
        jnp.concatenate(in_grads, axis=0),
        gain_sums[0],
        owned[0],
        owned[1],
        owned[2],
        owned[3],
        gain_sums[1],
        owned[4],
        owned[5],
        owned[6],
    )


def solution(mesh):
    placed = (
        P("dp", "seq", None),
        P(),
        P(),
        P("dp", "seq"),
        P("dp", "seq"),
        P("dp", "seq"),
        P("dp", "seq"),
        P(),
        P("dp", "seq"),
        P("dp", "seq"),
        P("dp", "seq"),
        P("dp", "seq", None),
    )
    return jax.shard_map(
        shards,
        mesh=mesh,
        in_specs=placed,
        out_specs=(
            P("dp", "seq", None),
            P("dp", "seq", None),
            P(),
            P("dp", "seq"),
            P("dp", "seq"),
            P("dp", "seq"),
            P("dp", "seq"),
            P(),
            P("dp", "seq"),
            P("dp", "seq"),
            P("dp", "seq"),
        ),
        check_vma=False,
    )
```

profile of v0, /device:TPU:0, one launch (start us, length us, event | category | flops | bytes accessed | tf_op | source)
XLA Modules:
  0.0 2132.1 jit_solution(3242470169576736334)
XLA Ops:
  11.0 32.3 %all_gather.39 = bf16[144,192]{0,1:T(8,128)(2,1)S(1)} all-gather(bf16[144,24]{0,1:T(8,128)(2,1)S(1)} %copy-done.88), channel_id=1, replica_groups=mesh['dp'=4,'seq'=8] {'seq'}, dimensions={1}, use_global_device_ids=true | all-gather | bytes 62208 | tf_op jit(solution)/shard_map/all_gather | solution.py:159
  52.6 30.9 %all_gather.36 = bf16[144,192]{0,1:T(8,128)(2,1)S(1)} all-gather(bf16[144,24]{0,1:T(8,128)(2,1)S(1)} %copy-done.89), channel_id=1, replica_groups=mesh['dp'=4,'seq'=8] {'seq'}, dimensions={1}, use_global_device_ids=true | all-gather | bytes 62208 | tf_op jit(solution)/shard_map/all_gather | solution.py:160
  98.8 32.9 %all-gather.1 = bf16[8,192,144]{1,2,0:T(8,128)(2,1)S(1)} all-gather(bf16[1,192,144]{1,2,0:T(8,128)(2,1)S(1)} %bitcast.660), channel_id=1, replica_groups=mesh['dp'=4,'seq'=8] {'seq'}, dimensions={0}, use_global_device_ids=true | all-gather | bytes 497664 | tf_op jit(solution)/shard_map/all_gather | solution.py:163
  133.2 33.0 %all-gather = bf16[8,192,144]{1,2,0:T(8,128)(2,1)S(1)} all-gather(bf16[1,192,144]{1,2,0:T(8,128)(2,1)S(1)} %bitcast.661), channel_id=1, replica_groups=mesh['dp'=4,'seq'=8] {'seq'}, dimensions={0}, use_global_device_ids=true | all-gather | bytes 497664 | tf_op jit(solution)/shard_map/all_gather | solution.py:162
  167.8 34.4 %all_gather.50 = bf16[384,576]{0,1:T(8,128)(2,1)} all-gather(bf16[384,72]{0,1:T(8,128)(2,1)S(1)} %copy-done.75), channel_id=1, replica_groups=mesh['dp'=4,'seq'=8] {'seq'}, dimensions={1}, use_global_device_ids=true | all-gather | bytes 497664 | tf_op jit(solution)/shard_map/all_gather | solution.py:164
  203.0 31.5 %all_gather.42 = bf16[144,576]{0,1:T(8,128)(2,1)S(1)} all-gather(bf16[144,72]{0,1:T(8,128)(2,1)S(1)} %copy.198), channel_id=1, replica_groups=mesh['dp'=4,'seq'=8] {'seq'}, dimensions={1}, use_global_device_ids=true | all-gather | bytes 186624 | tf_op jit(solution)/shard_map/all_gather | solution.py:158
  253.8 31.7 %all_gather.44 = bf16[144,576]{0,1:T(8,128)(2,1)S(1)} all-gather(bf16[144,72]{0,1:T(8,128)(2,1)S(1)} %copy.202), channel_id=1, replica_groups=mesh['dp'=4,'seq'=8] {'seq'}, dimensions={1}, use_global_device_ids=true | all-gather | bytes 186624 | tf_op jit(solution)/shard_map/all_gather | solution.py:161
  305.4 120.4 %while.56 = (s32[]{:T(128)}, bf16[4,256,576]{1,2,0:T(8,128)(2,1)}, f32[4,3,3,256,1]{3,2,1,4,0:T(4,128)S(1)}, bf16[4,2048,192]{1,2,0:T(8,128)(2,1)}, bf16[4,2048,...) while((s32[]{:T(128)}, bf16[4,256,576]{1,2,0:T(8,128)(2,1)}, ...), condition=%wide.region_6.7_spmd.clone, body=%wide.region_3.6_spmd.clone.sunk | while | flops 1265252096 | bytes 65300596 | solution.py:194
  427.5 123.7 %while.57 = (s32[]{:T(128)}, bf16[4,256,576]{1,2,0:T(8,128)(2,1)}, f32[4,3,3,256,1]{3,2,1,4,0:T(4,128)S(1)}, bf16[4,2048,192]{1,2,0:T(8,128)(2,1)}, bf16[4,2048,...) while((s32[]{:T(128)}, bf16[4,256,576]{1,2,0:T(8,128)(2,1)}, ...), condition=%wide.region_12.13_spmd.clone, body=%wide.region_9.12_spmd.clone.sunk | while | flops 1265252096 | bytes 65300596 | solution.py:194
  631.1 214.8 %while.58 = (s32[]{:T(128)}, f32[4,256,9,64]{1,3,2,0:T(8,128)S(1)}, f32[4,2048,192]{1,2,0:T(8,128)}, f32[4,2048,192]{1,2,0:T(8,128)}, bf16[4,2048,192]{1,2,0:T(8...) while((s32[]{:T(128)}, f32[4,256,9,64]{1,3,2,0:T(8,128)S(1)}, ...), condition=%wide.region_17.18_spmd.clone, body=%wide.region_15.17_spmd.clone.sunk | while | flops 3091740416 | bytes 162799776 | solution.py:257
  854.3 218.5 %while.59 = (s32[]{:T(128)}, f32[4,256,9,64]{1,3,2,0:T(8,128)S(1)}, f32[4,2048,192]{1,2,0:T(8,128)}, f32[4,2048,192]{1,2,0:T(8,128)}, bf16[4,2048,192]{1,2,0:T(8...) while((s32[]{:T(128)}, f32[4,256,9,64]{1,3,2,0:T(8,128)S(1)}, ...), condition=%wide.region_24.25_spmd.clone, body=%wide.region_22.24_spmd.clone.sunk | while | flops 3091740416 | bytes 162799776 | solution.py:257
  1111.6 34.1 %reduce-scatter.69.cloned.1.call-done = bf16[576,72]{0,1:T(8,128)(2,1)} async-done(((bf16[576,576]{0,1:T(8,128)(2,1)}), bf16[576,72]{0,1:T(8,128)(2,1)}) %reduce-scatter.69.cloned.1.call-update) | async-done | bytes 82960
  1147.4 67.5 %reduce-scatter.51.cloned.1.call-done = bf16[576,192]{0,1:T(8,128)(2,1)} async-done(((bf16[576,1536]{0,1:T(8,128)(2,1)}), bf16[576,192]{0,1:T(8,128)(2,1)}) %reduce-scatter.51.cloned.1.call-update) | async-done | bytes 221200 | tf_op jit(solution)/shard_map/reduce_scatter | solution.py:326
  1216.9 67.8 %reduce-scatter.49.cloned.1.call-done = bf16[576,192]{0,1:T(8,128)(2,1)} async-done(((bf16[576,1536]{0,1:T(8,128)(2,1)}), bf16[576,192]{0,1:T(8,128)(2,1)}) %reduce-scatter.49.cloned.1.call-update) | async-done | bytes 221200 | tf_op jit(solution)/shard_map/reduce_scatter | solution.py:323
  1286.6 66.6 %reduce-scatter.53.cloned.1.call-done = bf16[1536,72]{0,1:T(8,128)(2,1)} async-done(((bf16[1536,576]{0,1:T(8,128)(2,1)}), bf16[1536,72]{0,1:T(8,128)(2,1)}) %reduce-scatter.53.cloned.1.call-update) | async-done | bytes 221200 | tf_op jit(solution)/shard_map/reduce_scatter | solution.py:329
  1399.2 21.2 reduce-scatter.65.cloned.1.call-done
  1444.8 21.6 %reduce-scatter.67.cloned.1.call-done = bf16[384,72]{1,0:T(8,128)(2,1)} async-done(((bf16[1536,72]{1,0:T(8,128)(2,1)}), bf16[384,72]{1,0:T(8,128)(2,1)}) %reduce-scatter.67.cloned.1.call-update) | async-done | bytes 55312
  1468.0 120.7 %reduce-scatter.43.cloned.1.call-done = f32[4,256,192]{1,2,0:T(8,128)} async-done(((f32[4,2048,192]{1,2,0:T(8,128)}), f32[4,256,192]{1,2,0:T(8,128)}) %reduce-scatter.43.cloned.1.call-update) | async-done | bytes 786448 | tf_op jit(solution)/shard_map/reduce_scatter | solution.py:269
  1590.7 119.6 %reduce-scatter.41.cloned.1.call-done = f32[4,256,192]{1,2,0:T(8,128)} async-done(((f32[4,2048,192]{1,2,0:T(8,128)}), f32[4,256,192]{1,2,0:T(8,128)}) %reduce-scatter.41.cloned.1.call-update) | async-done | bytes 786448 | tf_op jit(solution)/shard_map/reduce_scatter | solution.py:268
  1712.4 119.3 %reduce-scatter.47.cloned.1.call-done = f32[4,256,192]{1,2,0:T(8,128)} async-done(((f32[4,2048,192]{1,2,0:T(8,128)}), f32[4,256,192]{1,2,0:T(8,128)}) %reduce-scatter.47.cloned.1.call-update) | async-done | bytes 786448 | tf_op jit(solution)/shard_map/reduce_scatter | solution.py:269
  1837.1 116.3 %reduce-scatter.45.cloned.1.call-done = f32[4,256,192]{1,2,0:T(8,128)} async-done(((f32[4,2048,192]{1,2,0:T(8,128)}), f32[4,256,192]{1,2,0:T(8,128)}) %reduce-scatter.45.cloned.1.call-update) | async-done | bytes 786448 | tf_op jit(solution)/shard_map/reduce_scatter | solution.py:268
  1973.9 41.0 %reduce-scatter.73.cloned.1.call-done = bf16[576,24]{0,1:T(8,128)(2,1)} async-done(((bf16[576,192]{0,1:T(8,128)(2,1)}), bf16[576,24]{0,1:T(8,128)(2,1)}) %reduce-scatter.73.cloned.1.call-update) | async-done | bytes 27664
  2024.6 51.7 %reduce-scatter.71.cloned.1.call-done = bf16[576,24]{0,1:T(8,128)(2,1)} async-done(((bf16[576,192]{0,1:T(8,128)(2,1)}), bf16[576,24]{0,1:T(8,128)(2,1)}) %reduce-scatter.71.cloned.1.call-update) | async-done | bytes 27664
  2082.0 40.2 %all-reduce.4 = (f32[576]{0:T(1024)}, f32[576]{0:T(1024)}) all-reduce(f32[576]{0:T(1024)S(1)} %add.357, f32[576]{0:T(1024)S(1)} %add.364), channel_id=1, replica_groups=mesh['dp'=4,'seq'=8] {'dp','seq'}, use_global_device_ids=true, to_apply=%region_30.31 | all-reduce | flops 1152 | bytes 9216 | tf_op jit(solution)/shard_map/psum | solution.py:356
  (624 shorter events, 1000.0 us)
Async XLA Ops:
  7.2 297.1 %all-gather.12.cloned.1.call-start = ((), (), s32[]{:S(2)}) async-start(), calls=%async_computation.19 | async-start | bytes 3538944 | tf_op jit(solution)/shard_map/all_gather | solution.py:191
  52.5 251.8 %all-gather.10.cloned.1.call-start = ((), (), s32[]{:S(2)}) async-start(), calls=%async_computation.18 | async-start | bytes 3538944 | tf_op jit(solution)/shard_map/all_gather | solution.py:192
  93.0 332.8 %all-gather.22.cloned.1.call-start = ((), (), s32[]{:S(2)}) async-start(), calls=%async_computation.24 | async-start | bytes 3538944 | tf_op jit(solution)/shard_map/all_gather | solution.py:191
  93.7 332.1 %all-gather.20.cloned.1.call-start = ((), (), s32[]{:S(2)}) async-start(), calls=%async_computation.23 | async-start | bytes 3538944 | tf_op jit(solution)/shard_map/all_gather | solution.py:192
  98.7 462.5 %all-gather.16.cloned.1.call-start = ((), (), s32[]{:S(2)}) async-start(), calls=%async_computation.21 | async-start | bytes 2211840 | tf_op jit(solution)/shard_map/all_gather | solution.py:172
  133.2 435.1 %all-gather.14.cloned.1.call-start = ((), (), s32[]{:S(2)}) async-start(), calls=%async_computation.20 | async-start | bytes 2211840 | tf_op jit(solution)/shard_map/all_gather | solution.py:171
  167.7 407.7 %all-gather.18.cloned.1.call-start = ((), (), s32[]{:S(2)}) async-start(), calls=%async_computation.22 | async-start | bytes 2211840 | tf_op jit(solution)/shard_map/all_gather | solution.py:173
  202.2 907.6 %reduce-scatter.75.cloned.1.call-start = ((), (), s32[]{:S(2)}) async-start(), calls=%async_computation.42 | async-start | bytes 829440
  622.9 522.8 %reduce-scatter.69.cloned.1.call-start = ((), (), s32[]{:S(2)}) async-start(), calls=%async_computation.39 | async-start | bytes 829440
  1084.3 130.7 %reduce-scatter.51.cloned.1.call-start = ((), (), s32[]{:S(2)}) async-start(), calls=%async_computation.30 | async-start | bytes 2211840 | tf_op jit(solution)/shard_map/reduce_scatter | solution.py:326
  1093.2 191.5 %reduce-scatter.49.cloned.1.call-start = ((), (), s32[]{:S(2)}) async-start(), calls=%async_computation.29 | async-start | bytes 2211840 | tf_op jit(solution)/shard_map/reduce_scatter | solution.py:323
  1102.4 250.8 %reduce-scatter.53.cloned.1.call-start = ((), (), s32[]{:S(2)}) async-start(), calls=%async_computation.31 | async-start | bytes 1990656 | tf_op jit(solution)/shard_map/reduce_scatter | solution.py:329
  1109.8 266.0 %reduce-scatter.61.cloned.1.call-start = ((), (), s32[]{:S(2)}) async-start(), calls=%async_computation.35 | async-start | bytes 184320
  1111.6 286.0 %reduce-scatter.55.cloned.1.call-start = ((), (), s32[]{:S(2)}) async-start(), calls=%async_computation.32 | async-start | bytes 184320
  1147.4 273.0 %reduce-scatter.65.cloned.1.call-start = ((), (), s32[]{:S(2)}) async-start(), calls=%async_computation.37 | async-start | bytes 368640
  1216.8 226.2 %reduce-scatter.63.cloned.1.call-start = ((), (), s32[]{:S(2)}) async-start(), calls=%async_computation.36 | async-start | bytes 368640
  1286.5 179.9 %reduce-scatter.67.cloned.1.call-start = ((), (), s32[]{:S(2)}) async-start(), calls=%async_computation.38 | async-start | bytes 491520
  1355.1 233.6 %reduce-scatter.43.cloned.1.call-start = ((), (), s32[]{:S(2)}) async-start(), calls=%async_computation.26 | async-start | bytes 7077888 | tf_op jit(solution)/shard_map/reduce_scatter | solution.py:269
  1355.6 354.7 %reduce-scatter.41.cloned.1.call-start = ((), (), s32[]{:S(2)}) async-start(), calls=%async_computation.25 | async-start | bytes 7077888 | tf_op jit(solution)/shard_map/reduce_scatter | solution.py:268
  1356.4 475.4 %reduce-scatter.47.cloned.1.call-start = ((), (), s32[]{:S(2)}) async-start(), calls=%async_computation.28 | async-start | bytes 7077888 | tf_op jit(solution)/shard_map/reduce_scatter | solution.py:269
  1357.0 596.4 %reduce-scatter.45.cloned.1.call-start = ((), (), s32[]{:S(2)}) async-start(), calls=%async_computation.27 | async-start | bytes 7077888 | tf_op jit(solution)/shard_map/reduce_scatter | solution.py:268
  1357.7 657.2 %reduce-scatter.73.cloned.1.call-start = ((), (), s32[]{:S(2)}) async-start(), calls=%async_computation.41 | async-start | bytes 276480
  1837.0 239.2 %reduce-scatter.71.cloned.1.call-start = ((), (), s32[]{:S(2)}) async-start(), calls=%async_computation.40 | async-start | bytes 276480
  1963.3 158.9 %reduce-scatter.59.cloned.1.call-start = ((), (), s32[]{:S(2)}) async-start(), calls=%async_computation.34 | async-start | bytes 184320
  (107 other events, 2310.6 us)
Sparse Core Ops, SparseCore 0:
  52.6 69.4 all-gather.11
  124.1 72.5 all-gather.9
  198.8 63.1 all-gather.21
  263.9 62.4 all-gather.19
  327.7 18.9 all-gather.15
  348.1 20.7 all-gather.13
  370.5 20.7 all-gather.17
  623.0 61.1 reduce-scatter.74
  1084.4 61.2 reduce-scatter.68
  1149.0 65.8 reduce-scatter.50
  1218.8 65.7 reduce-scatter.48
  1288.0 65.1 reduce-scatter.52
  1377.9 19.6 reduce-scatter.54
  1400.0 20.2 reduce-scatter.64
  1422.7 20.2 reduce-scatter.62
  1445.5 20.8 reduce-scatter.66
  1470.3 118.4 reduce-scatter.42
  1592.7 117.5 reduce-scatter.40
  1714.2 117.5 reduce-scatter.46
  1835.8 117.5 reduce-scatter.44
  1957.0 57.8 reduce-scatter.72
  2018.6 57.6 reduce-scatter.70
  2078.7 18.5 reduce-scatter.58
  2099.9 19.5 reduce-scatter.56
  (1 shorter events, 18.5 us)
where the time goes:
time: 2140 us; the launch traced here: 2130 us
  waiting for transfers between devices  892 us (42%)
  matrix products  527 us (25%)
  blocking collectives  295 us (14%)
  other arithmetic  235 us (11%)
  local copies, waits for them, and re-layouts  164 us (8%)
    reduce_scatter x2, waiting for transfers between devices, shards(): lax.psum_scatter(value_terms, 'seq', scatter_dimension=1, tiled=True)  240 us
    reduce_scatter x2, waiting for transfers between devices, shards(): lax.psum_scatter(key_terms, 'seq', scatter_dimension=1, tiled=True)  236 us
    unnamed x36, waiting for transfers between devices  214 us
    convert_element_type x8, other arithmetic, attend_back(): grad_scores = (attn_probs * (grad_probs - row_delta)).astype(jnp.bfloat16)  105 us
    dot_general x8, matrix products, attend_back(): jnp.einsum('rkgd,lkd->kgrl', grad_grp, value_grp, preferred_element_type=...  102 us
    reduce_sum x8, other arithmetic, attend(): row_total = jnp.sum(exp_scores, axis=-1, keepdims=True)  82 us
    dot_general x8, matrix products, attend(): jnp.einsum('kgrl,lkd->rkgd', attn_probs.astype(jnp.bfloat16), value_grp,...  71.9 us
    dot_general x8, matrix products, attend_back(): jnp.einsum('kgrl,rkgd->lkd', probs_low, grad_grp, preferred_element_type=...  70.1 us
  transfers between devices with their start and end apart: 25, of which 14 were waited for; matrix products, arithmetic and copies ran while one was open for 40% of the time, Pallas kernels for 0%

commit v1 on v0

--- a/solution.py
+++ b/solution.py
@@ -1,6 +1,10 @@
+import functools
+
 import jax
 import jax.numpy as jnp
 from jax import lax
+from jax.experimental import pallas as pl
+from jax.experimental.pallas import tpu as pltpu
 from jax.sharding import PartitionSpec as P
 
 HD = 64
@@ -56,7 +60,7 @@
     return tuple((old_sum + new_term for old_sum, new_term in zip(old_sums, new_terms)))
 
 
-def shards(
+def shards_general(
     hidden_in,
     span_order,
     attn_gain,
@@ -369,6 +373,653 @@
     )
 
 
+F32 = jnp.float32
+BF16 = jnp.bfloat16
+VMEM_BYTES = 56 * 2**20
+
+
+def dot(left, right, left_dim, right_dim):
+    dims = (((left_dim,), (right_dim,)), ((), ()))
+    return lax.dot_general(left, right, dims, preferred_element_type=F32)
+
+
+def span_slice(inv_ref, place, span):
+    return pl.ds(pl.multiple_of(inv_ref[place] * span, span), span)
+
+
+def lane_pair(ref, rows, inv_ref, block, span):
+    first = ref[rows, span_slice(inv_ref, 2 * block, span)]
+    second = ref[rows, span_slice(inv_ref, 2 * block + 1, span)]
+    return jnp.concatenate([first, second], axis=1)
+
+
+def row_pair(ref, head, inv_ref, block, span):
+    first = ref[head, span_slice(inv_ref, 2 * block, span), :]
+    second = ref[head, span_slice(inv_ref, 2 * block + 1, span), :]
+    return jnp.concatenate([first, second], axis=0)
+
+
+def qkv_kernel(x_ref, gain_ref, w_ref, cos_ref, sin_ref, q_ref, kt_ref, vt_ref, k_ref, v_ref, *, heads, kv_heads):
+    half = HD // 2
+    x = x_ref[...].astype(F32)
+    rstd = lax.rsqrt(jnp.mean(x * x, axis=-1, keepdims=True) + eps_norm)
+    normed = (x * rstd * gain_ref[...]).astype(BF16)
+    lin = dot(w_ref[...], normed, 1, 1)
+    cos, sin = cos_ref[...], sin_ref[...]
+    for head in range(heads + kv_heads):
+        top = lin[HD * head : HD * head + half]
+        low = lin[HD * head + half : HD * head + HD]
+        rot = jnp.concatenate([top * cos - low * sin, low * cos + top * sin], axis=0).astype(BF16)
+        if head < heads:
+            q_ref[HD * head : HD * head + HD, :] = rot * jnp.asarray(HD**-0.5, BF16)
+        else:
+            kv = head - heads
+            kt_ref[HD * kv : HD * kv + HD, :] = rot
+            k_ref[kv] = rot.T
+    for kv in range(kv_heads):
+        first = HD * (heads + kv_heads + kv)
+        val = lin[first : first + HD].astype(BF16)
+        vt_ref[HD * kv : HD * kv + HD, :] = val
+        v_ref[kv] = val.T
+
+
+def project_qkv(x, gain, w_t, cos_t, sin_t, heads, kv_heads, block=512):
+    tokens, width = x.shape
+    col = lambda rows: pl.BlockSpec((rows, block), lambda i: (0, i))
+    nat = pl.BlockSpec((kv_heads, block, HD), lambda i: (0, i, 0))
+    return pl.pallas_call(
+        functools.partial(qkv_kernel, heads=heads, kv_heads=kv_heads),
+        grid=(tokens // block,),
+        in_specs=[
+            pl.BlockSpec((block, width), lambda i: (i, 0)),
+            pl.BlockSpec((1, width), lambda i: (0, 0)),
+            pl.BlockSpec(w_t.shape, lambda i: (0, 0)),
+            col(HD // 2),
+            col(HD // 2),
+        ],
+        out_specs=[col(heads * HD), col(kv_heads * HD), col(kv_heads * HD), nat, nat],
+        out_shape=[
+            jax.ShapeDtypeStruct((heads * HD, tokens), BF16),
+            jax.ShapeDtypeStruct((kv_heads * HD, tokens), BF16),
+            jax.ShapeDtypeStruct((kv_heads * HD, tokens), BF16),
+            jax.ShapeDtypeStruct((kv_heads, tokens, HD), BF16),
+            jax.ShapeDtypeStruct((kv_heads, tokens, HD), BF16),
+        ],
+        compiler_params=pltpu.CompilerParams(vmem_limit_bytes=VMEM_BYTES),
+        cost_estimate=pl.CostEstimate(
+            flops=4 * tokens * width * w_t.shape[0], bytes_accessed=tokens * 5000, transcendentals=0
+        ),
+        name="project_qkv",
+    )(x, gain, w_t, cos_t, sin_t)
+
+
+def attend_kernel(inv_ref, q_ref, k_ref, v_ref, o_ref, on_ref, l_ref, *, blocks, span, group):
+    wide = 2 * span
+    row = lax.broadcasted_iota(jnp.int32, (wide, wide), 0)
+    col = lax.broadcasted_iota(jnp.int32, (wide, wide), 1)
+    keep = row <= col
+
+    def q_block(block, _):
+        queries = [
+            lane_pair(q_ref, slice(HD * h, HD * h + HD), inv_ref, block, span) for h in range(group)
+        ]
+
+        def scores_of(j):
+            keys = row_pair(k_ref, 0, inv_ref, j, span)
+            return tuple(dot(keys, query, 1, 0) for query in queries)
+
+        def take(j, scores, carry, masked):
+            values = lane_pair(v_ref, slice(0, HD), inv_ref, j, span)
+            out = []
+            for score, (peak, total, mixed) in zip(scores, carry):
+                if masked:
+                    score = jnp.where(keep, score, neg_big)
+                new_peak = jnp.maximum(peak, jnp.max(score, axis=0, keepdims=True))
+                prob = jnp.exp(score - new_peak)
+                shrink = jnp.exp(peak - new_peak)
+                total = total * shrink + jnp.sum(prob, axis=0, keepdims=True)
+                mixed = mixed * shrink + dot(values, prob.astype(BF16), 1, 0)
+                out.append((new_peak, total, mixed))
+            return tuple(out)
+
+        def body(j, carry):
+            scores, state = carry
+            following = scores_of(j + 1)
+            return following, take(j, scores, state, False)
+
+        empty = tuple(
+            (jnp.full((1, wide), neg_big, F32), jnp.zeros((1, wide), F32), jnp.zeros((HD, wide), F32))
+            for _ in range(group)
+        )
+        scores, state = lax.fori_loop(0, block, body, (scores_of(0), empty))
+        state = take(block, scores, state, True)
+        mixed = jnp.concatenate([m * (1.0 / t) for (_, t, m) in state], axis=0)
+        logs = jnp.concatenate(
+            [p + jnp.log(t) for (p, t, _) in state] + [jnp.zeros((8 - group, wide), F32)], axis=0
+        )
+        mixed_low = mixed.astype(BF16)
+        natural = mixed.T.astype(BF16)
+        for part in range(2):
+            where = span_slice(inv_ref, 2 * block + part, span)
+            cols = slice(part * span, part * span + span)
+            o_ref[:, where] = mixed_low[:, cols]
+            on_ref[0, where, :] = natural[cols, :]
+            l_ref[0, :, where] = logs[:, cols]
+        return 0
+
+    lax.fori_loop(0, blocks, q_block, 0)
+
+
+def attention_forward(inv, q_t, k_nat, v_t, span):
+    tokens = q_t.shape[1]
+    kv_heads = k_nat.shape[0]
+    group = q_t.shape[0] // (kv_heads * HD)
+    pairs = kv_heads * group * tokens * tokens
+    wide_spec = pl.BlockSpec((group * HD, tokens), lambda g, i: (g, 0))
+    nat_spec = pl.BlockSpec((1, tokens, HD), lambda g, i: (g, 0, 0))
+    return pl.pallas_call(
+        functools.partial(attend_kernel, blocks=tokens // (2 * span), span=span, group=group),
+        grid_spec=pltpu.PrefetchScalarGridSpec(
+            num_scalar_prefetch=1,
+            grid=(kv_heads,),
+            in_specs=[wide_spec, nat_spec, pl.BlockSpec((HD, tokens), lambda g, i: (g, 0))],
+            out_specs=[
+                wide_spec,
+                pl.BlockSpec((1, tokens, group * HD), lambda g, i: (g, 0, 0)),
+                pl.BlockSpec((1, 8, tokens), lambda g, i: (g, 0, 0)),
+            ],
+        ),
+        out_shape=[
+            jax.ShapeDtypeStruct(q_t.shape, BF16),
+            jax.ShapeDtypeStruct((kv_heads, tokens, group * HD), BF16),
+            jax.ShapeDtypeStruct((kv_heads, 8, tokens), F32),
+        ],
+        compiler_params=pltpu.CompilerParams(vmem_limit_bytes=VMEM_BYTES),
+        cost_estimate=pl.CostEstimate(
+            flops=16 * pairs * HD, bytes_accessed=tokens * 6000, transcendentals=pairs // 2
+        ),
+        name="attention_forward",
+    )(inv, q_t, k_nat, v_t)
+
+
+def attend_back_kernel(
+    inv_ref, q_ref, kt_ref, k_ref, v_ref, o_ref, do_ref, l_ref, cos_ref, sin_ref,
+    dq_ref, dk_ref, dv_ref, dk_sum, dv_sum, *, blocks, span, group,
+):
+    wide = 2 * span
+    row = lax.broadcasted_iota(jnp.int32, (wide, wide), 0)
+    col = lax.broadcasted_iota(jnp.int32, (wide, wide), 1)
+    keep = row <= col
+    half = HD // 2
+    dk_sum[...] = jnp.zeros_like(dk_sum)
+    dv_sum[...] = jnp.zeros_like(dv_sum)
+
+    def rope_back(grad, cos, sin):
+        top, low = grad[:half], grad[half:]
+        return jnp.concatenate([top * cos + low * sin, low * cos - top * sin], axis=0)
+
+    def q_block(step, _):
+        block = blocks - 1 - step
+        rows = [slice(HD * h, HD * h + HD) for h in range(group)]
+        queries = [lane_pair(q_ref, r, inv_ref, block, span) for r in rows]
+        grads = [lane_pair(do_ref, r, inv_ref, block, span) for r in rows]
+        logs = lane_pair(l_ref.at[0], slice(None), inv_ref, block, span)
+        deltas = [
+            jnp.sum(
+                lane_pair(o_ref, r, inv_ref, block, span).astype(F32) * grad.astype(F32),
+                axis=0,
+                keepdims=True,
+            )
+            for r, grad in zip(rows, grads)
+        ]
+
+        def take(j, dqs, masked):
+            keys = row_pair(k_ref, 0, inv_ref, j, span)
+            values = row_pair(v_ref, 0, inv_ref, j, span)
+            keys_t = lane_pair(kt_ref, slice(0, HD), inv_ref, j, span)
+            out = []
+            dk = dv = None
+            for h in range(group):
+                prob = jnp.exp(dot(keys, queries[h], 1, 0) - logs[h : h + 1])
+                if masked:
+                    prob = jnp.where(keep, prob, 0.0)
+                dprob = dot(values, grads[h], 1, 0)
+                dscore = (prob * (dprob - deltas[h])).astype(BF16)
+                dk_term = dot(queries[h], dscore, 1, 1)
+                dv_term = dot(grads[h], prob.astype(BF16), 1, 1)
+                dk = dk_term if dk is None else dk + dk_term
+                dv = dv_term if dv is None else dv + dv_term
+                out.append(dqs[h] + dot(keys_t, dscore, 1, 0))
+            place = pl.ds(pl.multiple_of(j * wide, wide), wide)
+            dk_sum[:, place] += dk
+            dv_sum[:, place] += dv
+            return tuple(out)
+
+        dqs = tuple(jnp.zeros((HD, wide), F32) for _ in range(group))
+        dqs = lax.fori_loop(0, block, lambda j, c: take(j, c, False), dqs)
+        dqs = take(block, dqs, True)
+        cos = lane_pair(cos_ref, slice(None), inv_ref, block, span)
+        sin = lane_pair(sin_ref, slice(None), inv_ref, block, span)
+        dq = jnp.concatenate([rope_back(g * HD**-0.5, cos, sin) for g in dqs], axis=0).astype(BF16)
+        place = pl.ds(pl.multiple_of(block * wide, wide), wide)
+        dk = rope_back(dk_sum[:, place], cos, sin).astype(BF16)
+        dv = dv_sum[:, place].astype(BF16)
+        for part in range(2):
+            where = span_slice(inv_ref, 2 * block + part, span)
+            cols = slice(part * span, part * span + span)
+            dq_ref[:, where] = dq[:, cols]
+            dk_ref[:, where] = dk[:, cols]
+            dv_ref[:, where] = dv[:, cols]
+        return 0
+
+    lax.fori_loop(0, blocks, q_block, 0)
+
+
+def attention_backward(inv, q_t, k_t, k_nat, v_nat, o_t, do_t, logs, cos_t, sin_t, span):
+    tokens = q_t.shape[1]
+    kv_heads = k_nat.shape[0]
+    group = q_t.shape[0] // (kv_heads * HD)
+    pairs = kv_heads * group * tokens * tokens
+    wide_spec = pl.BlockSpec((group * HD, tokens), lambda g, i: (g, 0))
+    kv_spec = pl.BlockSpec((HD, tokens), lambda g, i: (g, 0))
+    nat_spec = pl.BlockSpec((1, tokens, HD), lambda g, i: (g, 0, 0))
+    tab_spec = pl.BlockSpec((HD // 2, tokens), lambda g, i: (0, 0))
+    return pl.pallas_call(
+        functools.partial(attend_back_kernel, blocks=tokens // (2 * span), span=span, group=group),
+        grid_spec=pltpu.PrefetchScalarGridSpec(
+            num_scalar_prefetch=1,
+            grid=(kv_heads,),
+            in_specs=[
+                wide_spec, kv_spec, nat_spec, nat_spec, wide_spec, wide_spec,
+                pl.BlockSpec((1, 8, tokens), lambda g, i: (g, 0, 0)), tab_spec, tab_spec,
+            ],
+            out_specs=[wide_spec, kv_spec, kv_spec],
+            scratch_shapes=[pltpu.VMEM((HD, tokens), F32), pltpu.VMEM((HD, tokens), F32)],
+        ),
+        out_shape=[
+            jax.ShapeDtypeStruct(q_t.shape, BF16),
+            jax.ShapeDtypeStruct(k_t.shape, BF16),
+            jax.ShapeDtypeStruct(k_t.shape, BF16),
+        ],
+        compiler_params=pltpu.CompilerParams(vmem_limit_bytes=VMEM_BYTES),
+        cost_estimate=pl.CostEstimate(
+            flops=32 * pairs * HD, bytes_accessed=tokens * 9000, transcendentals=pairs // 2
+        ),
+        name="attention_backward",
+    )(inv, q_t, k_t, k_nat, v_nat, o_t, do_t, logs, cos_t, sin_t)
+
+
+def mlp_kernel(
+    x_ref, mixed_ref, mixed_t_ref, dy_ref, gain_ref, o_ref, gate_ref, up_ref, down_ref,
+    out_ref, dmid_ref, dmixed_ref, o_grad_ref, gate_grad_ref, up_grad_ref, down_grad_ref, gain_grad_ref,
+    o_sum, gate_sum, up_sum, down_sum, gain_sum, *, chunk,
+):
+    step, steps = pl.program_id(0), pl.num_programs(0)
+    groups, _, group_width = mixed_ref.shape
+    ff = gate_ref.shape[1]
+
+    @pl.when(step == 0)
+    def _():
+        o_sum[...] = jnp.zeros_like(o_sum)
+        gate_sum[...] = jnp.zeros_like(gate_sum)
+        up_sum[...] = jnp.zeros_like(up_sum)
+        down_sum[...] = jnp.zeros_like(down_sum)
+        gain_sum[...] = jnp.zeros_like(gain_sum)
+
+    gain = gain_ref[...]
+    mid = x_ref[...].astype(F32)
+    for g in range(groups):
+        mid += dot(mixed_ref[g], o_ref[g * group_width : (g + 1) * group_width, :], 1, 0)
+    rstd = lax.rsqrt(jnp.mean(mid * mid, axis=-1, keepdims=True) + eps_norm)
+    normed = (mid * rstd * gain).astype(BF16)
+    normed_t = normed.T
+    dy = dy_ref[...]
+    dy_t = dy.T
+    mlp_out = jnp.zeros_like(mid)
+    dnormed = jnp.zeros_like(mid)
+    for first in range(0, ff, chunk):
+        cols = slice(first, first + chunk)
+        gate = dot(normed, gate_ref[:, cols], 1, 0)
+        up = dot(normed, up_ref[:, cols], 1, 0)
+        dinner = dot(dy, down_ref[:, cols], 1, 0)
+        sig = 1.0 / (1.0 + jnp.exp(-gate))
+        silu = gate * sig
+        inner = (silu * up).astype(BF16)
+        dup = (dinner * silu).astype(BF16)
+        dgate = (dinner * up * sig * (1.0 + gate * (1.0 - sig))).astype(BF16)
+        mlp_out += dot(inner, down_ref[:, cols], 1, 1)
+        dnormed += dot(dgate, gate_ref[:, cols], 1, 1)
+        dnormed += dot(dup, up_ref[:, cols], 1, 1)
+        down_sum[:, cols] += dot(dy_t, inner, 1, 0)
+        gate_sum[:, cols] += dot(normed_t, dgate, 1, 0)
+        up_sum[:, cols] += dot(normed_t, dup, 1, 0)
+    out_ref[...] = (mid + mlp_out).astype(BF16)
+    scaled_mid = mid * rstd
+    gain_sum[...] += jnp.sum((dnormed * scaled_mid).reshape(-1, 8, mid.shape[1]), axis=0)
+    scaled = dnormed * gain
+    pull = jnp.mean(scaled * mid, axis=-1, keepdims=True)
+    dmid = dy.astype(F32) + rstd * scaled - scaled_mid * (rstd * rstd * pull)
+    dmid_ref[...] = dmid
+    dmid_low = dmid.astype(BF16)
+    o_sum[...] += dot(mixed_t_ref[...], dmid_low, 1, 0)
+    dmixed_ref[...] = dot(o_ref[...], dmid_low, 1, 1).astype(BF16)
+
+    @pl.when(step == steps - 1)
+    def _():
+        o_grad_ref[...] = o_sum[...].astype(BF16)
+        gate_grad_ref[...] = gate_sum[...].astype(BF16)
+        up_grad_ref[...] = up_sum[...].astype(BF16)
+        down_grad_ref[...] = down_sum[...].astype(BF16)
+        gain_grad_ref[...] = jnp.sum(gain_sum[...], axis=0, keepdims=True)
+
+
+def mlp_both(x, mixed, mixed_t, dy, gain, o_w, gate_w, up_w, down_t, block=256, chunk=512):
+    tokens, width = x.shape
+    groups, _, group_width = mixed.shape
+    ff = gate_w.shape[1]
+    tok = pl.BlockSpec((block, width), lambda i: (i, 0))
+    col = pl.BlockSpec((width, block), lambda i: (0, i))
+    once = lambda shape: pl.BlockSpec(shape, lambda i: (0, 0), pipeline_mode=pl.Buffered(1))
+    return pl.pallas_call(
+        functools.partial(mlp_kernel, chunk=chunk),
+        grid=(tokens // block,),
+        in_specs=[
+            tok,
+            pl.BlockSpec((groups, block, group_width), lambda i: (0, i, 0)),
+            col,
+            tok,
+            once((1, width)),
+            once((width, width)),
+            once((width, ff)),
+            once((width, ff)),
+            once((width, ff)),
+        ],
+        out_specs=[
+            tok, tok, col,
+            once((width, width)), once((width, ff)), once((width, ff)), once((width, ff)), once((1, width)),
+        ],
+        out_shape=[
+            jax.ShapeDtypeStruct((tokens, width), BF16),
+            jax.ShapeDtypeStruct((tokens, width), F32),
+            jax.ShapeDtypeStruct((width, tokens), BF16),
+            jax.ShapeDtypeStruct((width, width), BF16),
+            jax.ShapeDtypeStruct((width, ff), BF16),
+            jax.ShapeDtypeStruct((width, ff), BF16),
+            jax.ShapeDtypeStruct((width, ff), BF16),
+            jax.ShapeDtypeStruct((1, width), F32),
+        ],
+        scratch_shapes=[
+            pltpu.VMEM((width, width), F32),
+            pltpu.VMEM((width, ff), F32),
+            pltpu.VMEM((width, ff), F32),
+            pltpu.VMEM((width, ff), F32),
+            pltpu.VMEM((8, width), F32),
+        ],
+        compiler_params=pltpu.CompilerParams(vmem_limit_bytes=VMEM_BYTES),
+        cost_estimate=pl.CostEstimate(
+            flops=2 * tokens * width * (9 * ff + 3 * width),
+            bytes_accessed=tokens * width * 14,
+            transcendentals=tokens * ff,
+        ),
+        name="mlp_both",
+    )(x, mixed, mixed_t, dy, gain, o_w, gate_w, up_w, down_t)
+
+
+def qkv_back_kernel(
+    x_ref, dmid_ref, dq_ref, dk_ref, dv_ref, gain_ref, w_ref,
+    din_ref, w_grad_ref, gain_grad_ref, w_sum, gain_sum,
+):
+    step, steps = pl.program_id(0), pl.num_programs(0)
+
+    @pl.when(step == 0)
+    def _():
+        w_sum[...] = jnp.zeros_like(w_sum)
+        gain_sum[...] = jnp.zeros_like(gain_sum)
+
+    gain = gain_ref[...]
+    x = x_ref[...].astype(F32)
+    rstd = lax.rsqrt(jnp.mean(x * x, axis=-1, keepdims=True) + eps_norm)
+    scaled_x = x * rstd
+    normed = (scaled_x * gain).astype(BF16)
+    dlin = jnp.concatenate([dq_ref[...], dk_ref[...], dv_ref[...]], axis=0)
+    w_sum[...] += dot(dlin, normed, 1, 0)
+    dnormed = dot(dlin, w_ref[...], 0, 0)
+    gain_sum[...] += jnp.sum((dnormed * scaled_x).reshape(-1, 8, x.shape[1]), axis=0)
+    scaled = dnormed * gain
+    pull = jnp.mean(scaled * x, axis=-1, keepdims=True)
+    din_ref[...] = (dmid_ref[...] + rstd * scaled - scaled_x * (rstd * rstd * pull)).astype(BF16)
+
+    @pl.when(step == steps - 1)
+    def _():
+        w_grad_ref[...] = w_sum[...].astype(BF16)
+        gain_grad_ref[...] = jnp.sum(gain_sum[...], axis=0, keepdims=True)
+
+
+def project_back(x, dmid, dq_t, dk_t, dv_t, gain, w_t, block=512):
+    tokens, width = x.shape
+    feats = w_t.shape[0]
+    tok = pl.BlockSpec((block, width), lambda i: (i, 0))
+    col = lambda rows: pl.BlockSpec((rows, block), lambda i: (0, i))
+    once = lambda shape: pl.BlockSpec(shape, lambda i: (0, 0), pipeline_mode=pl.Buffered(1))
+    return pl.pallas_call(
+        qkv_back_kernel,
+        grid=(tokens // block,),
+        in_specs=[
+            tok, tok, col(dq_t.shape[0]), col(dk_t.shape[0]), col(dv_t.shape[0]),
+            once((1, width)), once((feats, width)),
+        ],
+        out_specs=[tok, once((feats, width)), once((1, width))],
+        out_shape=[
+            jax.ShapeDtypeStruct((tokens, width), BF16),
+            jax.ShapeDtypeStruct((feats, width), BF16),
+            jax.ShapeDtypeStruct((1, width), F32),
+        ],
+        scratch_shapes=[pltpu.VMEM((feats, width), F32), pltpu.VMEM((8, width), F32)],
+        compiler_params=pltpu.CompilerParams(vmem_limit_bytes=VMEM_BYTES),
+        cost_estimate=pl.CostEstimate(
+            flops=4 * tokens * width * feats, bytes_accessed=tokens * width * 12, transcendentals=0
+        ),
+        name="project_back",
+    )(x, dmid, dq_t, dk_t, dv_t, gain, w_t)
+
+
+def swap(array, axis, bit):
+    size = lax.axis_size(axis)
+    return lax.ppermute(array, axis, [(i, i ^ bit) for i in range(size)])
+
+
+def bits_of(axis):
+    size = lax.axis_size(axis)
+    return [1 << i for i in range(size.bit_length() - 1)]
+
+
+def gather_doubling(array):
+    whole = array[None]
+    for axis in ("seq", "dp"):
+        for bit in bits_of(axis):
+            upper = (lax.axis_index(axis) // bit) % 2 == 1
+            other = swap(whole, axis, bit)
+            whole = jnp.concatenate([jnp.where(upper, other, whole), jnp.where(upper, whole, other)], axis=0)
+    return whole.reshape(lax.axis_size("dp"), lax.axis_size("seq"), *array.shape)
+
+
+def scatter_halving(array):
+    rows, lanes = array.shape[2:]
+    part = array.reshape(-1, rows, lanes)
+    order = [("dp", b) for b in bits_of("dp")]
+    seq_bits = [("seq", b) for b in bits_of("seq")]
+    seq_size = lax.axis_size("seq")
+    dims = [2] * (len(order) + len(seq_bits))
+    part = part.reshape(*dims, rows, lanes)
+    names = [("dp", b) for b in reversed(bits_of("dp"))] + [("seq", b) for b in reversed(bits_of("seq"))]
+    for axis, bit in order + seq_bits:
+        place = names.index((axis, bit))
+        names.pop(place)
+        upper = (lax.axis_index(axis) // bit) % 2
+        mine = lax.dynamic_index_in_dim(part, upper, place, keepdims=False)
+        other = lax.dynamic_index_in_dim(part, 1 - upper, place, keepdims=False)
+        part = (mine.astype(F32) + swap(other, axis, bit).astype(F32)).astype(BF16)
+    return part.reshape(rows, lanes)
+
+
+def sum_doubling(array):
+    for axis in ("dp", "seq"):
+        for bit in bits_of(axis):
+            array = array + swap(array, axis, bit)
+    return array
+
+
+def to_sequences(block):
+    moved = lax.all_to_all(block, "seq", 0, 0, tiled=True)
+    return moved.reshape(-1, block.shape[2])
+
+
+def to_slots(tokens, seqs):
+    moved = lax.all_to_all(tokens.reshape(seqs, -1, tokens.shape[1]), "seq", 0, 0, tiled=True)
+    return moved
+
+
+def fold(matrix, lanes=128):
+    rows, cols = matrix.shape[-2:]
+    full = cols // lanes * lanes
+    parts = [matrix[..., :, c : c + lanes] for c in range(0, full, lanes)]
+    if full < cols:
+        rest = matrix[..., :, full:]
+        parts.append(jnp.concatenate([rest[..., : rows // 2, :], rest[..., rows // 2 :, :]], axis=-1))
+    return jnp.concatenate(parts, axis=-2)
+
+
+def unfold(packed, rows, cols, lanes=128):
+    full = cols // lanes
+    parts = [packed[..., i * rows : (i + 1) * rows, :] for i in range(full)]
+    if full * lanes < cols:
+        rest = packed[..., full * rows :, :]
+        parts.append(jnp.concatenate([rest[..., :, : lanes // 2], rest[..., :, lanes // 2 :]], axis=-2))
+    return jnp.concatenate(parts, axis=-1)
+
+
+def pad_lanes(matrix, lanes=128):
+    return jnp.pad(matrix, [(0, 0)] * (matrix.ndim - 1) + [(0, lanes - matrix.shape[-1])])
+
+
+def join(blocks):
+    dp, seq, rows, cols = blocks.shape
+    return blocks.transpose(0, 2, 1, 3).reshape(dp * rows, seq * cols)
+
+
+def cut(matrix, dp, seq):
+    rows, cols = matrix.shape
+    return matrix.reshape(dp, rows // dp, seq, cols // seq).transpose(0, 2, 1, 3)
+
+
+def shards_sequences(
+    hidden_in, span_order, attn_gain, q_weight, k_weight, v_weight, o_weight, mlp_gain,
+    gate_weight, up_weight, down_weight, out_grad,
+):
+    seqs, slots, width = hidden_in.shape
+    dp, seq = lax.axis_size("dp"), lax.axis_size("seq")
+    tokens = slots * seq
+    spans = span_order.shape[0]
+    span = tokens // spans
+    heads = width // HD
+    kv_heads = k_weight.shape[1] * seq // HD
+    rows, q_cols = q_weight.shape
+    kv_cols = k_weight.shape[1]
+
+    x = to_sequences(hidden_in)
+    qkv_shard = pad_lanes(jnp.concatenate([q_weight, k_weight, v_weight], axis=1))
+    qkv_all = gather_doubling(qkv_shard)
+    dy = to_sequences(out_grad)
+
+    rest_shard = jnp.concatenate(
+        [fold(gate_weight), fold(up_weight), fold(down_weight.T), pad_lanes(o_weight)], axis=0
+    )
+    rest_all = lax.all_gather(rest_shard, ("dp", "seq"), axis=0, tiled=False)
+    rest_all = rest_all.reshape(dp, seq, *rest_shard.shape)
+
+    inv = jnp.argsort(span_order).astype(jnp.int32)
+    slot_pos = slot_positions(jnp.arange(tokens, dtype=jnp.int32), span_order, span)
+    inv_freq = rope_base ** (-(jnp.arange(HD // 2, dtype=F32) * 2.0) / HD)
+    angles = slot_pos.astype(F32)[None, :] * inv_freq[:, None]
+    cos_t, sin_t = jnp.cos(angles), jnp.sin(angles)
+    gain_one = attn_gain.astype(F32)[None]
+    gain_two = mlp_gain.astype(F32)[None]
+
+    by_feature = qkv_all.transpose(1, 3, 0, 2).reshape(seq, qkv_shard.shape[1], width)
+    w_t = jnp.concatenate(
+        [
+            by_feature[:, :q_cols].reshape(-1, width),
+            by_feature[:, q_cols : q_cols + kv_cols].reshape(-1, width),
+            by_feature[:, q_cols + kv_cols : q_cols + 2 * kv_cols].reshape(-1, width),
+        ],
+        axis=0,
+    )
+    q_t, k_t, v_t, k_nat, v_nat = project_qkv(x, gain_one, w_t, cos_t, sin_t, heads, kv_heads)
+    o_t, o_nat, logs = attention_forward(inv, q_t, k_nat, v_t, span)
+
+    g_rows, g_cols = gate_weight.shape
+    d_rows, d_cols = down_weight.shape
+    part = g_rows * g_cols // 128
+    down_part = d_rows * d_cols // 128
+    gate_w = join(unfold(rest_all[:, :, :part], g_rows, g_cols))
+    up_w = join(unfold(rest_all[:, :, part : 2 * part], g_rows, g_cols))
+    down_blocks = unfold(rest_all[:, :, 2 * part : 2 * part + down_part], d_cols, d_rows)
+    down_t = down_blocks.transpose(1, 2, 0, 3).reshape(seq * d_cols, dp * d_rows)
+    o_cols = o_weight.shape[1]
+    o_w = join(rest_all[:, :, 2 * part + down_part :, :o_cols])
+
+    out, dmid, do_t, o_grad, gate_grad, up_grad, down_grad_t, gain_two_grad = mlp_both(
+        x, o_nat, o_t, dy, gain_two, o_w, gate_w, up_w, down_t
+    )
+    hidden_out = to_slots(out, seqs)
+    down_cut = down_grad_t.reshape(seq, d_cols, dp, d_rows).transpose(2, 0, 1, 3)
+    rest_grads = jnp.concatenate(
+        [
+            fold(cut(gate_grad, dp, seq)),
+            fold(cut(up_grad, dp, seq)),
+            fold(down_cut),
+            pad_lanes(cut(o_grad, dp, seq)),
+        ],
+        axis=2,
+    )
+    rest_sum = lax.psum_scatter(
+        rest_grads.reshape(dp * seq, *rest_grads.shape[2:]), ("dp", "seq"), scatter_dimension=0, tiled=True
+    )[0].astype(F32)
+
+    dq_t, dk_t, dv_t = attention_backward(
+        inv, q_t, k_t, k_nat, v_nat, o_t, do_t, logs, cos_t, sin_t, span
+    )
+    din, w_grad_t, gain_one_grad = project_back(x, dmid, dq_t, dk_t, dv_t, gain_one, w_t)
+    grad_in = to_slots(din, seqs).astype(F32)
+
+    q_part = w_grad_t[:width].reshape(seq, q_cols, dp, rows)
+    k_part = w_grad_t[width : width + kv_cols * seq].reshape(seq, kv_cols, dp, rows)
+    v_part = w_grad_t[width + kv_cols * seq :].reshape(seq, kv_cols, dp, rows)
+    qkv_grads = jnp.concatenate([q_part, k_part, v_part], axis=1).transpose(2, 0, 3, 1)
+    qkv_sum = scatter_halving(pad_lanes(qkv_grads)).astype(F32)
+    gains = sum_doubling(jnp.concatenate([gain_one_grad, gain_two_grad], axis=0))
+    return (
+        hidden_out,
+        grad_in,
+        gains[0],
+        qkv_sum[:, :q_cols],
+        qkv_sum[:, q_cols : q_cols + kv_cols],
+        qkv_sum[:, q_cols + kv_cols : q_cols + 2 * kv_cols],
+        rest_sum[2 * part + down_part :, :o_cols],
+        gains[1],
+        unfold(rest_sum[:part], g_rows, g_cols),
+        unfold(rest_sum[part : 2 * part], g_rows, g_cols),
+        unfold(rest_sum[2 * part : 2 * part + down_part], d_cols, d_rows).T,
+    )
+
+
+def shards(*args):
+    hidden_in = args[0]
+    if hidden_in.shape[0] == lax.axis_size("seq"):
+        return shards_sequences(*args)
+    return shards_general(*args)
+
+
 def solution(mesh):
     placed = (
         P("dp", "seq", None),

time: 2140 us -> 631 us (0.29)
  waiting for transfers between devices: 892 us -> 94.3 us
  matrix products: 527 us -> 0 us
  Pallas kernels: 0 us -> 250 us
  other arithmetic: 235 us -> 24.2 us
  blocking collectives: 295 us -> 91.7 us
  local copies, waits for them, and re-layouts: 164 us -> 112 us
  starting transfers between devices: 1.78 us -> 32.9 us
    reduce_scatter x7 -> x0, waiting for transfers between devices: 678 us -> none  [the longest x2 240 us: shards(): lax.psum_scatter(value_terms, 'seq', scatter_dimension=1, tiled=True)]
    dot_general x98 -> x0, matrix products: 527 us -> none  [the longest x8 102 us: attend_back(): jnp.einsum('rkgd,lkd->kgrl', grad_grp, value_grp, preferred_element_type=...]
    all_gather x11 -> x0, blocking collectives: 255 us -> none  [the longest x1 34.4 us: shards(): lax.all_gather(down_weight, 'seq', axis=1, tiled=True)]
    pallas_call x0 -> x5, Pallas kernels: none -> 250 us  [the longest x1 103 us: attention_backward(): pl.pallas_call(functools.partial(attend_back_kernel, blocks=tokens // (2...]
    unnamed x36 -> x3, waiting for transfers between devices: 214 us -> 0.03 us
    convert_element_type x19 -> x8, other arithmetic: 115 us -> 6.1 us  [the longest x1 2.62 us: shards_sequences(): grad_in = to_slots(din, seqs).astype(F32)]
    ppermute x0 -> x15, waiting for transfers between devices: none -> 94.2 us  [swap(): return lax.ppermute(array, axis, [(i, i ^ bit) for i in range(size)])]
    all_to_all x0 -> x1, blocking collectives: none -> 91.7 us  [to_sequences(): moved = lax.all_to_all(block, 'seq', 0, 0, tiled=True)]
  transfers between devices with their start and end apart: 25 -> 20, of which waited for: 14 -> 12; matrix products, arithmetic and copies ran while one was open for 40% -> 14% of each run, Pallas kernels for 0% -> 30%
where the time goes in v1:
time: 631 us; the launch traced here: 620 us
  Pallas kernels  250 us (40%)
  local copies, waits for them, and re-layouts  112 us (18%)
  waiting for transfers between devices  94.3 us (15%)
  blocking collectives  91.7 us (15%)
  starting transfers between devices  32.9 us (5%)
  other arithmetic  24.2 us (4%)
  between operations  15 us (2%)
    pallas_call x1, Pallas kernels, attention_backward(): pl.pallas_call(functools.partial(attend_back_kernel, blocks=tokens // (2...  103 us
    ppermute x15, waiting for transfers between devices, swap(): return lax.ppermute(array, axis, [(i, i ^ bit) for i in range(size)])  94.2 us
    all_to_all x1, blocking collectives, to_sequences(): moved = lax.all_to_all(block, 'seq', 0, 0, tiled=True)  91.7 us
    pallas_call x1, Pallas kernels, attention_forward(): pl.pallas_call(functools.partial(attend_kernel, blocks=tokens // (2 * spa...  64.1 us
    pallas_call x1, Pallas kernels, mlp_both(): pl.pallas_call(functools.partial(mlp_kernel, chunk=chunk), grid=(tokens /...  61.6 us
    unnamed x64, local copies, waits for them, and re-layouts  26 us
    ppermute x15, starting transfers between devices, swap(): return lax.ppermute(array, axis, [(i, i ^ bit) for i in range(size)])  19.2 us
    pallas_call x1, Pallas kernels, project_back(): pl.pallas_call(qkv_back_kernel, grid=(tokens // block,), in_specs=[tok, t...  13.4 us
  transfers between devices with their start and end apart: 20, of which 12 were waited for; matrix products, arithmetic and copies ran while one was open for 14% of the time, Pallas kernels for 30%

profile of v1, /device:TPU:0, one launch (start us, length us, event | category | flops | bytes accessed | tf_op | source)
XLA Modules:
  0.0 619.6 jit_solution(8585018263543098268)
XLA Ops:
  14.1 91.7 %all_to_all.20 = bf16[8,256,576]{1,2,0:T(8,128)(2,1)} all-to-all(bf16[8,256,576]{1,2,0:T(8,128)(2,1)} %param.12), channel_id=1, replica_groups=mesh['dp'=4,'seq'=8] {'seq'}, dimensions={0} | all-to-all | bytes 4718592 | tf_op jit(solution)/shard_map/all_to_all | solution.py:873
  112.0 17.2 %collective-permute-done = bf16[1,144,128]{2,1,0:T(8,128)(2,1)S(1)} collective-permute-done((bf16[1,144,128]{2,1,0:T(8,128)(2,1)S(1)}, bf16[1,144,128]{2,1,0:T(8,128)(2,1)S(1)}, u32[]{:S(2)}, u32[]{:S(2)}) %collective-permute-start) | collective-permute-done | bytes 36896 | tf_op jit(solution)/shard_map/ppermute | solution.py:828
  130.6 18.3 %collective-permute-done.1 = bf16[2,144,128]{2,1,0:T(8,128)(2,1)S(1)} collective-permute-done((bf16[2,144,128]{2,1,0:T(8,128)(2,1)S(1)}, bf16[2,144,128]{2,1,0:T(8,128)(2,1)S(1)}, u32[]{:S(2)}, u32[]{:S(2)}) %collective-permute-start.1) | collective-permute-done | bytes 73760 | tf_op jit(solution)/shard_map/ppermute | solution.py:828
  148.9 4.3 collective-permute-start.2
  153.2 15.7 %collective-permute-done.2 = bf16[4,144,128]{2,1,0:T(8,128)(2,1)S(1)} collective-permute-done((bf16[4,144,128]{2,1,0:T(8,128)(2,1)S(1)}, bf16[4,144,128]{2,1,0:T(8,128)(2,1)S(1)}, u32[]{:S(2)}, u32[]{:S(2)}) %collective-permute-start.2) | collective-permute-done | bytes 147488 | tf_op jit(solution)/shard_map/ppermute | solution.py:828
  178.5 8.6 %collective-permute-done.4 = bf16[16,144,128]{2,1,0:T(8,128)(2,1)S(1)} collective-permute-done((bf16[16,144,128]{2,1,0:T(8,128)(2,1)}, bf16[16,144,128]{2,1,0:T(8,128)(2,1)S(1)}, u32[]{:S(2)}, u32[]{:S(2)}) %collective-permute-start.4) | collective-permute-done | bytes 589856 | tf_op jit(solution)/shard_map/ppermute | solution.py:828
  198.0 4.3 copy.131
  204.9 8.3 %project_qkv.1 = (bf16[576,2048]{1,0:T(8,128)(2,1)}, bf16[192,2048]{1,0:T(8,128)(2,1)}, bf16[192,2048]{1,0:T(8,128)(2,1)}, bf16[3,2048,64]{2,1,0:T(8,128)(2,1)}, bf16[3,2048,64]{2,1,0:T(8,128)(2,1)}) custom-call(bf16[2048,576]{1,0:T(8,128)(2,1)} %bitcast.102, f32[1,576]{1,0:T(1,128)} %reshape.161.gain_ref, bf16[960,576]{1,0:T(8,128)(2,1)} %pad_maximum_fusion.1.w_ref, ...), custom_call_target="tpu_custom_call" | custom-call | flops 4529848320 | bytes 10240000 | tf_op jit(solution)/shard_map/project_qkv/pallas_call | solution.py:430
  213.2 64.1 %attention_forward.1 = (bf16[576,2048]{1,0:T(8,128)(2,1)}, bf16[3,2048,192]{2,1,0:T(8,128)(2,1)}, f32[3,8,2048]{2,1,0:T(8,128)}) custom-call(s32[16]{0:T(128)} %get-tuple-element.34.inv_ref, bf16[576,2048]{1,0:T(8,128)(2,1)} %get-tuple-element.35.q_ref, bf16[3,2048,64]{2,1,0:T(8,128)(2,1)} %get-tuple-element.36.k_ref, bf16[192,2048]{1,0:T(8,128)(2,1)} %get-tuple-element.37.v_ref), custom_call_target="tpu_custom_call" | custom-call | flops 38654705664 | bytes 12288000 | tf_op jit(solution)/shard_map/attention_forward/pallas_call | solution.py:520
  278.9 3.9 fusion.24
  304.0 61.6 %mlp_both.1 = (bf16[2048,576]{1,0:T(8,128)(2,1)}, f32[2048,576]{1,0:T(8,128)}, bf16[576,2048]{1,0:T(8,128)(2,1)}, bf16[576,576]{1,0:T(8,128)(2,1)}, bf16[576,153...) custom-call(bf16[2048,576]{1,0:T(8,128)(2,1)} %bitcast.103, ...), custom_call_target="tpu_custom_call" | custom-call | flops 36691771392 | bytes 16515072 | tf_op jit(solution)/shard_map/mlp_both/pallas_call | solution.py:723
  370.5 4.3 copy.149
  378.5 4.8 reshape.157
  388.2 4.1 reshape.158
  405.8 6.4 %copy.157 = bf16[4,8,792,128]{3,2,1,0:T(8,128)(2,1)} copy(bf16[4,8,792,128]{3,1,2,0:T(8,128)(2,1)} %pad_dynamic-update-slice_fusion) | data formatting | bytes 12976128 | tf_op jit(solution)/shard_map/concatenate | solution.py:976
  412.2 102.5 %attention_backward.1 = (bf16[576,2048]{1,0:T(8,128)(2,1)}, bf16[192,2048]{1,0:T(8,128)(2,1)}, bf16[192,2048]{1,0:T(8,128)(2,1)}) custom-call(s32[16]{0:T(128)} %get-tuple-element.34.inv_ref, bf16[576,2048]{1,0:T(8,128)(2,1)} %get-tuple-element.35.q_ref, bf16[192,2048]{1,0:T(8,128)(2,1)} %get-tuple-element.42.kt_ref, ...), custom_call_target="tpu_custom_call" | custom-call | flops 77309411328 | bytes 18432000 | tf_op jit(solution)/shard_map/attention_backward/pallas_call | solution.py:627
  514.8 13.4 %project_back.1 = (bf16[2048,576]{1,0:T(8,128)(2,1)}, bf16[960,576]{1,0:T(8,128)(2,1)}, f32[1,576]{1,0:T(1,128)}) custom-call(bf16[2048,576]{1,0:T(8,128)(2,1)} %bitcast.104, f32[2048,576]{1,0:T(8,128)} %get-tuple-element.41.dmid_ref, bf16[576,2048]{1,0:T(8,128)(2,1)} %get-tuple-element.46.dq_ref, bf16[192,2048]{1,0:T(8,128)(2,1)} %get-tuple-element.47.dk_ref, ...), custom_call_target="tpu_custom_call" | custom-call | flops 4529848320 | bytes 14155776 | tf_op jit(solution)/shard_map/project_back/pallas_call | solution.py:804
  528.2 4.3 copy.150
  533.9 6.2 %all-to-all-start.3 = ((bf16[8,256,576]{1,2,0:T(8,128)(2,1)}), bf16[8,256,576]{1,2,0:T(8,128)(2,1)S(1)}, u32[]{:S(2)}, u32[]{:S(2)}) async-start(bf16[8,256,576]{1,2,0:T(8,128)(2,1)} %copy.150), calls=%async_computation.3 | async-start | bytes 4718592 | tf_op jit(solution)/shard_map/all_to_all | solution.py:878
  562.6 7.5 %collective-permute-done.11 = bf16[2,2,2,144,128]{4,3,2,1,0:T(8,128)(2,1)S(1)} collective-permute-done((bf16[2,2,2,144,128]{4,3,2,1,0:T(8,128)(2,1)S(1)}, bf16[2,2,2,144,128]{4,3,2,1,0:T(8,128)(2,1)S(1)}, u32[]{:S(2)}, u32[]{:S(2)}) %collective-permute-start.11) | collective-permute-done | bytes 294944 | tf_op jit(solution)/shard_map/ppermute | solution.py:828
  574.8 4.5 collective-permute-done.12
  585.6 8.4 %collective-permute-done.8 = f32[2,576]{1,0:T(2,128)S(1)} collective-permute-done((f32[2,576]{1,0:T(2,128)S(1)}, f32[2,576]{1,0:T(2,128)S(1)}, u32[]{:S(2)}, u32[]{:S(2)}) %collective-permute-start.8) | collective-permute-done | bytes 4640 | tf_op jit(solution)/shard_map/ppermute | solution.py:828
  594.1 4.4 collective-permute-done.9
  599.3 4.2 collective-permute-done.14
  (180 shorter events, 131.6 us)
Async XLA Ops:
  7.2 270.2 %all-gather.3.cloned.1.call-start = ((), (), s32[]{:S(2)}) async-start(), calls=%async_computation.5 | async-start | bytes 6690816 | tf_op jit(solution)/shard_map/all_gather | solution.py:937
  105.8 96.5 %all-to-all-start.1 = ((bf16[8,256,576]{1,2,0:T(8,128)(2,1)}), bf16[8,256,576]{1,2,0:T(8,128)(2,1)S(1)}, u32[]{:S(2)}, u32[]{:S(2)}) async-start(bf16[8,256,576]{1,2,0:T(8,128)(2,1)} %param.23), calls=%async_computation.1 | async-start | bytes 4718592 | tf_op jit(solution)/shard_map/all_to_all | solution.py:873
  109.6 59.5 %copy-start.18 = (s32[16]{0:T(128)S(1)}, s32[16]{0:T(128)}, u32[]{:S(2)}) copy-start(s32[16]{0:T(128)} %param.13) | copy-start | bytes 196
  109.9 19.3 %collective-permute-start = (bf16[1,144,128]{2,1,0:T(8,128)(2,1)S(1)}, bf16[1,144,128]{2,1,0:T(8,128)(2,1)S(1)}, u32[]{:S(2)}, u32[]{:S(2)}) collective-permute-start(bf16[1,144,128]{2,1,0:T(8,128)(2,1)S(1)} %fusion.11), channel_id=1, source_target_pairs={{0,1},{1,0},{2,3},{3,2},{4,5},{5,4},{6,7},{7,6},{8,9},{9,8},{10,11... | collective-permute-start | bytes 110600 | tf_op jit(solution)/shard_map/ppermute | solution.py:828
  112.0 63.5 %copy-start.16 = (bf16[576]{0:T(1024)(128)(2,1)S(1)}, bf16[576]{0:T(1024)(128)(2,1)}, u32[]{:S(2)}) copy-start(bf16[576]{0:T(1024)(128)(2,1)} %param.14) | copy-start | bytes 3460
  112.0 64.1 %copy-start.17 = (bf16[576]{0:T(1024)(128)(2,1)S(1)}, bf16[576]{0:T(1024)(128)(2,1)}, u32[]{:S(2)}) copy-start(bf16[576]{0:T(1024)(128)(2,1)} %param.19) | copy-start | bytes 3460
  129.3 19.5 %collective-permute-start.1 = (bf16[2,144,128]{2,1,0:T(8,128)(2,1)S(1)}, bf16[2,144,128]{2,1,0:T(8,128)(2,1)S(1)}, u32[]{:S(2)}, u32[]{:S(2)}) collective-permute-start(bf16[2,144,128]{2,1,0:T(8,128)(2,1)S(1)} %pad_maximum_fusion.6), channel_id=1, source_target_pairs={{0,2},{1,3},{2,0},{3,1},{4,6},{5,7},{6,4},{7,5},{8,10},{9,11},{10,... | collective-permute-start | bytes 221192 | tf_op jit(solution)/shard_map/ppermute | solution.py:828
  148.9 20.0 %collective-permute-start.2 = (bf16[4,144,128]{2,1,0:T(8,128)(2,1)S(1)}, bf16[4,144,128]{2,1,0:T(8,128)(2,1)S(1)}, u32[]{:S(2)}, u32[]{:S(2)}) collective-permute-start(bf16[4,144,128]{2,1,0:T(8,128)(2,1)S(1)} %pad_maximum_fusion.5), channel_id=1, source_target_pairs={{0,4},{1,5},{2,6},{3,7},{4,0},{5,1},{6,2},{7,3},{8,12},{9,13},{10,... | collective-permute-start | bytes 442376 | tf_op jit(solution)/shard_map/ppermute | solution.py:828
  169.0 1.6 collective-permute-start.3
  171.5 15.6 %collective-permute-start.4 = (bf16[16,144,128]{2,1,0:T(8,128)(2,1)}, bf16[16,144,128]{2,1,0:T(8,128)(2,1)S(1)}, u32[]{:S(2)}, u32[]{:S(2)}) collective-permute-start(bf16[16,144,128]{2,1,0:T(8,128)(2,1)} %pad_maximum_fusion.3), channel_id=1, source_target_pairs={{0,16},{8,24},{16,0},{24,8},{1,17},{9,25},{17,1},{25,9},{2,18},{10... | collective-permute-start | bytes 1769480 | tf_op jit(solution)/shard_map/ppermute | solution.py:828
  374.8 157.7 %all-to-all-start.2 = ((bf16[8,256,576]{1,2,0:T(8,128)(2,1)}), bf16[8,256,576]{1,2,0:T(8,128)(2,1)S(1)}, u32[]{:S(2)}, u32[]{:S(2)}) async-start(bf16[8,256,576]{1,2,0:T(8,128)(2,1)} %copy.149), calls=%async_computation.2 | async-start | bytes 4718592 | tf_op jit(solution)/shard_map/all_to_all | solution.py:878
  378.5 229.1 %reduce-scatter.4.cloned.1.call-start = ((), (), s32[]{:S(2)}) async-start(), calls=%async_computation.6 | async-start | bytes 6690816
  533.9 71.1 %all-to-all-start.3 = ((bf16[8,256,576]{1,2,0:T(8,128)(2,1)}), bf16[8,256,576]{1,2,0:T(8,128)(2,1)S(1)}, u32[]{:S(2)}, u32[]{:S(2)}) async-start(bf16[8,256,576]{1,2,0:T(8,128)(2,1)} %copy.150), calls=%async_computation.3 | async-start | bytes 4718592 | tf_op jit(solution)/shard_map/all_to_all | solution.py:878
  555.6 6.9 %copy-start.12 = (f32[1,576]{1,0:T(1,128)S(1)}, f32[1,576]{1,0:T(1,128)}, u32[]{:S(2)}) copy-start(f32[1,576]{1,0:T(1,128)} %get-tuple-element.51) | copy-start | bytes 6916
  556.5 2.3 collective-permute-start.10
  560.9 9.1 %collective-permute-start.11 = (bf16[2,2,2,144,128]{4,3,2,1,0:T(8,128)(2,1)S(1)}, bf16[2,2,2,144,128]{4,3,2,1,0:T(8,128)(2,1)S(1)}, u32[]{:S(2)}, u32[]{:S(2)}) collective-permute-start(bf16[2,2,2,144,128]{4,3,2,1,0:T(8,128)(2,1)S(1)} %dynamic-slice_bitcast_fusion.1), channel_id=1, source_target_pairs={{0,16},{8,24},{16,0},{24,8},{1,17},{9,25},{17,1},{25,9},{2,18},{10... | collective-permute-start | bytes 884744 | tf_op jit(solution)/shard_map/ppermute | solution.py:828
  562.5 10.7 %collective-permute-start.5 = (f32[2,576]{1,0:T(2,128)S(1)}, f32[2,576]{1,0:T(2,128)S(1)}, u32[]{:S(2)}, u32[]{:S(2)}) collective-permute-start(f32[2,576]{1,0:T(2,128)S(1)} %pad_maximum_fusion.7), channel_id=1, source_target_pairs={{0,8},{8,0},{16,24},{24,16},{1,9},{9,1},{17,25},{25,17},{2,10},{10... | collective-permute-start | bytes 13832 | tf_op jit(solution)/shard_map/ppermute | solution.py:828
  571.1 8.1 %collective-permute-start.12 = (bf16[2,2,144,128]{3,2,1,0:T(8,128)(2,1)S(1)}, bf16[2,2,144,128]{3,2,1,0:T(8,128)(2,1)S(1)}, u32[]{:S(2)}, u32[]{:S(2)}) collective-permute-start(bf16[2,2,144,128]{3,2,1,0:T(8,128)(2,1)S(1)} %dynamic-slice_bitcast_fusion.2), channel_id=1, source_target_pairs={{0,1},{1,0},{2,3},{3,2},{4,5},{5,4},{6,7},{7,6},{8,9},{9,8},{10,11... | collective-permute-start | bytes 442376 | tf_op jit(solution)/shard_map/ppermute | solution.py:828
  573.2 6.2 %collective-permute-start.6 = (f32[2,576]{1,0:T(2,128)S(1)}, f32[2,576]{1,0:T(2,128)S(1)}, u32[]{:S(2)}, u32[]{:S(2)}) collective-permute-start(f32[2,576]{1,0:T(2,128)S(1)} %fusion.21), channel_id=1, source_target_pairs={{0,16},{8,24},{16,0},{24,8},{1,17},{9,25},{17,1},{25,9},{2,18},{10... | collective-permute-start | bytes 13832 | tf_op jit(solution)/shard_map/ppermute | solution.py:828
  579.3 19.2 %collective-permute-start.13 = (bf16[2,144,128]{2,1,0:T(8,128)(2,1)S(1)}, bf16[2,144,128]{2,1,0:T(8,128)(2,1)S(1)}, u32[]{:S(2)}, u32[]{:S(2)}) collective-permute-start(bf16[2,144,128]{2,1,0:T(8,128)(2,1)S(1)} %dynamic-slice_bitcast_fusion.3), channel_id=1, source_target_pairs={{0,2},{1,3},{2,0},{3,1},{4,6},{5,7},{6,4},{7,5},{8,10},{9,11},{10,... | collective-permute-start | bytes 221192 | tf_op jit(solution)/shard_map/ppermute | solution.py:828
  579.4 3.7 collective-permute-start.7
  583.1 10.8 %collective-permute-start.8 = (f32[2,576]{1,0:T(2,128)S(1)}, f32[2,576]{1,0:T(2,128)S(1)}, u32[]{:S(2)}, u32[]{:S(2)}) collective-permute-start(f32[2,576]{1,0:T(2,128)S(1)} %add.137), channel_id=1, source_target_pairs={{0,2},{1,3},{2,0},{3,1},{4,6},{5,7},{6,4},{7,5},{8,10},{9,11},{10,... | collective-permute-start | bytes 13832 | tf_op jit(solution)/shard_map/ppermute | solution.py:828
  594.0 4.5 collective-permute-start.9
  598.6 4.9 collective-permute-start.14
  (15 other events, 58.2 us)
Sparse Core Ops, SparseCore 0:
  14.3 92.7 all-gather.2
  412.4 111.1 reduce-scatter.3

commit v2 on v1

--- a/solution.py
+++ b/solution.py
@@ -399,61 +399,7 @@
     return jnp.concatenate([first, second], axis=0)
 
 
-def qkv_kernel(x_ref, gain_ref, w_ref, cos_ref, sin_ref, q_ref, kt_ref, vt_ref, k_ref, v_ref, *, heads, kv_heads):
-    half = HD // 2
-    x = x_ref[...].astype(F32)
-    rstd = lax.rsqrt(jnp.mean(x * x, axis=-1, keepdims=True) + eps_norm)
-    normed = (x * rstd * gain_ref[...]).astype(BF16)
-    lin = dot(w_ref[...], normed, 1, 1)
-    cos, sin = cos_ref[...], sin_ref[...]
-    for head in range(heads + kv_heads):
-        top = lin[HD * head : HD * head + half]
-        low = lin[HD * head + half : HD * head + HD]
-        rot = jnp.concatenate([top * cos - low * sin, low * cos + top * sin], axis=0).astype(BF16)
-        if head < heads:
-            q_ref[HD * head : HD * head + HD, :] = rot * jnp.asarray(HD**-0.5, BF16)
-        else:
-            kv = head - heads
-            kt_ref[HD * kv : HD * kv + HD, :] = rot
-            k_ref[kv] = rot.T
-    for kv in range(kv_heads):
-        first = HD * (heads + kv_heads + kv)
-        val = lin[first : first + HD].astype(BF16)
-        vt_ref[HD * kv : HD * kv + HD, :] = val
-        v_ref[kv] = val.T
-
-
-def project_qkv(x, gain, w_t, cos_t, sin_t, heads, kv_heads, block=512):
-    tokens, width = x.shape
-    col = lambda rows: pl.BlockSpec((rows, block), lambda i: (0, i))
-    nat = pl.BlockSpec((kv_heads, block, HD), lambda i: (0, i, 0))
-    return pl.pallas_call(
-        functools.partial(qkv_kernel, heads=heads, kv_heads=kv_heads),
-        grid=(tokens // block,),
-        in_specs=[
-            pl.BlockSpec((block, width), lambda i: (i, 0)),
-            pl.BlockSpec((1, width), lambda i: (0, 0)),
-            pl.BlockSpec(w_t.shape, lambda i: (0, 0)),
-            col(HD // 2),
-            col(HD // 2),
-        ],
-        out_specs=[col(heads * HD), col(kv_heads * HD), col(kv_heads * HD), nat, nat],
-        out_shape=[
-            jax.ShapeDtypeStruct((heads * HD, tokens), BF16),
-            jax.ShapeDtypeStruct((kv_heads * HD, tokens), BF16),
-            jax.ShapeDtypeStruct((kv_heads * HD, tokens), BF16),
-            jax.ShapeDtypeStruct((kv_heads, tokens, HD), BF16),
-            jax.ShapeDtypeStruct((kv_heads, tokens, HD), BF16),
-        ],
-        compiler_params=pltpu.CompilerParams(vmem_limit_bytes=VMEM_BYTES),
-        cost_estimate=pl.CostEstimate(
-            flops=4 * tokens * width * w_t.shape[0], bytes_accessed=tokens * 5000, transcendentals=0
-        ),
-        name="project_qkv",
-    )(x, gain, w_t, cos_t, sin_t)
-
-
-def attend_kernel(inv_ref, q_ref, k_ref, v_ref, o_ref, on_ref, l_ref, *, blocks, span, group):
+def attend_kernel(inv_ref, q_ref, k_ref, v_ref, o_ref, l_ref, *, blocks, span, group):
     wide = 2 * span
     row = lax.broadcasted_iota(jnp.int32, (wide, wide), 0)
     col = lax.broadcasted_iota(jnp.int32, (wide, wide), 1)
@@ -498,12 +444,10 @@
             [p + jnp.log(t) for (p, t, _) in state] + [jnp.zeros((8 - group, wide), F32)], axis=0
         )
         mixed_low = mixed.astype(BF16)
-        natural = mixed.T.astype(BF16)
         for part in range(2):
             where = span_slice(inv_ref, 2 * block + part, span)
             cols = slice(part * span, part * span + span)
             o_ref[:, where] = mixed_low[:, cols]
-            on_ref[0, where, :] = natural[cols, :]
             l_ref[0, :, where] = logs[:, cols]
         return 0
 
@@ -525,13 +469,11 @@
             in_specs=[wide_spec, nat_spec, pl.BlockSpec((HD, tokens), lambda g, i: (g, 0))],
             out_specs=[
                 wide_spec,
-                pl.BlockSpec((1, tokens, group * HD), lambda g, i: (g, 0, 0)),
                 pl.BlockSpec((1, 8, tokens), lambda g, i: (g, 0, 0)),
             ],
         ),
         out_shape=[
             jax.ShapeDtypeStruct(q_t.shape, BF16),
-            jax.ShapeDtypeStruct((kv_heads, tokens, group * HD), BF16),
             jax.ShapeDtypeStruct((kv_heads, 8, tokens), F32),
         ],
         compiler_params=pltpu.CompilerParams(vmem_limit_bytes=VMEM_BYTES),
@@ -649,172 +591,452 @@
     )(inv, q_t, k_t, k_nat, v_nat, o_t, do_t, logs, cos_t, sin_t)
 
 
+def flip(index, bits):
+    for bit in bits:
+        index = index + bit * (1 - 2 * ((index // bit) % 2))
+    return index
+
+
+def bits_of(size):
+    return [1 << i for i in range(size.bit_length() - 1)]
+
+
+def chains(dp, seq):
+    far, near = [("seq", b) for b in reversed(bits_of(seq)[1:])], [("seq", b) for b in bits_of(seq)[:1]]
+    chip, core = [("dp", b) for b in reversed(bits_of(dp)[1:])], [("dp", b) for b in bits_of(dp)[:1]]
+    return far + near + chip + core, far + chip + near + core
+
+
+def arrival_order(stages, dp, seq, my_dp, my_seq):
+    ids = jnp.arange(dp * seq, dtype=jnp.int32)
+    away = {"dp": (ids // seq) ^ my_dp, "seq": (ids % seq) ^ my_seq}
+    place = jnp.zeros_like(ids)
+    for at, (axis, bit) in enumerate(stages):
+        place = place + (1 << at) * ((away[axis] // bit) % 2)
+    return place
+
+
+def bring_kernel(x_ref, first_ref, second_ref, out_ref, all_one_ref, all_two_ref,
+                 local_sem, x_send, x_recv, w_send, w_recv, *, dp, seq):
+    my_dp, my_seq = lax.axis_index("dp"), lax.axis_index("seq")
+    orders = chains(dp, seq)
+    barrier = pltpu.get_barrier_semaphore()
+    peers = [(my_dp, flip(my_seq, [b for b in bits_of(seq) if away & b])) for away in range(1, seq)]
+    peers += [(flip(my_dp, [b]), my_seq) for b in bits_of(dp)]
+    for peer in peers:
+        pl.semaphore_signal(barrier, inc=1, device_id=peer, device_id_type=pl.DeviceIdType.MESH)
+    pl.semaphore_wait(barrier, len(peers))
+
+    shards_in = (first_ref, second_ref)
+    gathered = (all_one_ref, all_two_ref)
+
+    def weight_copy(chain, stage):
+        axis, bit = orders[chain][stage]
+        held = 1 << stage
+        peer = (flip(my_dp, [bit]), my_seq) if axis == "dp" else (my_dp, flip(my_seq, [bit]))
+        source = shards_in[chain] if stage == 0 else gathered[chain].at[pl.ds(0, held)]
+        return pltpu.make_async_remote_copy(
+            src_ref=source,
+            dst_ref=gathered[chain].at[pl.ds(held, held)],
+            send_sem=w_send.at[chain, stage],
+            recv_sem=w_recv.at[chain, stage],
+            device_id=peer,
+            device_id_type=pl.DeviceIdType.MESH,
+        )
+
+    own = [
+        pltpu.make_async_copy(shards_in[c], gathered[c].at[pl.ds(0, 1)], local_sem.at[c]) for c in range(2)
+    ]
+    own.append(pltpu.make_async_copy(x_ref.at[my_seq], out_ref.at[my_seq], local_sem.at[2]))
+    for copy in own:
+        copy.start()
+    copies = [[weight_copy(c, s) for s in range(len(orders[c]))] for c in range(2)]
+    for c in range(2):
+        copies[c][0].start()
+    moves = []
+    for away in range(1, seq):
+        peer = flip(my_seq, [b for b in bits_of(seq) if away & b])
+        moves.append(
+            pltpu.make_async_remote_copy(
+                src_ref=x_ref.at[peer],
+                dst_ref=out_ref.at[my_seq],
+                send_sem=x_send.at[away - 1],
+                recv_sem=x_recv.at[away - 1],
+                device_id=(my_dp, peer),
+                device_id_type=pl.DeviceIdType.MESH,
+            )
+        )
+    for move in moves:
+        move.start()
+    for c in range(2):
+        own[c].wait()
+    for stage in range(1, len(orders[0])):
+        for c in range(2):
+            copies[c][stage - 1].wait_recv()
+            copies[c][stage].start()
+    for c in range(2):
+        copies[c][-1].wait_recv()
+        for copy in copies[c]:
+            copy.wait_send()
+    for move in moves:
+        move.wait()
+    own[2].wait()
+
+
+def bring(x, first, second):
+    dp, seq = lax.axis_size("dp"), lax.axis_size("seq")
+    stages = len(chains(dp, seq)[0])
+    hbm = pl.BlockSpec(memory_space=pl.ANY)
+    return pl.pallas_call(
+        functools.partial(bring_kernel, dp=dp, seq=seq),
+        in_specs=[hbm] * 3,
+        out_specs=[hbm] * 3,
+        out_shape=[
+            jax.ShapeDtypeStruct(x.shape, x.dtype),
+            jax.ShapeDtypeStruct((dp * seq, *first.shape[1:]), first.dtype),
+            jax.ShapeDtypeStruct((dp * seq, *second.shape[1:]), second.dtype),
+        ],
+        scratch_shapes=[
+            pltpu.SemaphoreType.DMA((3,)),
+            pltpu.SemaphoreType.DMA((seq - 1,)),
+            pltpu.SemaphoreType.DMA((seq - 1,)),
+            pltpu.SemaphoreType.DMA((2, stages)),
+            pltpu.SemaphoreType.DMA((2, stages)),
+        ],
+        compiler_params=pltpu.CompilerParams(
+            collective_id=1, has_side_effects=True, vmem_limit_bytes=VMEM_BYTES
+        ),
+        name="bring",
+    )(x, first, second)
+
+
+def qkv_kernel(where_ref, x_ref, gain_ref, packed_ref, cos_ref, sin_ref,
+               q_ref, kt_ref, vt_ref, k_ref, v_ref, w_ref, w_wide, *, heads, kv_heads, dp, seq):
+    half = HD // 2
+    width = w_ref.shape[1]
+    q_cols, kv_cols = width // seq, kv_heads * HD // seq
+    kv_width = kv_heads * HD
+
+    @pl.when(pl.program_id(0) == 0)
+    def _():
+        for s in range(seq):
+            block = jnp.concatenate([packed_ref[where_ref[d * seq + s]] for d in range(dp)], axis=0)
+            turned = block.astype(F32).T
+            w_wide[q_cols * s : q_cols * s + q_cols, :] = turned[:q_cols]
+            first = width + kv_cols * s
+            w_wide[first : first + kv_cols, :] = turned[q_cols : q_cols + kv_cols]
+            first += kv_width
+            w_wide[first : first + kv_cols, :] = turned[q_cols + kv_cols : q_cols + 2 * kv_cols]
+        w_ref[...] = w_wide[...].astype(BF16)
+
+    x = x_ref[0].astype(F32)
+    rstd = lax.rsqrt(jnp.mean(x * x, axis=0, keepdims=True) + eps_norm)
+    normed = (x * rstd * gain_ref[...]).astype(BF16)
+    lin = dot(w_ref[...], normed, 1, 0)
+    cos, sin = cos_ref[...], sin_ref[...]
+    for head in range(heads + kv_heads):
+        top = lin[HD * head : HD * head + half]
+        low = lin[HD * head + half : HD * head + HD]
+        rot = jnp.concatenate([top * cos - low * sin, low * cos + top * sin], axis=0)
+        if head < heads:
+            q_ref[HD * head : HD * head + HD, :] = rot.astype(BF16) * jnp.asarray(HD**-0.5, BF16)
+        else:
+            kv = head - heads
+            kt_ref[HD * kv : HD * kv + HD, :] = rot.astype(BF16)
+            k_ref[kv] = rot.T.astype(BF16)
+    for kv in range(kv_heads):
+        first = HD * (heads + kv_heads + kv)
+        val = lin[first : first + HD]
+        vt_ref[HD * kv : HD * kv + HD, :] = val.astype(BF16)
+        v_ref[kv] = val.T.astype(BF16)
+
+
+def project_qkv(where, x, gain, packed, cos_t, sin_t, heads, kv_heads, rows):
+    blocks, width, block = x.shape
+    tokens = blocks * block
+    feats = (heads + 2 * kv_heads) * HD
+    dp, seq = lax.axis_size("dp"), lax.axis_size("seq")
+    col = lambda rows: pl.BlockSpec((rows, block), lambda i, w: (0, i))
+    nat = pl.BlockSpec((kv_heads, block, HD), lambda i, w: (0, i, 0))
+    return pl.pallas_call(
+        functools.partial(qkv_kernel, heads=heads, kv_heads=kv_heads, dp=dp, seq=seq),
+        grid_spec=pltpu.PrefetchScalarGridSpec(
+            num_scalar_prefetch=1,
+            grid=(blocks,),
+            in_specs=[
+                pl.BlockSpec((1, width, block), lambda i, w: (i, 0, 0)),
+                pl.BlockSpec((width, 1), lambda i, w: (0, 0)),
+                pl.BlockSpec((dp * seq, rows, packed.shape[2]), lambda i, w: (0, 0, 0)),
+                col(HD // 2),
+                col(HD // 2),
+            ],
+            out_specs=[
+                col(heads * HD), col(kv_heads * HD), col(kv_heads * HD), nat, nat,
+                pl.BlockSpec((feats, width), lambda i, w: (0, 0)),
+            ],
+            scratch_shapes=[pltpu.VMEM((feats, width), F32)],
+        ),
+        out_shape=[
+            jax.ShapeDtypeStruct((heads * HD, tokens), BF16),
+            jax.ShapeDtypeStruct((kv_heads * HD, tokens), BF16),
+            jax.ShapeDtypeStruct((kv_heads * HD, tokens), BF16),
+            jax.ShapeDtypeStruct((kv_heads, tokens, HD), BF16),
+            jax.ShapeDtypeStruct((kv_heads, tokens, HD), BF16),
+            jax.ShapeDtypeStruct((feats, width), BF16),
+        ],
+        compiler_params=pltpu.CompilerParams(vmem_limit_bytes=VMEM_BYTES),
+        cost_estimate=pl.CostEstimate(
+            flops=4 * tokens * width * feats, bytes_accessed=tokens * 5000, transcendentals=0
+        ),
+        name="project_qkv",
+    )(where, x, gain, packed, cos_t, sin_t)
+
+
+def side_by_side(ref):
+    return jnp.concatenate([ref[i] for i in range(ref.shape[0])], axis=1)
+
+
 def mlp_kernel(
-    x_ref, mixed_ref, mixed_t_ref, dy_ref, gain_ref, o_ref, gate_ref, up_ref, down_ref,
-    out_ref, dmid_ref, dmixed_ref, o_grad_ref, gate_grad_ref, up_grad_ref, down_grad_ref, gain_grad_ref,
-    o_sum, gate_sum, up_sum, down_sum, gain_sum, *, chunk,
+    one_ref, two_ref, x_ref, mixed_ref, dy_ref, gain_ref, o_pack, gate_pack, rest_pack,
+    out_ref, dmid_ref, dmixed_ref, grads_ref, gain_grad_ref,
+    o_w, o_t, gate_w, gate_t, up_w, up_t, down_w, down_t, o_sum, gate_sum, up_sum, down_sum, gain_sum,
+    *, chunk, dp, seq,
 ):
     step, steps = pl.program_id(0), pl.num_programs(0)
-    groups, _, group_width = mixed_ref.shape
-    ff = gate_ref.shape[1]
+    width, ff = gate_w.shape
+    lanes = o_pack.shape[2]
+    rows = width // dp
+    o_cols, ff_cols, ff_rows = width // seq, ff // seq, ff // dp
+    spare = ff_cols - lanes
+    padded = -(-o_cols // 16) * 16
 
     @pl.when(step == 0)
     def _():
+        for total in (o_sum, gate_sum, up_sum, down_sum, gain_sum):
+            total[...] = jnp.zeros_like(total)
+        for s in range(seq):
+            ones = [one_ref[d * seq + s] for d in range(dp)]
+            twos = [two_ref[d * seq + s] for d in range(dp)]
+            stack = lambda ref, where, first: jnp.concatenate(
+                [ref[w, first : first + rows, :] for w in where], axis=0
+            ).astype(F32).T
+            o_sum[o_cols * s : o_cols * s + o_cols, :] = stack(o_pack, ones, 0)[:o_cols]
+            gate_t[ff_cols * s : ff_cols * s + lanes, :] = stack(gate_pack, ones, 0).astype(BF16)
+            up_t[ff_cols * s : ff_cols * s + lanes, :] = stack(rest_pack, twos, 0).astype(BF16)
+            both = stack(rest_pack, twos, rows).astype(BF16)
+            gate_t[ff_cols * s + lanes : ff_cols * (s + 1), :] = both[:spare]
+            up_t[ff_cols * s + lanes : ff_cols * (s + 1), :] = both[spare : 2 * spare]
+            for d in range(dp):
+                for t in range(ff_rows // lanes):
+                    first = 2 * rows + padded * t
+                    piece = rest_pack[twos[d], first : first + padded, :].astype(F32)[:o_cols]
+                    cols = slice(ff_rows * d + lanes * t, ff_rows * d + lanes * (t + 1))
+                    down_sum[o_cols * s : o_cols * s + o_cols, cols] = piece
+        o_t[...] = o_sum[...].astype(BF16)
+        o_w[...] = o_sum[...].T.astype(BF16)
+        down_t[...] = down_sum[...].astype(BF16)
+        for first in range(0, ff, lanes):
+            part = slice(first, first + lanes)
+            down_w[part, :] = down_sum[:, part].T.astype(BF16)
+            gate_w[:, part] = gate_t[part, :].T
+            up_w[:, part] = up_t[part, :].T
         o_sum[...] = jnp.zeros_like(o_sum)
-        gate_sum[...] = jnp.zeros_like(gate_sum)
-        up_sum[...] = jnp.zeros_like(up_sum)
         down_sum[...] = jnp.zeros_like(down_sum)
-        gain_sum[...] = jnp.zeros_like(gain_sum)
 
     gain = gain_ref[...]
-    mid = x_ref[...].astype(F32)
-    for g in range(groups):
-        mid += dot(mixed_ref[g], o_ref[g * group_width : (g + 1) * group_width, :], 1, 0)
-    rstd = lax.rsqrt(jnp.mean(mid * mid, axis=-1, keepdims=True) + eps_norm)
+    mixed = mixed_ref[...]
+    mid = dot(o_t[...], mixed, 1, 0) + side_by_side(x_ref).astype(F32)
+    rstd = lax.rsqrt(jnp.mean(mid * mid, axis=0, keepdims=True) + eps_norm)
     normed = (mid * rstd * gain).astype(BF16)
-    normed_t = normed.T
-    dy = dy_ref[...]
-    dy_t = dy.T
-    mlp_out = jnp.zeros_like(mid)
+    dy = side_by_side(dy_ref)
+    added = jnp.zeros_like(mid)
     dnormed = jnp.zeros_like(mid)
     for first in range(0, ff, chunk):
-        cols = slice(first, first + chunk)
-        gate = dot(normed, gate_ref[:, cols], 1, 0)
-        up = dot(normed, up_ref[:, cols], 1, 0)
-        dinner = dot(dy, down_ref[:, cols], 1, 0)
+        part = slice(first, first + chunk)
+        gate = dot(gate_t[part, :], normed, 1, 0)
+        up = dot(up_t[part, :], normed, 1, 0)
+        dinner = dot(down_w[part, :], dy, 1, 0)
         sig = 1.0 / (1.0 + jnp.exp(-gate))
         silu = gate * sig
         inner = (silu * up).astype(BF16)
         dup = (dinner * silu).astype(BF16)
         dgate = (dinner * up * sig * (1.0 + gate * (1.0 - sig))).astype(BF16)
-        mlp_out += dot(inner, down_ref[:, cols], 1, 1)
-        dnormed += dot(dgate, gate_ref[:, cols], 1, 1)
-        dnormed += dot(dup, up_ref[:, cols], 1, 1)
-        down_sum[:, cols] += dot(dy_t, inner, 1, 0)
-        gate_sum[:, cols] += dot(normed_t, dgate, 1, 0)
-        up_sum[:, cols] += dot(normed_t, dup, 1, 0)
-    out_ref[...] = (mid + mlp_out).astype(BF16)
+        added += dot(down_t[:, part], inner, 1, 0)
+        dnormed += dot(gate_w[:, part], dgate, 1, 0)
+        dnormed += dot(up_w[:, part], dup, 1, 0)
+        down_sum[:, part] += dot(dy, inner, 1, 1)
+        gate_sum[part, :] += dot(dgate, normed, 1, 1)
+        up_sum[part, :] += dot(dup, normed, 1, 1)
+    out = (mid + added).astype(BF16)
     scaled_mid = mid * rstd
-    gain_sum[...] += jnp.sum((dnormed * scaled_mid).reshape(-1, 8, mid.shape[1]), axis=0)
+    product = dnormed * scaled_mid
+    gain_sum[...] += sum(product[:, c : c + lanes] for c in range(0, product.shape[1], lanes))
     scaled = dnormed * gain
-    pull = jnp.mean(scaled * mid, axis=-1, keepdims=True)
+    pull = jnp.mean(scaled * mid, axis=0, keepdims=True)
     dmid = dy.astype(F32) + rstd * scaled - scaled_mid * (rstd * rstd * pull)
-    dmid_ref[...] = dmid
     dmid_low = dmid.astype(BF16)
-    o_sum[...] += dot(mixed_t_ref[...], dmid_low, 1, 0)
-    dmixed_ref[...] = dot(o_ref[...], dmid_low, 1, 1).astype(BF16)
+    block = out_ref.shape[2]
+    for i in range(out_ref.shape[0]):
+        out_ref[i] = out[:, block * i : block * (i + 1)]
+        dmid_ref[i] = dmid[:, block * i : block * (i + 1)]
+    o_sum[...] += dot(dmid_low, mixed, 1, 1)
+    dmixed_ref[...] = dot(o_w[...], dmid_low, 1, 0).astype(BF16)
 
     @pl.when(step == steps - 1)
     def _():
-        o_grad_ref[...] = o_sum[...].astype(BF16)
-        gate_grad_ref[...] = gate_sum[...].astype(BF16)
-        up_grad_ref[...] = up_sum[...].astype(BF16)
-        down_grad_ref[...] = down_sum[...].astype(BF16)
-        gain_grad_ref[...] = jnp.sum(gain_sum[...], axis=0, keepdims=True)
-
-
-def mlp_both(x, mixed, mixed_t, dy, gain, o_w, gate_w, up_w, down_t, block=256, chunk=512):
-    tokens, width = x.shape
-    groups, _, group_width = mixed.shape
-    ff = gate_w.shape[1]
-    tok = pl.BlockSpec((block, width), lambda i: (i, 0))
-    col = pl.BlockSpec((width, block), lambda i: (0, i))
-    once = lambda shape: pl.BlockSpec(shape, lambda i: (0, 0), pipeline_mode=pl.Buffered(1))
+        gain_grad_ref[...] = gain_sum[...]
+        for s in range(seq):
+            tall = lambda total, first, count: total[first : first + count, :]
+            blank = jnp.zeros((lanes - o_cols, width), F32)
+            o_piece = jnp.concatenate([tall(o_sum, o_cols * s, o_cols), blank], axis=0).T.astype(BF16)
+            gate_piece = tall(gate_sum, ff_cols * s, lanes).T.astype(BF16)
+            up_piece = tall(up_sum, ff_cols * s, lanes).T.astype(BF16)
+            both = jnp.concatenate(
+                [tall(gate_sum, ff_cols * s + lanes, spare), tall(up_sum, ff_cols * s + lanes, spare)], axis=0
+            ).T.astype(BF16)
+            for d in range(dp):
+                at = d * seq + s
+                band = slice(rows * d, rows * (d + 1))
+                for i, piece in enumerate((o_piece, gate_piece, up_piece, both)):
+                    grads_ref[at, rows * i : rows * (i + 1), :] = piece[band]
+                for t in range(ff_rows // lanes):
+                    first = 4 * rows + padded * t
+                    cols = slice(ff_rows * d + lanes * t, ff_rows * d + lanes * (t + 1))
+                    piece = down_sum[o_cols * s : o_cols * (s + 1), cols]
+                    piece = jnp.concatenate([piece, jnp.zeros((padded - o_cols, lanes), F32)], axis=0)
+                    grads_ref[at, first : first + padded, :] = piece.astype(BF16)
+
+
+def mlp_both(one, two, x, mixed, dy, gain, first_pack, second_pack, ff, rows, batch=2, chunk=512):
+    blocks, width, block = x.shape
+    tokens = blocks * block
+    dp, seq = lax.axis_size("dp"), lax.axis_size("seq")
+    lanes = first_pack.shape[2]
+    tok = pl.BlockSpec((batch, width, block), lambda i, a, b: (i, 0, 0))
+    col = pl.BlockSpec((width, batch * block), lambda i, a, b: (0, i))
+    single = pl.Buffered(1)
+    once = lambda shape: pl.BlockSpec(shape, lambda i, a, b: (0,) * len(shape), pipeline_mode=single)
+    pick = lambda which: pl.BlockSpec(
+        (dp * seq, rows, lanes), lambda i, a, b: (0, which, 0), pipeline_mode=single
+    )
+    grad_rows = first_pack.shape[1] - rows + second_pack.shape[1]
     return pl.pallas_call(
-        functools.partial(mlp_kernel, chunk=chunk),
-        grid=(tokens // block,),
-        in_specs=[
-            tok,
-            pl.BlockSpec((groups, block, group_width), lambda i: (0, i, 0)),
-            col,
-            tok,
-            once((1, width)),
-            once((width, width)),
-            once((width, ff)),
-            once((width, ff)),
-            once((width, ff)),
+        functools.partial(mlp_kernel, chunk=chunk, dp=dp, seq=seq),
+        grid_spec=pltpu.PrefetchScalarGridSpec(
+            num_scalar_prefetch=2,
+            grid=(blocks // batch,),
+            in_specs=[tok, col, tok, once((width, 1)), pick(1), pick(2), once(second_pack.shape)],
+            out_specs=[tok, tok, col, once((dp * seq, grad_rows, lanes)), once((width, lanes))],
+            scratch_shapes=[
+                pltpu.VMEM((width, width), BF16),
+                pltpu.VMEM((width, width), BF16),
+                pltpu.VMEM((width, ff), BF16),
+                pltpu.VMEM((ff, width), BF16),
+                pltpu.VMEM((width, ff), BF16),
+                pltpu.VMEM((ff, width), BF16),
+                pltpu.VMEM((ff, width), BF16),
+                pltpu.VMEM((width, ff), BF16),
+                pltpu.VMEM((width, width), F32),
+                pltpu.VMEM((ff, width), F32),
+                pltpu.VMEM((ff, width), F32),
+                pltpu.VMEM((width, ff), F32),
+                pltpu.VMEM((width, lanes), F32),
+            ],
+        ),
+        out_shape=[
+            jax.ShapeDtypeStruct(x.shape, BF16),
+            jax.ShapeDtypeStruct(x.shape, F32),
+            jax.ShapeDtypeStruct((width, tokens), BF16),
+            jax.ShapeDtypeStruct((dp * seq, grad_rows, lanes), BF16),
+            jax.ShapeDtypeStruct((width, lanes), F32),
         ],
-        out_specs=[
-            tok, tok, col,
-            once((width, width)), once((width, ff)), once((width, ff)), once((width, ff)), once((1, width)),
-        ],
-        out_shape=[
-            jax.ShapeDtypeStruct((tokens, width), BF16),
-            jax.ShapeDtypeStruct((tokens, width), F32),
-            jax.ShapeDtypeStruct((width, tokens), BF16),
-            jax.ShapeDtypeStruct((width, width), BF16),
-            jax.ShapeDtypeStruct((width, ff), BF16),
-            jax.ShapeDtypeStruct((width, ff), BF16),
-            jax.ShapeDtypeStruct((width, ff), BF16),
-            jax.ShapeDtypeStruct((1, width), F32),
-        ],
-        scratch_shapes=[
-            pltpu.VMEM((width, width), F32),
-            pltpu.VMEM((width, ff), F32),
-            pltpu.VMEM((width, ff), F32),
-            pltpu.VMEM((width, ff), F32),
-            pltpu.VMEM((8, width), F32),
-        ],
-        compiler_params=pltpu.CompilerParams(vmem_limit_bytes=VMEM_BYTES),
+        compiler_params=pltpu.CompilerParams(vmem_limit_bytes=60 * 2**20),
         cost_estimate=pl.CostEstimate(
             flops=2 * tokens * width * (9 * ff + 3 * width),
             bytes_accessed=tokens * width * 14,
             transcendentals=tokens * ff,
         ),
         name="mlp_both",
-    )(x, mixed, mixed_t, dy, gain, o_w, gate_w, up_w, down_t)
+    )(one, two, x, mixed, dy, gain, first_pack, first_pack, second_pack)
 
 
 def qkv_back_kernel(
-    x_ref, dmid_ref, dq_ref, dk_ref, dv_ref, gain_ref, w_ref,
-    din_ref, w_grad_ref, gain_grad_ref, w_sum, gain_sum,
+    x_ref, dmid_ref, dq_ref, dk_ref, dv_ref, gain_ref, w_t_ref,
+    din_ref, grads_ref, gain_grad_ref, w_nat, w_sum, gain_sum, *, dp, seq, kv_width,
 ):
     step, steps = pl.program_id(0), pl.num_programs(0)
+    width = w_nat.shape[0]
+    lanes = grads_ref.shape[2]
+    rows = width // dp
+    q_cols, kv_cols = width // seq, kv_width // seq
 
     @pl.when(step == 0)
     def _():
         w_sum[...] = jnp.zeros_like(w_sum)
         gain_sum[...] = jnp.zeros_like(gain_sum)
+        w_nat[...] = w_t_ref[...].T
 
     gain = gain_ref[...]
-    x = x_ref[...].astype(F32)
-    rstd = lax.rsqrt(jnp.mean(x * x, axis=-1, keepdims=True) + eps_norm)
+    x = side_by_side(x_ref).astype(F32)
+    rstd = lax.rsqrt(jnp.mean(x * x, axis=0, keepdims=True) + eps_norm)
     scaled_x = x * rstd
     normed = (scaled_x * gain).astype(BF16)
     dlin = jnp.concatenate([dq_ref[...], dk_ref[...], dv_ref[...]], axis=0)
-    w_sum[...] += dot(dlin, normed, 1, 0)
-    dnormed = dot(dlin, w_ref[...], 0, 0)
-    gain_sum[...] += jnp.sum((dnormed * scaled_x).reshape(-1, 8, x.shape[1]), axis=0)
+    w_sum[...] += dot(dlin, normed, 1, 1)
+    dnormed = dot(w_nat[...], dlin, 1, 0)
+    product = dnormed * scaled_x
+    gain_sum[...] += sum(product[:, c : c + lanes] for c in range(0, product.shape[1], lanes))
     scaled = dnormed * gain
-    pull = jnp.mean(scaled * x, axis=-1, keepdims=True)
-    din_ref[...] = (dmid_ref[...] + rstd * scaled - scaled_x * (rstd * rstd * pull)).astype(BF16)
+    pull = jnp.mean(scaled * x, axis=0, keepdims=True)
+    din = side_by_side(dmid_ref) + rstd * scaled - scaled_x * (rstd * rstd * pull)
+    block = din_ref.shape[2]
+    for i in range(din_ref.shape[0]):
+        din_ref[i] = din[:, block * i : block * (i + 1)].astype(BF16)
 
     @pl.when(step == steps - 1)
     def _():
-        w_grad_ref[...] = w_sum[...].astype(BF16)
-        gain_grad_ref[...] = jnp.sum(gain_sum[...], axis=0, keepdims=True)
-
-
-def project_back(x, dmid, dq_t, dk_t, dv_t, gain, w_t, block=512):
-    tokens, width = x.shape
+        gain_grad_ref[...] = gain_sum[...]
+        blank = jnp.zeros((lanes - q_cols - 2 * kv_cols, width), F32)
+        for s in range(seq):
+            first = width + kv_cols * s
+            piece = jnp.concatenate(
+                [
+                    w_sum[q_cols * s : q_cols * (s + 1), :],
+                    w_sum[first : first + kv_cols, :],
+                    w_sum[first + kv_width : first + kv_width + kv_cols, :],
+                    blank,
+                ],
+                axis=0,
+            ).T.astype(BF16)
+            for d in range(dp):
+                grads_ref[d * seq + s] = piece[rows * d : rows * (d + 1)]
+
+
+def project_back(x, dmid, dq_t, dk_t, dv_t, gain, w_t, lanes, batch=2):
+    blocks, width, block = x.shape
+    tokens = blocks * block
     feats = w_t.shape[0]
-    tok = pl.BlockSpec((block, width), lambda i: (i, 0))
-    col = lambda rows: pl.BlockSpec((rows, block), lambda i: (0, i))
-    once = lambda shape: pl.BlockSpec(shape, lambda i: (0, 0), pipeline_mode=pl.Buffered(1))
+    dp, seq = lax.axis_size("dp"), lax.axis_size("seq")
+    tok = pl.BlockSpec((batch, width, block), lambda i: (i, 0, 0))
+    col = lambda rows: pl.BlockSpec((rows, batch * block), lambda i: (0, i))
+    once = lambda shape: pl.BlockSpec(shape, lambda i: (0,) * len(shape), pipeline_mode=pl.Buffered(1))
+    packed = (dp * seq, width // dp, lanes)
     return pl.pallas_call(
-        qkv_back_kernel,
-        grid=(tokens // block,),
+        functools.partial(qkv_back_kernel, dp=dp, seq=seq, kv_width=dk_t.shape[0]),
+        grid=(blocks // batch,),
         in_specs=[
             tok, tok, col(dq_t.shape[0]), col(dk_t.shape[0]), col(dv_t.shape[0]),
-            once((1, width)), once((feats, width)),
+            once((width, 1)), once((feats, width)),
         ],
-        out_specs=[tok, once((feats, width)), once((1, width))],
+        out_specs=[tok, once(packed), once((width, lanes))],
         out_shape=[
-            jax.ShapeDtypeStruct((tokens, width), BF16),
-            jax.ShapeDtypeStruct((feats, width), BF16),
-            jax.ShapeDtypeStruct((1, width), F32),
+            jax.ShapeDtypeStruct(x.shape, BF16),
+            jax.ShapeDtypeStruct(packed, BF16),
+            jax.ShapeDtypeStruct((width, lanes), F32),
         ],
-        scratch_shapes=[pltpu.VMEM((feats, width), F32), pltpu.VMEM((8, width), F32)],
+        scratch_shapes=[
+            pltpu.VMEM((width, feats), BF16), pltpu.VMEM((feats, width), F32), pltpu.VMEM((width, lanes), F32),
+        ],
         compiler_params=pltpu.CompilerParams(vmem_limit_bytes=VMEM_BYTES),
         cost_estimate=pl.CostEstimate(
             flops=4 * tokens * width * feats, bytes_accessed=tokens * width * 12, transcendentals=0
@@ -828,31 +1050,11 @@
     return lax.ppermute(array, axis, [(i, i ^ bit) for i in range(size)])
 
 
-def bits_of(axis):
-    size = lax.axis_size(axis)
-    return [1 << i for i in range(size.bit_length() - 1)]
-
-
-def gather_doubling(array):
-    whole = array[None]
-    for axis in ("seq", "dp"):
-        for bit in bits_of(axis):
-            upper = (lax.axis_index(axis) // bit) % 2 == 1
-            other = swap(whole, axis, bit)
-            whole = jnp.concatenate([jnp.where(upper, other, whole), jnp.where(upper, whole, other)], axis=0)
-    return whole.reshape(lax.axis_size("dp"), lax.axis_size("seq"), *array.shape)
-
-
-def scatter_halving(array):
-    rows, lanes = array.shape[2:]
-    part = array.reshape(-1, rows, lanes)
-    order = [("dp", b) for b in bits_of("dp")]
-    seq_bits = [("seq", b) for b in bits_of("seq")]
-    seq_size = lax.axis_size("seq")
-    dims = [2] * (len(order) + len(seq_bits))
-    part = part.reshape(*dims, rows, lanes)
-    names = [("dp", b) for b in reversed(bits_of("dp"))] + [("seq", b) for b in reversed(bits_of("seq"))]
-    for axis, bit in order + seq_bits:
+def scatter_halving(array, dp, seq):
+    rows, lanes = array.shape[1:]
+    names = [("dp", b) for b in reversed(bits_of(dp))] + [("seq", b) for b in reversed(bits_of(seq))]
+    part = array.reshape(*[2] * len(names), rows, lanes)
+    for axis, bit in [("dp", b) for b in bits_of(dp)] + [("seq", b) for b in bits_of(seq)]:
         place = names.index((axis, bit))
         names.pop(place)
         upper = (lax.axis_index(axis) // bit) % 2
@@ -862,142 +1064,94 @@
     return part.reshape(rows, lanes)
 
 
-def sum_doubling(array):
-    for axis in ("dp", "seq"):
-        for bit in bits_of(axis):
+def sum_doubling(array, dp, seq):
+    for axis, size in (("dp", dp), ("seq", seq)):
+        for bit in bits_of(size):
             array = array + swap(array, axis, bit)
     return array
 
 
-def to_sequences(block):
-    moved = lax.all_to_all(block, "seq", 0, 0, tiled=True)
-    return moved.reshape(-1, block.shape[2])
-
-
-def to_slots(tokens, seqs):
-    moved = lax.all_to_all(tokens.reshape(seqs, -1, tokens.shape[1]), "seq", 0, 0, tiled=True)
-    return moved
-
-
-def fold(matrix, lanes=128):
-    rows, cols = matrix.shape[-2:]
-    full = cols // lanes * lanes
-    parts = [matrix[..., :, c : c + lanes] for c in range(0, full, lanes)]
-    if full < cols:
-        rest = matrix[..., :, full:]
-        parts.append(jnp.concatenate([rest[..., : rows // 2, :], rest[..., rows // 2 :, :]], axis=-1))
-    return jnp.concatenate(parts, axis=-2)
-
-
-def unfold(packed, rows, cols, lanes=128):
-    full = cols // lanes
-    parts = [packed[..., i * rows : (i + 1) * rows, :] for i in range(full)]
-    if full * lanes < cols:
-        rest = packed[..., full * rows :, :]
-        parts.append(jnp.concatenate([rest[..., :, : lanes // 2], rest[..., :, lanes // 2 :]], axis=-2))
-    return jnp.concatenate(parts, axis=-1)
-
-
-def pad_lanes(matrix, lanes=128):
-    return jnp.pad(matrix, [(0, 0)] * (matrix.ndim - 1) + [(0, lanes - matrix.shape[-1])])
-
-
-def join(blocks):
-    dp, seq, rows, cols = blocks.shape
-    return blocks.transpose(0, 2, 1, 3).reshape(dp * rows, seq * cols)
-
-
-def cut(matrix, dp, seq):
-    rows, cols = matrix.shape
-    return matrix.reshape(dp, rows // dp, seq, cols // seq).transpose(0, 2, 1, 3)
+def exchange(blocks):
+    return lax.all_to_all(blocks, "seq", 0, 0, tiled=True)
+
+
+def pad_lanes(matrix, lanes):
+    return jnp.pad(matrix, ((0, 0), (0, lanes - matrix.shape[1])))
 
 
 def shards_sequences(
     hidden_in, span_order, attn_gain, q_weight, k_weight, v_weight, o_weight, mlp_gain,
     gate_weight, up_weight, down_weight, out_grad,
 ):
+    lanes = 128
     seqs, slots, width = hidden_in.shape
     dp, seq = lax.axis_size("dp"), lax.axis_size("seq")
     tokens = slots * seq
-    spans = span_order.shape[0]
-    span = tokens // spans
+    span = tokens // span_order.shape[0]
     heads = width // HD
     kv_heads = k_weight.shape[1] * seq // HD
     rows, q_cols = q_weight.shape
     kv_cols = k_weight.shape[1]
-
-    x = to_sequences(hidden_in)
-    qkv_shard = pad_lanes(jnp.concatenate([q_weight, k_weight, v_weight], axis=1))
-    qkv_all = gather_doubling(qkv_shard)
-    dy = to_sequences(out_grad)
-
-    rest_shard = jnp.concatenate(
-        [fold(gate_weight), fold(up_weight), fold(down_weight.T), pad_lanes(o_weight)], axis=0
-    )
-    rest_all = lax.all_gather(rest_shard, ("dp", "seq"), axis=0, tiled=False)
-    rest_all = rest_all.reshape(dp, seq, *rest_shard.shape)
-
+    ff = down_weight.shape[0] * dp
+    ff_rows = down_weight.shape[0]
+    padded = -(-q_cols // 16) * 16
+
+    first = jnp.concatenate(
+        [
+            pad_lanes(jnp.concatenate([q_weight, k_weight, v_weight], axis=1), lanes),
+            pad_lanes(o_weight, lanes),
+            gate_weight[:, :lanes],
+        ],
+        axis=0,
+    )
+    down_turned = jnp.pad(down_weight.T, ((0, padded - q_cols), (0, 0)))
+    second = jnp.concatenate(
+        [up_weight[:, :lanes], jnp.concatenate([gate_weight[:, lanes:], up_weight[:, lanes:]], axis=1)]
+        + [down_turned[:, c : c + lanes] for c in range(0, ff_rows, lanes)],
+        axis=0,
+    )
+    x, first_all, second_all = bring(hidden_in.transpose(0, 2, 1), first[None], second[None])
+    out_grad, x = lax.optimization_barrier((out_grad, x))
+    dy = exchange(out_grad.transpose(0, 2, 1))
+
+    my_dp, my_seq = lax.axis_index("dp"), lax.axis_index("seq")
+    where_one, where_two = [arrival_order(c, dp, seq, my_dp, my_seq) for c in chains(dp, seq)]
     inv = jnp.argsort(span_order).astype(jnp.int32)
     slot_pos = slot_positions(jnp.arange(tokens, dtype=jnp.int32), span_order, span)
     inv_freq = rope_base ** (-(jnp.arange(HD // 2, dtype=F32) * 2.0) / HD)
     angles = slot_pos.astype(F32)[None, :] * inv_freq[:, None]
     cos_t, sin_t = jnp.cos(angles), jnp.sin(angles)
-    gain_one = attn_gain.astype(F32)[None]
-    gain_two = mlp_gain.astype(F32)[None]
-
-    by_feature = qkv_all.transpose(1, 3, 0, 2).reshape(seq, qkv_shard.shape[1], width)
-    w_t = jnp.concatenate(
-        [
-            by_feature[:, :q_cols].reshape(-1, width),
-            by_feature[:, q_cols : q_cols + kv_cols].reshape(-1, width),
-            by_feature[:, q_cols + kv_cols : q_cols + 2 * kv_cols].reshape(-1, width),
-        ],
-        axis=0,
-    )
-    q_t, k_t, v_t, k_nat, v_nat = project_qkv(x, gain_one, w_t, cos_t, sin_t, heads, kv_heads)
-    o_t, o_nat, logs = attention_forward(inv, q_t, k_nat, v_t, span)
-
-    g_rows, g_cols = gate_weight.shape
-    d_rows, d_cols = down_weight.shape
-    part = g_rows * g_cols // 128
-    down_part = d_rows * d_cols // 128
-    gate_w = join(unfold(rest_all[:, :, :part], g_rows, g_cols))
-    up_w = join(unfold(rest_all[:, :, part : 2 * part], g_rows, g_cols))
-    down_blocks = unfold(rest_all[:, :, 2 * part : 2 * part + down_part], d_cols, d_rows)
-    down_t = down_blocks.transpose(1, 2, 0, 3).reshape(seq * d_cols, dp * d_rows)
-    o_cols = o_weight.shape[1]
-    o_w = join(rest_all[:, :, 2 * part + down_part :, :o_cols])
-
-    out, dmid, do_t, o_grad, gate_grad, up_grad, down_grad_t, gain_two_grad = mlp_both(
-        x, o_nat, o_t, dy, gain_two, o_w, gate_w, up_w, down_t
-    )
-    hidden_out = to_slots(out, seqs)
-    down_cut = down_grad_t.reshape(seq, d_cols, dp, d_rows).transpose(2, 0, 1, 3)
-    rest_grads = jnp.concatenate(
-        [
-            fold(cut(gate_grad, dp, seq)),
-            fold(cut(up_grad, dp, seq)),
-            fold(down_cut),
-            pad_lanes(cut(o_grad, dp, seq)),
-        ],
-        axis=2,
-    )
-    rest_sum = lax.psum_scatter(
-        rest_grads.reshape(dp * seq, *rest_grads.shape[2:]), ("dp", "seq"), scatter_dimension=0, tiled=True
-    )[0].astype(F32)
+    gain_one = attn_gain.astype(F32)[:, None]
+    gain_two = mlp_gain.astype(F32)[:, None]
+
+    q_t, k_t, v_t, k_nat, v_nat, w_t = project_qkv(
+        where_one, x, gain_one, first_all, cos_t, sin_t, heads, kv_heads, rows
+    )
+    o_t, logs = attention_forward(inv, q_t, k_nat, v_t, span)
+    out, dmid, do_t, rest_grads, gain_two_terms = mlp_both(
+        where_one, where_two, x, o_t, dy, gain_two, first_all, second_all, ff, rows
+    )
+    hidden_out = exchange(out).transpose(0, 2, 1)
+    rest_sum = lax.psum_scatter(rest_grads, ("dp", "seq"), scatter_dimension=0, tiled=True)[0].astype(F32)
 
     dq_t, dk_t, dv_t = attention_backward(
         inv, q_t, k_t, k_nat, v_nat, o_t, do_t, logs, cos_t, sin_t, span
     )
-    din, w_grad_t, gain_one_grad = project_back(x, dmid, dq_t, dk_t, dv_t, gain_one, w_t)
-    grad_in = to_slots(din, seqs).astype(F32)
-
-    q_part = w_grad_t[:width].reshape(seq, q_cols, dp, rows)
-    k_part = w_grad_t[width : width + kv_cols * seq].reshape(seq, kv_cols, dp, rows)
-    v_part = w_grad_t[width + kv_cols * seq :].reshape(seq, kv_cols, dp, rows)
-    qkv_grads = jnp.concatenate([q_part, k_part, v_part], axis=1).transpose(2, 0, 3, 1)
-    qkv_sum = scatter_halving(pad_lanes(qkv_grads)).astype(F32)
-    gains = sum_doubling(jnp.concatenate([gain_one_grad, gain_two_grad], axis=0))
+    din, qkv_grads, gain_one_terms = project_back(x, dmid, dq_t, dk_t, dv_t, gain_one, w_t, lanes)
+    grad_in = exchange(din).astype(F32).transpose(0, 2, 1)
+    qkv_sum = scatter_halving(qkv_grads, dp, seq).astype(F32)
+    gains = sum_doubling(
+        jnp.stack([jnp.sum(gain_one_terms, axis=1), jnp.sum(gain_two_terms, axis=1)]), dp, seq
+    )
+    o_sum, gate_sum, up_sum, both_sum = [rest_sum[rows * i : rows * (i + 1)] for i in range(4)]
+    spare = gate_weight.shape[1] - lanes
+    down_sum = jnp.concatenate(
+        [
+            rest_sum[4 * rows + padded * t : 4 * rows + padded * t + q_cols]
+            for t in range(ff_rows // lanes)
+        ],
+        axis=1,
+    )
     return (
         hidden_out,
         grad_in,
@@ -1005,17 +1159,16 @@
         qkv_sum[:, :q_cols],
         qkv_sum[:, q_cols : q_cols + kv_cols],
         qkv_sum[:, q_cols + kv_cols : q_cols + 2 * kv_cols],
-        rest_sum[2 * part + down_part :, :o_cols],
+        o_sum[:, :q_cols],
         gains[1],
-        unfold(rest_sum[:part], g_rows, g_cols),
-        unfold(rest_sum[part : 2 * part], g_rows, g_cols),
-        unfold(rest_sum[2 * part : 2 * part + down_part], d_cols, d_rows).T,
+        jnp.concatenate([gate_sum, both_sum[:, :spare]], axis=1),
+        jnp.concatenate([up_sum, both_sum[:, spare:]], axis=1),
+        down_sum.T,
     )
 
 
 def shards(*args):
-    hidden_in = args[0]
-    if hidden_in.shape[0] == lax.axis_size("seq"):
+    if args[0].shape[0] == lax.axis_size("seq"):
         return shards_sequences(*args)
     return shards_general(*args)
 

time: 631 us -> 473 us (0.75); the launches traced: 620 us -> 472 us
  Pallas kernels: 250 us -> 356 us
  local copies, waits for them, and re-layouts: 112 us -> 16.7 us
  blocking collectives: 91.7 us -> 0 us
  waiting for transfers between devices: 94.3 us -> 36.3 us
  other arithmetic: 24.2 us -> 15.5 us
    pallas_call x2 -> x3, Pallas kernels: 74.9 us -> 181 us  [the longest x1 103 us: bring(): pl.pallas_call(functools.partial(bring_kernel, dp=dp, seq=seq), in_specs=...]
    all_to_all x1 -> x0, blocking collectives: 91.7 us -> none  [to_sequences(): moved = lax.all_to_all(block, 'seq', 0, 0, tiled=True)]
    ppermute x15 -> x10, waiting for transfers between devices: 94.2 us -> 36.3 us  [swap(): return lax.ppermute(array, axis, [(i, i ^ bit) for i in range(size)])]
    reshape x15 -> x0, local copies, waits for them, and re-layouts: 40.4 us -> none  [the longest x3 10.6 us: cut(): matrix.reshape(dp, rows // dp, seq, cols // seq).transpose(0, 2, 1, 3)]
    slice x19 -> x7, local copies, waits for them, and re-layouts: 26.1 us -> 3.06 us  [the longest x1 0.77 us: shards_sequences(): gate_weight[:, :lanes]]
    unnamed x64 -> x26, local copies, waits for them, and re-layouts: 26 us -> 9.55 us
    concatenate x3 -> x1, local copies, waits for them, and re-layouts: 8.48 us -> 0.73 us  [shards_sequences(): jnp.concatenate([up_weight[:, :lanes], jnp.concatenate([gate_weight[:, la...]
    all_to_all x2 -> x0, local copies, waits for them, and re-layouts: 6.94 us -> none  [to_sequences(): moved = lax.all_to_all(block, 'seq', 0, 0, tiled=True)]
  transfers between devices with their start and end apart: 20 -> 14, of which waited for: 12 -> 7; matrix products, arithmetic and copies ran while one was open for 14% -> 3% of each run, Pallas kernels for 30% -> 40%
where the time goes in v2:
time: 473 us; the launch traced here: 472 us
  Pallas kernels  356 us (75%)
  waiting for transfers between devices  36.3 us (8%)
  starting transfers between devices  32.8 us (7%)
  local copies, waits for them, and re-layouts  16.7 us (4%)
  other arithmetic  15.5 us (3%)
  between operations  14.3 us (3%)
    pallas_call x1, Pallas kernels, bring(): pl.pallas_call(functools.partial(bring_kernel, dp=dp, seq=seq), in_specs=...  103 us
    pallas_call x1, Pallas kernels, attention_backward(): pl.pallas_call(functools.partial(attend_back_kernel, blocks=tokens // (2...  103 us
    pallas_call x1, Pallas kernels, mlp_both(): pl.pallas_call(functools.partial(mlp_kernel, chunk=chunk, dp=dp, seq=seq)...  64.3 us
    pallas_call x1, Pallas kernels, attention_forward(): pl.pallas_call(functools.partial(attend_kernel, blocks=tokens // (2 * spa...  61.5 us
    ppermute x10, waiting for transfers between devices, swap(): return lax.ppermute(array, axis, [(i, i ^ bit) for i in range(size)])  36.3 us
    ppermute x10, starting transfers between devices, swap(): return lax.ppermute(array, axis, [(i, i ^ bit) for i in range(size)])  17.1 us
    all_to_all x3, starting transfers between devices, exchange(): return lax.all_to_all(blocks, 'seq', 0, 0, tiled=True)  15.7 us
    pallas_call x1, Pallas kernels, project_back(): pl.pallas_call(functools.partial(qkv_back_kernel, dp=dp, seq=seq, kv_widt...  13.5 us
  transfers between devices with their start and end apart: 14, of which 7 were waited for; matrix products, arithmetic and copies ran while one was open for 3% of the time, Pallas kernels for 40%

profile of v2, /device:TPU:0, one launch (start us, length us, event | category | flops | bytes accessed | tf_op | source)
XLA Modules:
  0.0 471.9 jit_solution(17344582518568203776)
XLA Ops:
  16.5 103.0 %bring.1 = (bf16[8,576,256]{2,1,0:T(8,128)(2,1)}, bf16[32,432,128]{2,1,0:T(8,128)(2,1)}, bf16[32,528,128]{2,1,0:T(8,128)(2,1)}) custom-call(bf16[8,576,256]{2,1,0:T(8,128)(2,1)} %bitcast.53, bf16[1,432,128]{2,1,0:T(8,128)(2,1)} %fusion.8.first_ref, bf16[1,528,128]{2,1,0:T(8,128)(2,1)} %bitcast.60), custom_call_target="tpu_custom_call" | custom-call | tf_op jit(solution)/shard_map/bring/pallas_call | solution.py:690
  119.6 3.8 all-to-all-start
  126.5 1.8 multiply_sine_fusion
  128.9 11.3 %project_qkv.1 = (bf16[576,2048]{1,0:T(8,128)(2,1)}, bf16[192,2048]{1,0:T(8,128)(2,1)}, bf16[192,2048]{1,0:T(8,128)(2,1)}, bf16[3,2048,64]{2,1,0:T(8,128)(2,1)},...) custom-call(s32[32]{0:T(128)} %get-tuple-element.121.where_ref.one_ref, ...), custom_call_target="tpu_custom_call" | custom-call | flops 4529848320 | bytes 10240000 | tf_op jit(solution)/shard_map/project_qkv/pallas_call | solution.py:761
  140.2 61.5 %attention_forward.1 = (bf16[576,2048]{1,0:T(8,128)(2,1)}, f32[3,8,2048]{2,1,0:T(8,128)}) custom-call(s32[16]{0:T(128)} %get-tuple-element.38.inv_ref, bf16[576,2048]{1,0:T(8,128)(2,1)} %get-tuple-element.40.q_ref, bf16[3,2048,64]{2,1,0:T(8,128)(2,1)} %get-tuple-element.41.k_ref, bf16[192,2048]{1,0:T(8,128)(2,1)} %get-tuple-element.42.v_ref), custom_call_target="tpu_custom_call" | custom-call | flops 38654705664 | bytes 12288000 | tf_op jit(solution)/shard_map/attention_forward/pallas_call | solution.py:464
  203.1 64.3 %mlp_both.1 = (bf16[8,576,256]{2,1,0:T(8,128)(2,1)}, f32[8,576,256]{2,1,0:T(8,128)}, bf16[576,2048]{1,0:T(8,128)(2,1)}, bf16[32,816,128]{2,1,0:T(8,128)(2,1)}, f32[576,128]{1,0:T(8,128)}) custom-call(s32[32]{0:T(128)} %get-tuple-element.121.where_ref.one_ref, s32[32]{0:T(128)} %get-tuple-element.120.two_ref, bf16[8,576,256]{2,1,0:T(8,128)(2,1)} %get-tuple-element.37.x_ref, ...), custom_call_target="tpu_custom_call" | custom-call | flops 36691771392 | bytes 16515072 | tf_op jit(solution)/shard_map/mlp_both/pallas_call | solution.py:923
  267.5 5.9 %all-to-all-start.1 = ((bf16[8,576,256]{2,1,0:T(8,128)(2,1)}), bf16[8,576,256]{2,1,0:T(8,128)(2,1)S(1)}, u32[]{:S(2)}, u32[]{:S(2)}) async-start(bf16[8,576,256]{2,1,0:T(8,128)(2,1)} %get-tuple-element.46), calls=%async_computation.1 | async-start | bytes 4718592 | tf_op jit(solution)/shard_map/all_to_all | solution.py:1075
  273.4 102.6 %attention_backward.1 = (bf16[576,2048]{1,0:T(8,128)(2,1)}, bf16[192,2048]{1,0:T(8,128)(2,1)}, bf16[192,2048]{1,0:T(8,128)(2,1)}) custom-call(s32[16]{0:T(128)} %get-tuple-element.38.inv_ref, bf16[576,2048]{1,0:T(8,128)(2,1)} %get-tuple-element.40.q_ref, bf16[192,2048]{1,0:T(8,128)(2,1)} %get-tuple-element.48.kt_ref, ...), custom_call_target="tpu_custom_call" | custom-call | flops 77309411328 | bytes 18432000 | tf_op jit(solution)/shard_map/attention_backward/pallas_call | solution.py:569
  376.0 13.5 %project_back.1 = (bf16[8,576,256]{2,1,0:T(8,128)(2,1)}, bf16[32,144,128]{2,1,0:T(8,128)(2,1)}, f32[576,128]{1,0:T(8,128)}) custom-call(bf16[8,576,256]{2,1,0:T(8,128)(2,1)} %get-tuple-element.37.x_ref, f32[8,576,256]{2,1,0:T(8,128)} %get-tuple-element.47.dmid_ref, bf16[576,2048]{1,0:T(8,128)(2,1)} %get-tuple-element.52.dq_ref, ...), custom_call_target="tpu_custom_call" | custom-call | flops 4529848320 | bytes 14155776 | tf_op jit(solution)/shard_map/project_back/pallas_call | solution.py:1024
  390.9 6.0 %all-to-all-start.2 = ((bf16[8,576,256]{2,1,0:T(8,128)(2,1)}), bf16[8,576,256]{2,1,0:T(8,128)(2,1)S(1)}, u32[]{:S(2)}, u32[]{:S(2)}) async-start(bf16[8,576,256]{2,1,0:T(8,128)(2,1)} %get-tuple-element.56), calls=%async_computation.2 | async-start | bytes 4718592 | tf_op jit(solution)/shard_map/all_to_all | solution.py:1075
  397.8 2.2 collective-permute-done.5
  401.2 1.8 collective-permute-start.6
  405.4 4.9 %collective-permute-done.6 = bf16[2,2,2,144,128]{4,3,2,1,0:T(8,128)(2,1)S(1)} collective-permute-done((bf16[2,2,2,144,128]{4,3,2,1,0:T(8,128)(2,1)S(1)}, bf16[2,2,2,144,128]{4,3,2,1,0:T(8,128)(2,1)S(1)}, u32[]{:S(2)}, u32[]{:S(2)}) %collective-permute-start.6) | collective-permute-done | bytes 294944 | tf_op jit(solution)/shard_map/ppermute | solution.py:1050
  410.5 2.1 collective-permute-start.7
  412.6 1.8 collective-permute-start.1
  414.4 5.7 %collective-permute-done.7 = bf16[2,2,144,128]{3,2,1,0:T(8,128)(2,1)S(1)} collective-permute-done((bf16[2,2,144,128]{3,2,1,0:T(8,128)(2,1)S(1)}, bf16[2,2,144,128]{3,2,1,0:T(8,128)(2,1)S(1)}, u32[]{:S(2)}, u32[]{:S(2)}) %collective-permute-start.7) | collective-permute-done | bytes 147488 | tf_op jit(solution)/shard_map/ppermute | solution.py:1050
  420.8 2.5 collective-permute-start.2
  423.3 1.6 collective-permute-done.2
  425.0 1.5 collective-permute-start.3
  426.5 10.8 %collective-permute-done.3 = f32[2,576]{1,0:T(2,128)S(1)} collective-permute-done((f32[2,576]{1,0:T(2,128)S(1)}, f32[2,576]{1,0:T(2,128)S(1)}, u32[]{:S(2)}, u32[]{:S(2)}) %collective-permute-start.3) | collective-permute-done | bytes 4640 | tf_op jit(solution)/shard_map/ppermute | solution.py:1050
  437.3 6.6 %collective-permute-start.4 = (f32[2,576]{1,0:T(2,128)S(1)}, f32[2,576]{1,0:T(2,128)S(1)}, u32[]{:S(2)}, u32[]{:S(2)}) collective-permute-start(f32[2,576]{1,0:T(2,128)S(1)} %add.205), channel_id=1, source_target_pairs={{0,4},{1,5},{2,6},{3,7},{4,0},{5,1},{6,2},{7,3},{8,12},{9,13},{10,... | collective-permute-start | bytes 13832 | tf_op jit(solution)/shard_map/ppermute | solution.py:1050
  444.0 6.7 %collective-permute-done.4 = f32[2,576]{1,0:T(2,128)S(1)} collective-permute-done((f32[2,576]{1,0:T(2,128)S(1)}, f32[2,576]{1,0:T(2,128)S(1)}, u32[]{:S(2)}, u32[]{:S(2)}) %collective-permute-start.4) | collective-permute-done | bytes 4640 | tf_op jit(solution)/shard_map/ppermute | solution.py:1050
  451.4 4.2 collective-permute-done.9
  457.2 2.6 convert_bitcast_fusion
  (85 shorter events, 28.7 us)
Async XLA Ops:
  12.6 4.0 copy-start.5
  119.5 3.9 copy-start.8
  119.5 4.0 copy-start.6
  119.6 6.1 %copy-start.7 = (bf16[576]{0:T(1024)(128)(2,1)S(1)}, bf16[576]{0:T(1024)(128)(2,1)}, u32[]{:S(2)}) copy-start(bf16[576]{0:T(1024)(128)(2,1)} %param.19) | copy-start | bytes 3460
  119.6 82.1 %all-to-all-start = ((bf16[8,576,256]{2,1,0:T(8,128)(2,1)}), bf16[8,576,256]{2,1,0:T(8,128)(2,1)S(1)}, u32[]{:S(2)}, u32[]{:S(2)}) async-start(bf16[8,576,256]{2,1,0:T(8,128)(2,1)} %bitcast.4), calls=%async_computation | async-start | bytes 4718592 | tf_op jit(solution)/shard_map/all_to_all | solution.py:1075
  123.3 336.4 %reduce-scatter.2.cloned.1.call-start = ((), (), s32[]{:S(2)}) async-start(), calls=%async_computation.4 | async-start | bytes 6893568 | tf_op jit(solution)/shard_map/reduce_scatter | solution.py:1135
  201.6 1.5 copy-start.2
  267.5 122.0 %all-to-all-start.1 = ((bf16[8,576,256]{2,1,0:T(8,128)(2,1)}), bf16[8,576,256]{2,1,0:T(8,128)(2,1)S(1)}, u32[]{:S(2)}, u32[]{:S(2)}) async-start(bf16[8,576,256]{2,1,0:T(8,128)(2,1)} %get-tuple-element.46), calls=%async_computation.1 | async-start | bytes 4718592 | tf_op jit(solution)/shard_map/all_to_all | solution.py:1075
  389.5 1.4 copy-start
  389.5 7.4 %copy-start.3 = (bf16[32,144,128]{2,1,0:T(8,128)(2,1)S(1)}, bf16[32,144,128]{2,1,0:T(8,128)(2,1)}, u32[]{:S(2)}) copy-start(bf16[32,144,128]{2,1,0:T(8,128)(2,1)} %get-tuple-element.59) | copy-start | bytes 3538948
  390.9 66.3 %all-to-all-start.2 = ((bf16[8,576,256]{2,1,0:T(8,128)(2,1)}), bf16[8,576,256]{2,1,0:T(8,128)(2,1)S(1)}, u32[]{:S(2)}, u32[]{:S(2)}) async-start(bf16[8,576,256]{2,1,0:T(8,128)(2,1)} %get-tuple-element.56), calls=%async_computation.2 | async-start | bytes 4718592 | tf_op jit(solution)/shard_map/all_to_all | solution.py:1075
  397.7 2.2 collective-permute-start.5
  401.2 9.1 %collective-permute-start.6 = (bf16[2,2,2,144,128]{4,3,2,1,0:T(8,128)(2,1)S(1)}, bf16[2,2,2,144,128]{4,3,2,1,0:T(8,128)(2,1)S(1)}, u32[]{:S(2)}, u32[]{:S(2)}) collective-permute-start(bf16[2,2,2,144,128]{4,3,2,1,0:T(8,128)(2,1)S(1)} %dynamic-slice_bitcast_fusion.1), channel_id=1, source_target_pairs={{0,16},{8,24},{16,0},{24,8},{1,17},{9,25},{17,1},{25,9},{2,18},{10... | collective-permute-start | bytes 884744 | tf_op jit(solution)/shard_map/ppermute | solution.py:1050
  405.3 7.2 %collective-permute-start = (f32[2,576]{1,0:T(2,128)S(1)}, f32[2,576]{1,0:T(2,128)S(1)}, u32[]{:S(2)}, u32[]{:S(2)}) collective-permute-start(f32[2,576]{1,0:T(2,128)S(1)} %pad_maximum_fusion.2), channel_id=1, source_target_pairs={{0,8},{8,0},{16,24},{24,16},{1,9},{9,1},{17,25},{25,17},{2,10},{10... | collective-permute-start | bytes 13832 | tf_op jit(solution)/shard_map/ppermute | solution.py:1050
  410.5 9.6 %collective-permute-start.7 = (bf16[2,2,144,128]{3,2,1,0:T(8,128)(2,1)S(1)}, bf16[2,2,144,128]{3,2,1,0:T(8,128)(2,1)S(1)}, u32[]{:S(2)}, u32[]{:S(2)}) collective-permute-start(bf16[2,2,144,128]{3,2,1,0:T(8,128)(2,1)S(1)} %dynamic-slice_bitcast_fusion.2), channel_id=1, source_target_pairs={{0,1},{1,0},{2,3},{3,2},{4,5},{5,4},{6,7},{7,6},{8,9},{9,8},{10,11... | collective-permute-start | bytes 442376 | tf_op jit(solution)/shard_map/ppermute | solution.py:1050
  412.6 8.2 %collective-permute-start.1 = (f32[2,576]{1,0:T(2,128)S(1)}, f32[2,576]{1,0:T(2,128)S(1)}, u32[]{:S(2)}, u32[]{:S(2)}) collective-permute-start(f32[2,576]{1,0:T(2,128)S(1)} %fusion.36), channel_id=1, source_target_pairs={{0,16},{8,24},{16,0},{24,8},{1,17},{9,25},{17,1},{25,9},{2,18},{10... | collective-permute-start | bytes 13832 | tf_op jit(solution)/shard_map/ppermute | solution.py:1050
  420.2 30.5 %collective-permute-start.8 = (bf16[2,144,128]{2,1,0:T(8,128)(2,1)S(1)}, bf16[2,144,128]{2,1,0:T(8,128)(2,1)S(1)}, u32[]{:S(2)}, u32[]{:S(2)}) collective-permute-start(bf16[2,144,128]{2,1,0:T(8,128)(2,1)S(1)} %dynamic-slice_bitcast_fusion.3), channel_id=1, source_target_pairs={{0,2},{1,3},{2,0},{3,1},{4,6},{5,7},{6,4},{7,5},{8,10},{9,11},{10,... | collective-permute-start | bytes 221192 | tf_op jit(solution)/shard_map/ppermute | solution.py:1050
  420.8 4.2 collective-permute-start.2
  425.0 12.3 %collective-permute-start.3 = (f32[2,576]{1,0:T(2,128)S(1)}, f32[2,576]{1,0:T(2,128)S(1)}, u32[]{:S(2)}, u32[]{:S(2)}) collective-permute-start(f32[2,576]{1,0:T(2,128)S(1)} %add.204), channel_id=1, source_target_pairs={{0,2},{1,3},{2,0},{3,1},{4,6},{5,7},{6,4},{7,5},{8,10},{9,11},{10,... | collective-permute-start | bytes 13832 | tf_op jit(solution)/shard_map/ppermute | solution.py:1050
  437.3 13.4 %collective-permute-start.4 = (f32[2,576]{1,0:T(2,128)S(1)}, f32[2,576]{1,0:T(2,128)S(1)}, u32[]{:S(2)}, u32[]{:S(2)}) collective-permute-start(f32[2,576]{1,0:T(2,128)S(1)} %add.205), channel_id=1, source_target_pairs={{0,4},{1,5},{2,6},{3,7},{4,0},{5,1},{6,2},{7,3},{8,12},{9,13},{10,... | collective-permute-start | bytes 13832 | tf_op jit(solution)/shard_map/ppermute | solution.py:1050
  450.7 4.9 %collective-permute-start.9 = (bf16[144,128]{1,0:T(8,128)(2,1)S(1)}, bf16[144,128]{1,0:T(8,128)(2,1)S(1)}, u32[]{:S(2)}, u32[]{:S(2)}) collective-permute-start(bf16[144,128]{1,0:T(8,128)(2,1)S(1)} %dynamic-slice_bitcast_fusion.4), channel_id=1, source_target_pairs={{0,4},{1,5},{2,6},{3,7},{4,0},{5,1},{6,2},{7,3},{8,12},{9,13},{10,... | collective-permute-start | bytes 110600 | tf_op jit(solution)/shard_map/ppermute | solution.py:1050
  455.7 4.1 copy-start.4
  459.8 3.9 copy-start.1
Sparse Core Ops, SparseCore 0:
  267.6 119.7 reduce-scatter.1

commit v3 on v2

--- a/solution.py
+++ b/solution.py
@@ -601,10 +601,12 @@
     return [1 << i for i in range(size.bit_length() - 1)]
 
 
-def chains(dp, seq):
-    far, near = [("seq", b) for b in reversed(bits_of(seq)[1:])], [("seq", b) for b in bits_of(seq)[:1]]
-    chip, core = [("dp", b) for b in reversed(bits_of(dp)[1:])], [("dp", b) for b in bits_of(dp)[:1]]
-    return far + near + chip + core, far + chip + near + core
+def seq_stages(seq):
+    return [("seq", b) for b in reversed(bits_of(seq)[1:])] + [("seq", b) for b in bits_of(seq)[:1]]
+
+
+def all_stages(dp, seq):
+    return seq_stages(seq) + [("dp", b) for b in reversed(bits_of(dp))]
 
 
 def arrival_order(stages, dp, seq, my_dp, my_seq):
@@ -616,64 +618,79 @@
     return place
 
 
+def greet(peers):
+    barrier = pltpu.get_barrier_semaphore()
+    for peer in peers:
+        pl.semaphore_signal(barrier, inc=1, device_id=peer, device_id_type=pl.DeviceIdType.MESH)
+    pl.semaphore_wait(barrier, len(peers))
+
+
+def seq_peer(my_dp, my_seq, away, seq):
+    return my_dp, flip(my_seq, [b for b in bits_of(seq) if away & b])
+
+
+def stage_peer(my_dp, my_seq, stage):
+    axis, bit = stage
+    return (flip(my_dp, [bit]), my_seq) if axis == "dp" else (my_dp, flip(my_seq, [bit]))
+
+
+def all_peers(my_dp, my_seq, dp, seq):
+    peers = [seq_peer(my_dp, my_seq, away, seq) for away in range(1, seq)]
+    return peers + [(flip(my_dp, [b]), my_seq) for b in bits_of(dp)]
+
+
 def bring_kernel(x_ref, first_ref, second_ref, out_ref, all_one_ref, all_two_ref,
                  local_sem, x_send, x_recv, w_send, w_recv, *, dp, seq):
     my_dp, my_seq = lax.axis_index("dp"), lax.axis_index("seq")
-    orders = chains(dp, seq)
-    barrier = pltpu.get_barrier_semaphore()
-    peers = [(my_dp, flip(my_seq, [b for b in bits_of(seq) if away & b])) for away in range(1, seq)]
-    peers += [(flip(my_dp, [b]), my_seq) for b in bits_of(dp)]
-    for peer in peers:
-        pl.semaphore_signal(barrier, inc=1, device_id=peer, device_id_type=pl.DeviceIdType.MESH)
-    pl.semaphore_wait(barrier, len(peers))
-
+    orders = all_stages(dp, seq), seq_stages(seq)
+    greet(all_peers(my_dp, my_seq, dp, seq))
     shards_in = (first_ref, second_ref)
     gathered = (all_one_ref, all_two_ref)
 
     def weight_copy(chain, stage):
-        axis, bit = orders[chain][stage]
         held = 1 << stage
-        peer = (flip(my_dp, [bit]), my_seq) if axis == "dp" else (my_dp, flip(my_seq, [bit]))
         source = shards_in[chain] if stage == 0 else gathered[chain].at[pl.ds(0, held)]
         return pltpu.make_async_remote_copy(
             src_ref=source,
             dst_ref=gathered[chain].at[pl.ds(held, held)],
             send_sem=w_send.at[chain, stage],
             recv_sem=w_recv.at[chain, stage],
-            device_id=peer,
+            device_id=stage_peer(my_dp, my_seq, orders[chain][stage]),
             device_id_type=pl.DeviceIdType.MESH,
         )
 
+    copies = [[weight_copy(c, s) for s in range(len(orders[c]))] for c in range(2)]
+    for c in range(2):
+        copies[c][0].start()
     own = [
         pltpu.make_async_copy(shards_in[c], gathered[c].at[pl.ds(0, 1)], local_sem.at[c]) for c in range(2)
     ]
     own.append(pltpu.make_async_copy(x_ref.at[my_seq], out_ref.at[my_seq], local_sem.at[2]))
     for copy in own:
         copy.start()
-    copies = [[weight_copy(c, s) for s in range(len(orders[c]))] for c in range(2)]
-    for c in range(2):
-        copies[c][0].start()
     moves = []
     for away in range(1, seq):
-        peer = flip(my_seq, [b for b in bits_of(seq) if away & b])
+        peer = seq_peer(my_dp, my_seq, away, seq)
         moves.append(
             pltpu.make_async_remote_copy(
-                src_ref=x_ref.at[peer],
+                src_ref=x_ref.at[peer[1]],
                 dst_ref=out_ref.at[my_seq],
                 send_sem=x_send.at[away - 1],
                 recv_sem=x_recv.at[away - 1],
-                device_id=(my_dp, peer),
+                device_id=peer,
                 device_id_type=pl.DeviceIdType.MESH,
             )
         )
-    for move in moves:
-        move.start()
     for c in range(2):
         own[c].wait()
     for stage in range(1, len(orders[0])):
         for c in range(2):
-            copies[c][stage - 1].wait_recv()
-            copies[c][stage].start()
+            if stage < len(orders[c]):
+                copies[c][stage - 1].wait_recv()
+                copies[c][stage].start()
+        if stage == 1:
+            for move in moves:
+                move.start()
     for c in range(2):
         copies[c][-1].wait_recv()
         for copy in copies[c]:
@@ -685,7 +702,7 @@
 
 def bring(x, first, second):
     dp, seq = lax.axis_size("dp"), lax.axis_size("seq")
-    stages = len(chains(dp, seq)[0])
+    stages = len(all_stages(dp, seq))
     hbm = pl.BlockSpec(memory_space=pl.ANY)
     return pl.pallas_call(
         functools.partial(bring_kernel, dp=dp, seq=seq),
@@ -694,7 +711,7 @@
         out_shape=[
             jax.ShapeDtypeStruct(x.shape, x.dtype),
             jax.ShapeDtypeStruct((dp * seq, *first.shape[1:]), first.dtype),
-            jax.ShapeDtypeStruct((dp * seq, *second.shape[1:]), second.dtype),
+            jax.ShapeDtypeStruct((seq, *second.shape[1:]), second.dtype),
         ],
         scratch_shapes=[
             pltpu.SemaphoreType.DMA((3,)),
@@ -797,14 +814,15 @@
 
 
 def mlp_kernel(
-    one_ref, two_ref, x_ref, mixed_ref, dy_ref, gain_ref, o_pack, gate_pack, rest_pack,
-    out_ref, dmid_ref, dmixed_ref, grads_ref, gain_grad_ref,
-    o_w, o_t, gate_w, gate_t, up_w, up_t, down_w, down_t, o_sum, gate_sum, up_sum, down_sum, gain_sum,
-    *, chunk, dp, seq,
+    where_ref, x_ref, mixed_ref, dy_ref, gain_ref, *more, chunk, dp, seq,
 ):
+    packs = more[:dp]
+    out_ref, dmid_ref, dmixed_ref, grads_ref, gain_grad_ref = more[dp : dp + 5]
+    (o_w, o_t, gate_w, gate_t, up_w, up_t, down_w, down_t, o_sum, gate_sum, up_sum, down_sum, gain_sum,
+     pack, pack_sem) = more[dp + 5 :]
     step, steps = pl.program_id(0), pl.num_programs(0)
     width, ff = gate_w.shape
-    lanes = o_pack.shape[2]
+    lanes = pack.shape[3]
     rows = width // dp
     o_cols, ff_cols, ff_rows = width // seq, ff // seq, ff // dp
     spare = ff_cols - lanes
@@ -814,22 +832,31 @@
     def _():
         for total in (o_sum, gate_sum, up_sum, down_sum, gain_sum):
             total[...] = jnp.zeros_like(total)
+        fetches = [
+            pltpu.make_async_copy(
+                packs[i], pack.at[flip(lax.axis_index("dp"), row_bits(i, dp))], pack_sem.at[i]
+            )
+            for i in range(dp)
+        ]
+        for fetch in fetches:
+            fetch.start()
+        for fetch in fetches:
+            fetch.wait()
         for s in range(seq):
-            ones = [one_ref[d * seq + s] for d in range(dp)]
-            twos = [two_ref[d * seq + s] for d in range(dp)]
-            stack = lambda ref, where, first: jnp.concatenate(
-                [ref[w, first : first + rows, :] for w in where], axis=0
+            at = where_ref[s]
+            stack = lambda first: jnp.concatenate(
+                [pack[d, at, first : first + rows, :] for d in range(dp)], axis=0
             ).astype(F32).T
-            o_sum[o_cols * s : o_cols * s + o_cols, :] = stack(o_pack, ones, 0)[:o_cols]
-            gate_t[ff_cols * s : ff_cols * s + lanes, :] = stack(gate_pack, ones, 0).astype(BF16)
-            up_t[ff_cols * s : ff_cols * s + lanes, :] = stack(rest_pack, twos, 0).astype(BF16)
-            both = stack(rest_pack, twos, rows).astype(BF16)
+            o_sum[o_cols * s : o_cols * s + o_cols, :] = stack(0)[:o_cols]
+            gate_t[ff_cols * s : ff_cols * s + lanes, :] = stack(rows).astype(BF16)
+            up_t[ff_cols * s : ff_cols * s + lanes, :] = stack(2 * rows).astype(BF16)
+            both = stack(3 * rows).astype(BF16)
             gate_t[ff_cols * s + lanes : ff_cols * (s + 1), :] = both[:spare]
             up_t[ff_cols * s + lanes : ff_cols * (s + 1), :] = both[spare : 2 * spare]
             for d in range(dp):
                 for t in range(ff_rows // lanes):
-                    first = 2 * rows + padded * t
-                    piece = rest_pack[twos[d], first : first + padded, :].astype(F32)[:o_cols]
+                    first = 4 * rows + padded * t
+                    piece = pack[d, at, first : first + padded, :].astype(F32)[:o_cols]
                     cols = slice(ff_rows * d + lanes * t, ff_rows * d + lanes * (t + 1))
                     down_sum[o_cols * s : o_cols * s + o_cols, cols] = piece
         o_t[...] = o_sum[...].astype(BF16)
@@ -884,7 +911,7 @@
 
     @pl.when(step == steps - 1)
     def _():
-        gain_grad_ref[...] = gain_sum[...]
+        gain_grad_ref[...] = jnp.sum(gain_sum[...].T, axis=0, keepdims=True)
         for s in range(seq):
             tall = lambda total, first, count: total[first : first + count, :]
             blank = jnp.zeros((lanes - o_cols, width), F32)
@@ -907,26 +934,36 @@
                     grads_ref[at, first : first + padded, :] = piece.astype(BF16)
 
 
-def mlp_both(one, two, x, mixed, dy, gain, first_pack, second_pack, ff, rows, batch=2, chunk=512):
+def row_bits(at, dp):
+    return [b for i, b in enumerate(reversed(bits_of(dp))) if (at >> i) & 1]
+
+
+def gather_rows(array, dp):
+    held = [array]
+    for at in range(1, dp):
+        mask = sum(row_bits(at, dp))
+        held.append(lax.ppermute(array, "dp", [(i, i ^ mask) for i in range(dp)]))
+    return held
+
+
+def mlp_both(where, x, mixed, dy, gain, packs, ff, batch=2, chunk=512):
     blocks, width, block = x.shape
     tokens = blocks * block
     dp, seq = lax.axis_size("dp"), lax.axis_size("seq")
-    lanes = first_pack.shape[2]
-    tok = pl.BlockSpec((batch, width, block), lambda i, a, b: (i, 0, 0))
-    col = pl.BlockSpec((width, batch * block), lambda i, a, b: (0, i))
-    single = pl.Buffered(1)
-    once = lambda shape: pl.BlockSpec(shape, lambda i, a, b: (0,) * len(shape), pipeline_mode=single)
-    pick = lambda which: pl.BlockSpec(
-        (dp * seq, rows, lanes), lambda i, a, b: (0, which, 0), pipeline_mode=single
+    grad_rows, lanes = packs[0].shape[1:]
+    tok = pl.BlockSpec((batch, width, block), lambda i, w: (i, 0, 0))
+    col = pl.BlockSpec((width, batch * block), lambda i, w: (0, i))
+    once = lambda shape: pl.BlockSpec(
+        shape, lambda i, w: (0,) * len(shape), pipeline_mode=pl.Buffered(1)
     )
-    grad_rows = first_pack.shape[1] - rows + second_pack.shape[1]
+    hbm = pl.BlockSpec(memory_space=pl.ANY)
     return pl.pallas_call(
         functools.partial(mlp_kernel, chunk=chunk, dp=dp, seq=seq),
         grid_spec=pltpu.PrefetchScalarGridSpec(
-            num_scalar_prefetch=2,
+            num_scalar_prefetch=1,
             grid=(blocks // batch,),
-            in_specs=[tok, col, tok, once((width, 1)), pick(1), pick(2), once(second_pack.shape)],
-            out_specs=[tok, tok, col, once((dp * seq, grad_rows, lanes)), once((width, lanes))],
+            in_specs=[tok, col, tok, once((width, 1))] + [hbm] * dp,
+            out_specs=[tok, tok, col, once((dp * seq, grad_rows, lanes)), once((1, width))],
             scratch_shapes=[
                 pltpu.VMEM((width, width), BF16),
                 pltpu.VMEM((width, width), BF16),
@@ -941,6 +978,8 @@
                 pltpu.VMEM((ff, width), F32),
                 pltpu.VMEM((width, ff), F32),
                 pltpu.VMEM((width, lanes), F32),
+                pltpu.VMEM((dp, *packs[0].shape), BF16),
+                pltpu.SemaphoreType.DMA((dp,)),
             ],
         ),
         out_shape=[
@@ -948,7 +987,7 @@
             jax.ShapeDtypeStruct(x.shape, F32),
             jax.ShapeDtypeStruct((width, tokens), BF16),
             jax.ShapeDtypeStruct((dp * seq, grad_rows, lanes), BF16),
-            jax.ShapeDtypeStruct((width, lanes), F32),
+            jax.ShapeDtypeStruct((1, width), F32),
         ],
         compiler_params=pltpu.CompilerParams(vmem_limit_bytes=60 * 2**20),
         cost_estimate=pl.CostEstimate(
@@ -957,21 +996,32 @@
             transcendentals=tokens * ff,
         ),
         name="mlp_both",
-    )(one, two, x, mixed, dy, gain, first_pack, first_pack, second_pack)
-
-
-def qkv_back_kernel(
-    x_ref, dmid_ref, dq_ref, dk_ref, dv_ref, gain_ref, w_t_ref,
-    din_ref, grads_ref, gain_grad_ref, w_nat, w_sum, gain_sum, *, dp, seq, kv_width,
+    )(where, x, mixed, dy, gain, *packs)
+
+
+def across(index, other, size):
+    for bit in bits_of(size):
+        index = index + bit * ((other // bit) % 2) * (1 - 2 * ((index // bit) % 2))
+    return index
+
+
+def finish_kernel(
+    x_ref, dmid_ref, dq_ref, dk_ref, dv_ref, gain_ref, w_t_ref, other_gain_ref,
+    out_ref, grads_ref, gains_ref,
+    w_nat, w_sum, gain_sum, din, packed, landed, gain_held, gain_landed,
+    own_sem, d_send, d_recv, r_send, r_recv, g_send, g_recv, *, dp, seq, kv_width,
 ):
-    step, steps = pl.program_id(0), pl.num_programs(0)
+    step, steps = pl.program_id(0), seq // 2
+    my_dp, my_seq = lax.axis_index("dp"), lax.axis_index("seq")
     width = w_nat.shape[0]
-    lanes = grads_ref.shape[2]
+    lanes = grads_ref.shape[1]
     rows = width // dp
     q_cols, kv_cols = width // seq, kv_width // seq
+    stages = all_stages(dp, seq)
 
     @pl.when(step == 0)
     def _():
+        greet(all_peers(my_dp, my_seq, dp, seq))
         w_sum[...] = jnp.zeros_like(w_sum)
         gain_sum[...] = jnp.zeros_like(gain_sum)
         w_nat[...] = w_t_ref[...].T
@@ -988,14 +1038,35 @@
     gain_sum[...] += sum(product[:, c : c + lanes] for c in range(0, product.shape[1], lanes))
     scaled = dnormed * gain
     pull = jnp.mean(scaled * x, axis=0, keepdims=True)
-    din = side_by_side(dmid_ref) + rstd * scaled - scaled_x * (rstd * rstd * pull)
-    block = din_ref.shape[2]
-    for i in range(din_ref.shape[0]):
-        din_ref[i] = din[:, block * i : block * (i + 1)].astype(BF16)
+    total = side_by_side(dmid_ref) + rstd * scaled - scaled_x * (rstd * rstd * pull)
+    pair = across(my_seq // 2, steps - 1 - step, seq // 2)
+    block = din.shape[2]
+    for i in range(2):
+        din[2 * pair + i] = total[:, block * i : block * (i + 1)].astype(BF16)
+
+    def move(away):
+        peer = seq_peer(my_dp, my_seq, away, seq)
+        return pltpu.make_async_remote_copy(
+            src_ref=din.at[peer[1]],
+            dst_ref=out_ref.at[my_seq],
+            send_sem=d_send.at[away - 1],
+            recv_sem=d_recv.at[away - 1],
+            device_id=peer,
+            device_id_type=pl.DeviceIdType.MESH,
+        )
+
+    for back in range(1, steps):
+
+        @pl.when(step == steps - 1 - back)
+        def _():
+            move(2 * back).start()
+            move(2 * back + 1).start()
 
     @pl.when(step == steps - 1)
     def _():
-        gain_grad_ref[...] = gain_sum[...]
+        move(1).start()
+        own = pltpu.make_async_copy(din.at[my_seq], out_ref.at[my_seq], own_sem)
+        own.start()
         blank = jnp.zeros((lanes - q_cols - 2 * kv_cols, width), F32)
         for s in range(seq):
             first = width + kv_cols * s
@@ -1009,66 +1080,107 @@
                 axis=0,
             ).T.astype(BF16)
             for d in range(dp):
-                grads_ref[d * seq + s] = piece[rows * d : rows * (d + 1)]
-
-
-def project_back(x, dmid, dq_t, dk_t, dv_t, gain, w_t, lanes, batch=2):
+                place = 0
+                for at, (axis, bit) in enumerate(stages):
+                    mine = ((my_dp if axis == "dp" else my_seq) // bit) % 2
+                    theirs = ((d if axis == "dp" else s) // bit) % 2
+                    place = place + (1 << at) * (1 - mine if theirs else mine)
+                packed[place] = piece[rows * d : rows * (d + 1)]
+        gain_row = jnp.sum(gain_sum[...].T, axis=0, keepdims=True)
+        gain_held[0] = jnp.concatenate(
+            [gain_row, other_gain_ref[...], jnp.zeros((6, width), F32)], axis=0
+        )
+        sent = []
+        for turn, at in enumerate(reversed(range(len(stages)))):
+            half = 1 << at
+            peer = stage_peer(my_dp, my_seq, stages[at])
+            send = pltpu.make_async_remote_copy(
+                src_ref=packed.at[pl.ds(half, half)],
+                dst_ref=landed.at[pl.ds(half, half)],
+                send_sem=r_send.at[at],
+                recv_sem=r_recv.at[at],
+                device_id=peer,
+                device_id_type=pl.DeviceIdType.MESH,
+            )
+            gain_copy = pltpu.make_async_remote_copy(
+                src_ref=gain_held.at[turn],
+                dst_ref=gain_landed.at[turn],
+                send_sem=g_send.at[turn],
+                recv_sem=g_recv.at[turn],
+                device_id=peer,
+                device_id_type=pl.DeviceIdType.MESH,
+            )
+            send.start()
+            gain_copy.start()
+            sent += [send, gain_copy]
+            gain_copy.wait_recv()
+            gain_held[turn + 1] = gain_held[turn] + gain_landed[turn]
+            send.wait_recv()
+            both = packed[0:half].astype(F32) + landed[half : 2 * half].astype(F32)
+            if at == 0:
+                grads_ref[...] = both[0]
+            else:
+                packed[0:half] = both.astype(BF16)
+        gains_ref[...] = gain_held[len(stages)]
+        for copy in sent:
+            copy.wait_send()
+        for away in range(1, seq):
+            move(away).wait()
+        own.wait()
+
+
+def finish(x, dmid, dq_t, dk_t, dv_t, gain, w_t, other_gain, lanes):
     blocks, width, block = x.shape
     tokens = blocks * block
     feats = w_t.shape[0]
     dp, seq = lax.axis_size("dp"), lax.axis_size("seq")
-    tok = pl.BlockSpec((batch, width, block), lambda i: (i, 0, 0))
-    col = lambda rows: pl.BlockSpec((rows, batch * block), lambda i: (0, i))
+    rows = width // dp
+    stages = len(all_stages(dp, seq))
+
+    def pair(i):
+        return across(lax.axis_index("seq") // 2, seq // 2 - 1 - i, seq // 2)
+
+    tok = pl.BlockSpec((2, width, block), lambda i: (pair(i), 0, 0))
+    col = lambda rows: pl.BlockSpec((rows, 2 * block), lambda i: (0, pair(i)))
     once = lambda shape: pl.BlockSpec(shape, lambda i: (0,) * len(shape), pipeline_mode=pl.Buffered(1))
-    packed = (dp * seq, width // dp, lanes)
     return pl.pallas_call(
-        functools.partial(qkv_back_kernel, dp=dp, seq=seq, kv_width=dk_t.shape[0]),
-        grid=(blocks // batch,),
+        functools.partial(finish_kernel, dp=dp, seq=seq, kv_width=dk_t.shape[0]),
+        grid=(blocks // 2,),
         in_specs=[
             tok, tok, col(dq_t.shape[0]), col(dk_t.shape[0]), col(dv_t.shape[0]),
-            once((width, 1)), once((feats, width)),
+            once((width, 1)), once((feats, width)), once((1, width)),
         ],
-        out_specs=[tok, once(packed), once((width, lanes))],
+        out_specs=[pl.BlockSpec(memory_space=pl.ANY), once((rows, lanes)), once((8, width))],
         out_shape=[
             jax.ShapeDtypeStruct(x.shape, BF16),
-            jax.ShapeDtypeStruct(packed, BF16),
-            jax.ShapeDtypeStruct((width, lanes), F32),
+            jax.ShapeDtypeStruct((rows, lanes), F32),
+            jax.ShapeDtypeStruct((8, width), F32),
         ],
         scratch_shapes=[
-            pltpu.VMEM((width, feats), BF16), pltpu.VMEM((feats, width), F32), pltpu.VMEM((width, lanes), F32),
+            pltpu.VMEM((width, feats), BF16),
+            pltpu.VMEM((feats, width), F32),
+            pltpu.VMEM((width, lanes), F32),
+            pltpu.VMEM(x.shape, BF16),
+            pltpu.VMEM((dp * seq, rows, lanes), BF16),
+            pltpu.VMEM((dp * seq, rows, lanes), BF16),
+            pltpu.VMEM((stages + 1, 8, width), F32),
+            pltpu.VMEM((stages, 8, width), F32),
+            pltpu.SemaphoreType.DMA,
+            pltpu.SemaphoreType.DMA((seq - 1,)),
+            pltpu.SemaphoreType.DMA((seq - 1,)),
+            pltpu.SemaphoreType.DMA((stages,)),
+            pltpu.SemaphoreType.DMA((stages,)),
+            pltpu.SemaphoreType.DMA((stages,)),
+            pltpu.SemaphoreType.DMA((stages,)),
         ],
-        compiler_params=pltpu.CompilerParams(vmem_limit_bytes=VMEM_BYTES),
+        compiler_params=pltpu.CompilerParams(
+            collective_id=2, has_side_effects=True, vmem_limit_bytes=VMEM_BYTES
+        ),
         cost_estimate=pl.CostEstimate(
             flops=4 * tokens * width * feats, bytes_accessed=tokens * width * 12, transcendentals=0
         ),
-        name="project_back",
-    )(x, dmid, dq_t, dk_t, dv_t, gain, w_t)
-
-
-def swap(array, axis, bit):
-    size = lax.axis_size(axis)
-    return lax.ppermute(array, axis, [(i, i ^ bit) for i in range(size)])
-
-
-def scatter_halving(array, dp, seq):
-    rows, lanes = array.shape[1:]
-    names = [("dp", b) for b in reversed(bits_of(dp))] + [("seq", b) for b in reversed(bits_of(seq))]
-    part = array.reshape(*[2] * len(names), rows, lanes)
-    for axis, bit in [("dp", b) for b in bits_of(dp)] + [("seq", b) for b in bits_of(seq)]:
-        place = names.index((axis, bit))
-        names.pop(place)
-        upper = (lax.axis_index(axis) // bit) % 2
-        mine = lax.dynamic_index_in_dim(part, upper, place, keepdims=False)
-        other = lax.dynamic_index_in_dim(part, 1 - upper, place, keepdims=False)
-        part = (mine.astype(F32) + swap(other, axis, bit).astype(F32)).astype(BF16)
-    return part.reshape(rows, lanes)
-
-
-def sum_doubling(array, dp, seq):
-    for axis, size in (("dp", dp), ("seq", seq)):
-        for bit in bits_of(size):
-            array = array + swap(array, axis, bit)
-    return array
+        name="finish",
+    )(x, dmid, dq_t, dk_t, dv_t, gain, w_t, other_gain)
 
 
 def exchange(blocks):
@@ -1096,26 +1208,26 @@
     ff_rows = down_weight.shape[0]
     padded = -(-q_cols // 16) * 16
 
-    first = jnp.concatenate(
+    first = pad_lanes(jnp.concatenate([q_weight, k_weight, v_weight], axis=1), lanes)
+    down_turned = jnp.pad(down_weight.T, ((0, padded - q_cols), (0, 0)))
+    second = jnp.concatenate(
         [
-            pad_lanes(jnp.concatenate([q_weight, k_weight, v_weight], axis=1), lanes),
             pad_lanes(o_weight, lanes),
             gate_weight[:, :lanes],
-        ],
-        axis=0,
-    )
-    down_turned = jnp.pad(down_weight.T, ((0, padded - q_cols), (0, 0)))
-    second = jnp.concatenate(
-        [up_weight[:, :lanes], jnp.concatenate([gate_weight[:, lanes:], up_weight[:, lanes:]], axis=1)]
+            up_weight[:, :lanes],
+            jnp.concatenate([gate_weight[:, lanes:], up_weight[:, lanes:]], axis=1),
+        ]
         + [down_turned[:, c : c + lanes] for c in range(0, ff_rows, lanes)],
         axis=0,
     )
-    x, first_all, second_all = bring(hidden_in.transpose(0, 2, 1), first[None], second[None])
+    x, first_all, second_row = bring(hidden_in.transpose(0, 2, 1), first[None], second[None])
     out_grad, x = lax.optimization_barrier((out_grad, x))
     dy = exchange(out_grad.transpose(0, 2, 1))
+    second_all = gather_rows(second_row, dp)
 
     my_dp, my_seq = lax.axis_index("dp"), lax.axis_index("seq")
-    where_one, where_two = [arrival_order(c, dp, seq, my_dp, my_seq) for c in chains(dp, seq)]
+    where_first = arrival_order(all_stages(dp, seq), dp, seq, my_dp, my_seq)
+    where_second = arrival_order(seq_stages(seq), dp, seq, my_dp, my_seq)[:seq]
     inv = jnp.argsort(span_order).astype(jnp.int32)
     slot_pos = slot_positions(jnp.arange(tokens, dtype=jnp.int32), span_order, span)
     inv_freq = rope_base ** (-(jnp.arange(HD // 2, dtype=F32) * 2.0) / HD)
@@ -1125,11 +1237,11 @@
     gain_two = mlp_gain.astype(F32)[:, None]
 
     q_t, k_t, v_t, k_nat, v_nat, w_t = project_qkv(
-        where_one, x, gain_one, first_all, cos_t, sin_t, heads, kv_heads, rows
+        where_first, x, gain_one, first_all, cos_t, sin_t, heads, kv_heads, rows
     )
     o_t, logs = attention_forward(inv, q_t, k_nat, v_t, span)
-    out, dmid, do_t, rest_grads, gain_two_terms = mlp_both(
-        where_one, where_two, x, o_t, dy, gain_two, first_all, second_all, ff, rows
+    out, dmid, do_t, rest_grads, gain_two_term = mlp_both(
+        where_second, x, o_t, dy, gain_two, second_all, ff
     )
     hidden_out = exchange(out).transpose(0, 2, 1)
     rest_sum = lax.psum_scatter(rest_grads, ("dp", "seq"), scatter_dimension=0, tiled=True)[0].astype(F32)
@@ -1137,12 +1249,8 @@
     dq_t, dk_t, dv_t = attention_backward(
         inv, q_t, k_t, k_nat, v_nat, o_t, do_t, logs, cos_t, sin_t, span
     )
-    din, qkv_grads, gain_one_terms = project_back(x, dmid, dq_t, dk_t, dv_t, gain_one, w_t, lanes)
-    grad_in = exchange(din).astype(F32).transpose(0, 2, 1)
-    qkv_sum = scatter_halving(qkv_grads, dp, seq).astype(F32)
-    gains = sum_doubling(
-        jnp.stack([jnp.sum(gain_one_terms, axis=1), jnp.sum(gain_two_terms, axis=1)]), dp, seq
-    )
+    din, qkv_sum, gains = finish(x, dmid, dq_t, dk_t, dv_t, gain_one, w_t, gain_two_term, lanes)
+    grad_in = din.astype(F32).transpose(0, 2, 1)
     o_sum, gate_sum, up_sum, both_sum = [rest_sum[rows * i : rows * (i + 1)] for i in range(4)]
     spare = gate_weight.shape[1] - lanes
     down_sum = jnp.concatenate(

time: 473 us -> 440 us (0.930)
  waiting for transfers between devices: 36.3 us -> 0.03 us
  Pallas kernels: 356 us -> 381 us
  starting transfers between devices: 32.8 us -> 12.9 us
    pallas_call x1, Pallas kernels: 13.5 us -> 67.1 us  [finish(): pl.pallas_call(functools.partial(finish_kernel, dp=dp, seq=seq, kv_width=...]
    ppermute x10 -> x3, waiting for transfers between devices: 36.3 us -> 0.01 us  [gather_rows(): held.append(lax.ppermute(array, 'dp', [(i, i ^ mask) for i in range(dp)]))]
    pallas_call x1, Pallas kernels: 103 us -> 73.6 us  [bring(): pl.pallas_call(functools.partial(bring_kernel, dp=dp, seq=seq), in_specs=...]
    ppermute x10 -> x3, starting transfers between devices: 17.1 us -> 2.21 us  [gather_rows(): held.append(lax.ppermute(array, 'dp', [(i, i ^ mask) for i in range(dp)]))]
    all_to_all x3 -> x2, starting transfers between devices: 15.7 us -> 10.6 us  [exchange(): return lax.all_to_all(blocks, 'seq', 0, 0, tiled=True)]
    unnamed x26 -> x23, local copies, waits for them, and re-layouts: 9.55 us -> 10.3 us
  transfers between devices with their start and end apart: 14 -> 6, of which waited for: 7 -> 0; matrix products, arithmetic and copies ran while one was open for 3% -> 3% of each run, Pallas kernels for 40% -> 55%
where the time goes in v3:
time: 440 us; the launch traced here: 438 us
  Pallas kernels  381 us (87%)
  local copies, waits for them, and re-layouts  17.5 us (4%)
  between operations  14.2 us (3%)
  starting transfers between devices  12.9 us (3%)
  other arithmetic  12.4 us (3%)
    pallas_call x1, Pallas kernels, attention_backward(): pl.pallas_call(functools.partial(attend_back_kernel, blocks=tokens // (2...  103 us
    pallas_call x1, Pallas kernels, bring(): pl.pallas_call(functools.partial(bring_kernel, dp=dp, seq=seq), in_specs=...  73.6 us
    pallas_call x1, Pallas kernels, finish(): pl.pallas_call(functools.partial(finish_kernel, dp=dp, seq=seq, kv_width=...  67.1 us
    pallas_call x1, Pallas kernels, mlp_both(): pl.pallas_call(functools.partial(mlp_kernel, chunk=chunk, dp=dp, seq=seq)...  64.9 us
    pallas_call x1, Pallas kernels, attention_forward(): pl.pallas_call(functools.partial(attend_kernel, blocks=tokens // (2 * spa...  61.8 us
    pallas_call x1, Pallas kernels, project_qkv(): pl.pallas_call(functools.partial(qkv_kernel, heads=heads, kv_heads=kv_hea...  11.2 us
    all_to_all x2, starting transfers between devices, exchange(): return lax.all_to_all(blocks, 'seq', 0, 0, tiled=True)  10.6 us
    unnamed x23, local copies, waits for them, and re-layouts  10.3 us
  transfers between devices with their start and end apart: 6, of which 0 were waited for; matrix products, arithmetic and copies ran while one was open for 3% of the time, Pallas kernels for 55%

profile of v3, /device:TPU:0, one launch (start us, length us, event | category | flops | bytes accessed | tf_op | source)
XLA Modules:
  0.0 438.3 jit_solution(5609175833193141418)
XLA Ops:
  7.2 0.8 copy.34
  8.0 0.8 copy.35
  10.4 0.8 pad_dynamic-update-slice_fusion
  11.2 0.8 slice_dynamic-update-slice_fusion.1
  15.0 1.5 fusion.5.first_ref
  16.5 73.6 %bring.1 = (bf16[8,576,256]{2,1,0:T(8,128)(2,1)}, bf16[32,144,128]{2,1,0:T(8,128)(2,1)}, bf16[8,816,128]{2,1,0:T(8,128)(2,1)}) custom-call(bf16[8,576,256]{2,1,0:T(8,128)(2,1)} %bitcast.26, bf16[1,144,128]{2,1,0:T(8,128)(2,1)} %fusion.5.first_ref, bf16[1,816,128]{2,1,0:T(8,128)(2,1)} %bitcast.31), custom_call_target="tpu_custom_call" | custom-call | tf_op jit(solution)/shard_map/bring/pallas_call | solution.py:707
  90.7 1.1 collective-permute-start.1
  92.3 4.7 %all-to-all-start = ((bf16[8,576,256]{2,1,0:T(8,128)(2,1)}), bf16[8,576,256]{2,1,0:T(8,128)(2,1)S(1)}, u32[]{:S(2)}, u32[]{:S(2)}) async-start(bf16[8,576,256]{2,1,0:T(8,128)(2,1)} %bitcast.4), calls=%async_computation | async-start | bytes 4718592 | tf_op jit(solution)/shard_map/all_to_all | solution.py:1187
  97.1 1.3 sort.17
  98.5 0.9 reshape.65.gain_ref
  99.9 1.8 multiply_sine_fusion
  101.6 11.2 %project_qkv.1 = (bf16[576,2048]{1,0:T(8,128)(2,1)}, bf16[192,2048]{1,0:T(8,128)(2,1)}, bf16[192,2048]{1,0:T(8,128)(2,1)}, bf16[3,2048,64]{2,1,0:T(8,128)(2,1)},...) custom-call(s32[32]{0:T(128)} %fusion.26.where_ref, bf16[8,576,256]{2,1,0:T(8,128)(2,1)} %get-tuple-element.37.x_ref, ...), custom_call_target="tpu_custom_call" | custom-call | flops 4529848320 | bytes 10240000 | tf_op jit(solution)/shard_map/project_qkv/pallas_call | solution.py:778
  112.9 61.8 %attention_forward.1 = (bf16[576,2048]{1,0:T(8,128)(2,1)}, f32[3,8,2048]{2,1,0:T(8,128)}) custom-call(s32[16]{0:T(128)} %get-tuple-element.38.inv_ref, bf16[576,2048]{1,0:T(8,128)(2,1)} %get-tuple-element.40.q_ref, bf16[3,2048,64]{2,1,0:T(8,128)(2,1)} %get-tuple-element.41.k_ref, bf16[192,2048]{1,0:T(8,128)(2,1)} %get-tuple-element.42.v_ref), custom_call_target="tpu_custom_call" | custom-call | flops 38654705664 | bytes 12288000 | tf_op jit(solution)/shard_map/attention_forward/pallas_call | solution.py:464
  174.7 0.9 reshape.66.gain_ref
  176.1 1.4 copy-done
  177.5 64.9 %mlp_both.1 = (bf16[8,576,256]{2,1,0:T(8,128)(2,1)}, f32[8,576,256]{2,1,0:T(8,128)}, bf16[576,2048]{1,0:T(8,128)(2,1)}, bf16[32,816,128]{2,1,0:T(8,128)(2,1)}, f32[1,576]{1,0:T(1,128)}) custom-call(s32[8]{0:T(128)} %bitcast.32, bf16[8,576,256]{2,1,0:T(8,128)(2,1)} %get-tuple-element.37.x_ref, bf16[576,2048]{1,0:T(8,128)(2,1)} %get-tuple-element.43.mixed_ref.o_ref, ...), custom_call_target="tpu_custom_call" | custom-call | flops 36691771392 | bytes 16515072 | tf_op jit(solution)/shard_map/mlp_both/pallas_call | solution.py:960
  242.5 5.9 %all-to-all-start.1 = ((bf16[8,576,256]{2,1,0:T(8,128)(2,1)}), bf16[8,576,256]{2,1,0:T(8,128)(2,1)S(1)}, u32[]{:S(2)}, u32[]{:S(2)}) async-start(bf16[8,576,256]{2,1,0:T(8,128)(2,1)} %get-tuple-element.46), calls=%async_computation.1 | async-start | bytes 4718592 | tf_op jit(solution)/shard_map/all_to_all | solution.py:1187
  248.4 102.6 %attention_backward.1 = (bf16[576,2048]{1,0:T(8,128)(2,1)}, bf16[192,2048]{1,0:T(8,128)(2,1)}, bf16[192,2048]{1,0:T(8,128)(2,1)}) custom-call(s32[16]{0:T(128)} %get-tuple-element.38.inv_ref, bf16[576,2048]{1,0:T(8,128)(2,1)} %get-tuple-element.40.q_ref, bf16[192,2048]{1,0:T(8,128)(2,1)} %get-tuple-element.48.kt_ref, ...), custom_call_target="tpu_custom_call" | custom-call | flops 77309411328 | bytes 18432000 | tf_op jit(solution)/shard_map/attention_backward/pallas_call | solution.py:569
  351.1 67.1 %finish.1 = (bf16[8,576,256]{2,1,0:T(8,128)(2,1)}, f32[144,128]{1,0:T(8,128)}, f32[8,576]{1,0:T(8,128)}) custom-call(bf16[8,576,256]{2,1,0:T(8,128)(2,1)} %get-tuple-element.37.x_ref, f32[8,576,256]{2,1,0:T(8,128)} %get-tuple-element.47.dmid_ref, bf16[576,2048]{1,0:T(8,128)(2,1)} %get-tuple-element.52.dq_ref, bf16[192,2048]{1,0:T(8,128)(2,1)} %get-tuple-element.53.dk_ref, ...), custom_call_target="tpu_custom_call" | custom-call | flops 4529848320 | bytes 14155776 | tf_op jit(solution)/shard_map/finish/pallas_call | solution.py:1146
  418.2 1.1 fusion.33
  420.6 1.4 slice_reduce_fusion
  422.0 4.3 convert_bitcast_fusion
  426.3 1.0 fusion.32
  429.4 1.4 copy.49
  (44 shorter events, 11.1 us)
Async XLA Ops:
  15.0 1.5 copy-start.2
  90.1 85.9 %collective-permute-start.2 = (bf16[8,816,128]{2,1,0:T(8,128)(2,1)}, bf16[8,816,128]{2,1,0:T(8,128)(2,1)}, u32[]{:S(2)}, u32[]{:S(2)}) collective-permute-start(bf16[8,816,128]{2,1,0:T(8,128)(2,1)} %get-tuple-element.45.more_0_), channel_id=1, source_target_pairs={{0,24},{8,16},{16,8},{24,0},{1,25},{9,17},{17,9},{25,1},{2,26},{10... | collective-permute-start | bytes 5013512 | tf_op jit(solution)/shard_map/ppermute | solution.py:945
  90.7 85.4 %collective-permute-start.1 = (bf16[8,816,128]{2,1,0:T(8,128)(2,1)}, bf16[8,816,128]{2,1,0:T(8,128)(2,1)}, u32[]{:S(2)}, u32[]{:S(2)}) collective-permute-start(bf16[8,816,128]{2,1,0:T(8,128)(2,1)} %get-tuple-element.45.more_0_), channel_id=1, source_target_pairs={{0,8},{8,0},{16,24},{24,16},{1,9},{9,1},{17,25},{25,17},{2,10},{10... | collective-permute-start | bytes 5013512 | tf_op jit(solution)/shard_map/ppermute | solution.py:945
  91.8 84.3 %collective-permute-start = (bf16[8,816,128]{2,1,0:T(8,128)(2,1)}, bf16[8,816,128]{2,1,0:T(8,128)(2,1)}, u32[]{:S(2)}, u32[]{:S(2)}) collective-permute-start(bf16[8,816,128]{2,1,0:T(8,128)(2,1)} %get-tuple-element.45.more_0_), channel_id=1, source_target_pairs={{0,16},{8,24},{16,0},{24,8},{1,17},{9,25},{17,1},{25,9},{2,18},{10... | collective-permute-start | bytes 5013512 | tf_op jit(solution)/shard_map/ppermute | solution.py:945
  92.3 4.8 %copy-start.5 = (s32[16]{0:T(128)S(1)}, s32[16]{0:T(128)}, u32[]{:S(2)}) copy-start(s32[16]{0:T(128)} %param.13) | copy-start | bytes 196
  92.3 6.1 %copy-start.3 = (bf16[576]{0:T(1024)(128)(2,1)S(1)}, bf16[576]{0:T(1024)(128)(2,1)}, u32[]{:S(2)}) copy-start(bf16[576]{0:T(1024)(128)(2,1)} %param.14) | copy-start | bytes 3460
  92.3 83.7 %all-to-all-start = ((bf16[8,576,256]{2,1,0:T(8,128)(2,1)}), bf16[8,576,256]{2,1,0:T(8,128)(2,1)S(1)}, u32[]{:S(2)}, u32[]{:S(2)}) async-start(bf16[8,576,256]{2,1,0:T(8,128)(2,1)} %bitcast.4), calls=%async_computation | async-start | bytes 4718592 | tf_op jit(solution)/shard_map/all_to_all | solution.py:1187
  97.0 329.3 %reduce-scatter.2.cloned.1.call-start = ((), (), s32[]{:S(2)}) async-start(), calls=%async_computation.3 | async-start | bytes 6893568 | tf_op jit(solution)/shard_map/reduce_scatter | solution.py:1247
  112.9 61.8 %copy-start.4 = (bf16[576]{0:T(1024)(128)(2,1)S(1)}, bf16[576]{0:T(1024)(128)(2,1)}, u32[]{:S(2)}) copy-start(bf16[576]{0:T(1024)(128)(2,1)} %param.19) | copy-start | bytes 3460
  176.1 1.4 copy-start
  242.5 183.8 %all-to-all-start.1 = ((bf16[8,576,256]{2,1,0:T(8,128)(2,1)}), bf16[8,576,256]{2,1,0:T(8,128)(2,1)S(1)}, u32[]{:S(2)}, u32[]{:S(2)}) async-start(bf16[8,576,256]{2,1,0:T(8,128)(2,1)} %get-tuple-element.46), calls=%async_computation.1 | async-start | bytes 4718592 | tf_op jit(solution)/shard_map/all_to_all | solution.py:1187
  429.4 1.4 copy-start.1
Sparse Core Ops, SparseCore 0:
  242.6 119.2 reduce-scatter.1

commit v4 on v3

--- a/solution.py
+++ b/solution.py
@@ -399,59 +399,65 @@
     return jnp.concatenate([first, second], axis=0)
 
 
-def attend_kernel(inv_ref, q_ref, k_ref, v_ref, o_ref, l_ref, *, blocks, span, group):
+def attend_kernel(inv_ref, q_ref, k_ref, v_ref, o_ref, l_ref, acc_ref, *, blocks, span, group):
     wide = 2 * span
     row = lax.broadcasted_iota(jnp.int32, (wide, wide), 0)
     col = lax.broadcasted_iota(jnp.int32, (wide, wide), 1)
     keep = row <= col
 
-    def q_block(block, _):
+    def one_block(block, odd):
         queries = [
             lane_pair(q_ref, slice(HD * h, HD * h + HD), inv_ref, block, span) for h in range(group)
         ]
-
-        def scores_of(j):
-            keys = row_pair(k_ref, 0, inv_ref, j, span)
-            return tuple(dot(keys, query, 1, 0) for query in queries)
-
-        def take(j, scores, carry, masked):
-            values = lane_pair(v_ref, slice(0, HD), inv_ref, j, span)
-            out = []
-            for score, (peak, total, mixed) in zip(scores, carry):
-                if masked:
+        acc_ref[...] = jnp.zeros_like(acc_ref)
+
+        def step(first, count, state, diagonal):
+            state = list(state)
+            keys = [row_pair(k_ref, 0, inv_ref, first + u, span) for u in range(count)]
+            values = [lane_pair(v_ref, slice(0, HD), inv_ref, first + u, span) for u in range(count)]
+            items = [(u, h) for u in range(count) for h in range(group)]
+            scores = [dot(keys[u], queries[h], 1, 0) for u, h in items]
+            probs = []
+            for (u, h), score in zip(items, scores):
+                peak, total = state[h]
+                if diagonal and u == count - 1:
                     score = jnp.where(keep, score, neg_big)
                 new_peak = jnp.maximum(peak, jnp.max(score, axis=0, keepdims=True))
                 prob = jnp.exp(score - new_peak)
                 shrink = jnp.exp(peak - new_peak)
-                total = total * shrink + jnp.sum(prob, axis=0, keepdims=True)
-                mixed = mixed * shrink + dot(values, prob.astype(BF16), 1, 0)
-                out.append((new_peak, total, mixed))
-            return tuple(out)
-
-        def body(j, carry):
-            scores, state = carry
-            following = scores_of(j + 1)
-            return following, take(j, scores, state, False)
-
-        empty = tuple(
-            (jnp.full((1, wide), neg_big, F32), jnp.zeros((1, wide), F32), jnp.zeros((HD, wide), F32))
-            for _ in range(group)
-        )
-        scores, state = lax.fori_loop(0, block, body, (scores_of(0), empty))
-        state = take(block, scores, state, True)
-        mixed = jnp.concatenate([m * (1.0 / t) for (_, t, m) in state], axis=0)
+                state[h] = (new_peak, total * shrink + jnp.sum(prob, axis=0, keepdims=True))
+                probs.append((prob.astype(BF16), shrink))
+            for (u, h), (prob, shrink) in zip(items, probs):
+                cols = slice(h * wide, (h + 1) * wide)
+                acc_ref[:, cols] = acc_ref[:, cols] * shrink + dot(values[u], prob, 1, 0)
+            return tuple(state)
+
+        state = tuple(
+            (jnp.full((1, wide), neg_big, F32), jnp.zeros((1, wide), F32)) for _ in range(group)
+        )
+        state = lax.fori_loop(0, block // 4, lambda j, s: step(4 * j, 4, s, False), state)
+        state = lax.fori_loop(
+            2 * (block // 4), block // 2, lambda j, s: step(2 * j, 2, s, False), state
+        )
+        state = step(block - 1, 2, state, True) if odd else step(block, 1, state, True)
+        mixed = jnp.concatenate(
+            [acc_ref[:, wide * h : wide * (h + 1)] * (1.0 / state[h][1]) for h in range(group)], axis=0
+        ).astype(BF16)
         logs = jnp.concatenate(
-            [p + jnp.log(t) for (p, t, _) in state] + [jnp.zeros((8 - group, wide), F32)], axis=0
-        )
-        mixed_low = mixed.astype(BF16)
+            [p + jnp.log(t) for p, t in state] + [jnp.zeros((8 - group, wide), F32)], axis=0
+        )
         for part in range(2):
             where = span_slice(inv_ref, 2 * block + part, span)
             cols = slice(part * span, part * span + span)
-            o_ref[:, where] = mixed_low[:, cols]
+            o_ref[:, where] = mixed[:, cols]
             l_ref[0, :, where] = logs[:, cols]
+
+    def two_blocks(pair, _):
+        for odd in (0, 1):
+            one_block(2 * pair + odd, odd)
         return 0
 
-    lax.fori_loop(0, blocks, q_block, 0)
+    lax.fori_loop(0, blocks // 2, two_blocks, 0)
 
 
 def attention_forward(inv, q_t, k_nat, v_t, span):
@@ -471,6 +477,7 @@
                 wide_spec,
                 pl.BlockSpec((1, 8, tokens), lambda g, i: (g, 0, 0)),
             ],
+            scratch_shapes=[pltpu.VMEM((HD, group * 2 * span), F32)],
         ),
         out_shape=[
             jax.ShapeDtypeStruct(q_t.shape, BF16),
@@ -486,7 +493,7 @@
 
 def attend_back_kernel(
     inv_ref, q_ref, kt_ref, k_ref, v_ref, o_ref, do_ref, l_ref, cos_ref, sin_ref,
-    dq_ref, dk_ref, dv_ref, dk_sum, dv_sum, *, blocks, span, group,
+    dq_ref, dk_ref, dv_ref, dk_sum, dv_sum, dq_sum, *, blocks, span, group,
 ):
     wide = 2 * span
     row = lax.broadcasted_iota(jnp.int32, (wide, wide), 0)
@@ -500,8 +507,7 @@
         top, low = grad[:half], grad[half:]
         return jnp.concatenate([top * cos + low * sin, low * cos - top * sin], axis=0)
 
-    def q_block(step, _):
-        block = blocks - 1 - step
+    def one_block(block, odd):
         rows = [slice(HD * h, HD * h + HD) for h in range(group)]
         queries = [lane_pair(q_ref, r, inv_ref, block, span) for r in rows]
         grads = [lane_pair(do_ref, r, inv_ref, block, span) for r in rows]
@@ -514,35 +520,69 @@
             )
             for r, grad in zip(rows, grads)
         ]
-
-        def take(j, dqs, masked):
-            keys = row_pair(k_ref, 0, inv_ref, j, span)
-            values = row_pair(v_ref, 0, inv_ref, j, span)
-            keys_t = lane_pair(kt_ref, slice(0, HD), inv_ref, j, span)
-            out = []
-            dk = dv = None
-            for h in range(group):
-                prob = jnp.exp(dot(keys, queries[h], 1, 0) - logs[h : h + 1])
-                if masked:
+        dq_sum[...] = jnp.zeros_like(dq_sum)
+
+        def step(first, count, diagonal):
+            keys = [row_pair(k_ref, 0, inv_ref, first + u, span) for u in range(count)]
+            values = [row_pair(v_ref, 0, inv_ref, first + u, span) for u in range(count)]
+            keys_t = [lane_pair(kt_ref, slice(0, HD), inv_ref, first + u, span) for u in range(count)]
+            items = [(u, h) for u in range(count) for h in range(group)]
+            ahead, ready, dqs, sums = {}, {}, {}, {}
+
+            def products(i):
+                u, h = items[i]
+                ahead[i] = dot(keys[u], queries[h], 1, 0), dot(values[u], grads[h], 1, 0)
+
+            def softmax_part(i):
+                u, h = items[i]
+                score, dprob = ahead.pop(i)
+                prob = jnp.exp(score - logs[h : h + 1])
+                if diagonal and u == count - 1:
                     prob = jnp.where(keep, prob, 0.0)
-                dprob = dot(values, grads[h], 1, 0)
-                dscore = (prob * (dprob - deltas[h])).astype(BF16)
-                dk_term = dot(queries[h], dscore, 1, 1)
-                dv_term = dot(grads[h], prob.astype(BF16), 1, 1)
-                dk = dk_term if dk is None else dk + dk_term
-                dv = dv_term if dv is None else dv + dv_term
-                out.append(dqs[h] + dot(keys_t, dscore, 1, 0))
-            place = pl.ds(pl.multiple_of(j * wide, wide), wide)
-            dk_sum[:, place] += dk
-            dv_sum[:, place] += dv
-            return tuple(out)
-
-        dqs = tuple(jnp.zeros((HD, wide), F32) for _ in range(group))
-        dqs = lax.fori_loop(0, block, lambda j, c: take(j, c, False), dqs)
-        dqs = take(block, dqs, True)
+                ready[i] = prob.astype(BF16), (prob * (dprob - deltas[h])).astype(BF16)
+
+            def gradients(i):
+                u, h = items[i]
+                prob, dscore = ready.pop(i)
+                dq = dot(keys_t[u], dscore, 1, 0)
+                dqs[h] = dqs[h] + dq if h in dqs else dq
+                if u == count - 1:
+                    dq_sum[:, wide * h : wide * (h + 1)] += dqs[h]
+                dk, dv = dot(queries[h], dscore, 1, 1), dot(grads[h], prob, 1, 1)
+                if u in sums:
+                    dk, dv = dk + sums[u][0], dv + sums[u][1]
+                sums[u] = dk, dv
+                if h == group - 1:
+                    place = pl.ds(pl.multiple_of((first + u) * wide, wide), wide)
+                    dk_sum[:, place] += dk
+                    dv_sum[:, place] += dv
+
+            lead = 2
+            for i in range(min(lead, len(items))):
+                products(i)
+            for i in range(len(items) + 1):
+                if i + lead < len(items):
+                    products(i + lead)
+                if i > 0:
+                    gradients(i - 1)
+                if i < len(items):
+                    softmax_part(i)
+
+        def pair_step(j, _):
+            step(2 * j, 2, False)
+            return 0
+
+        lax.fori_loop(0, block // 2, pair_step, 0)
+        if odd:
+            step(block - 1, 2, True)
+        else:
+            step(block, 1, True)
         cos = lane_pair(cos_ref, slice(None), inv_ref, block, span)
         sin = lane_pair(sin_ref, slice(None), inv_ref, block, span)
-        dq = jnp.concatenate([rope_back(g * HD**-0.5, cos, sin) for g in dqs], axis=0).astype(BF16)
+        dq = jnp.concatenate(
+            [rope_back(dq_sum[:, wide * h : wide * (h + 1)] * HD**-0.5, cos, sin) for h in range(group)],
+            axis=0,
+        ).astype(BF16)
         place = pl.ds(pl.multiple_of(block * wide, wide), wide)
         dk = rope_back(dk_sum[:, place], cos, sin).astype(BF16)
         dv = dv_sum[:, place].astype(BF16)
@@ -552,9 +592,13 @@
             dq_ref[:, where] = dq[:, cols]
             dk_ref[:, where] = dk[:, cols]
             dv_ref[:, where] = dv[:, cols]
+
+    def two_blocks(step, _):
+        for odd in (1, 0):
+            one_block(blocks - 2 - 2 * step + odd, odd)
         return 0
 
-    lax.fori_loop(0, blocks, q_block, 0)
+    lax.fori_loop(0, blocks // 2, two_blocks, 0)
 
 
 def attention_backward(inv, q_t, k_t, k_nat, v_nat, o_t, do_t, logs, cos_t, sin_t, span):
@@ -576,7 +620,11 @@
                 pl.BlockSpec((1, 8, tokens), lambda g, i: (g, 0, 0)), tab_spec, tab_spec,
             ],
             out_specs=[wide_spec, kv_spec, kv_spec],
-            scratch_shapes=[pltpu.VMEM((HD, tokens), F32), pltpu.VMEM((HD, tokens), F32)],
+            scratch_shapes=[
+                pltpu.VMEM((HD, tokens), F32),
+                pltpu.VMEM((HD, tokens), F32),
+                pltpu.VMEM((HD, group * 2 * span), F32),
+            ],
         ),
         out_shape=[
             jax.ShapeDtypeStruct(q_t.shape, BF16),
@@ -1276,7 +1324,8 @@
 
 
 def shards(*args):
-    if args[0].shape[0] == lax.axis_size("seq"):
+    seqs, spans = args[0].shape[0], args[1].shape[0]
+    if seqs == lax.axis_size("seq") and spans % 4 == 0:
         return shards_sequences(*args)
     return shards_general(*args)
 

time: 440 us -> 406 us (0.923)
  Pallas kernels: 381 us -> 325 us
  waiting for transfers between devices: 0.03 us -> 23.9 us
    pallas_call x1, Pallas kernels: 103 us -> 60.9 us  [attention_backward(): pl.pallas_call(functools.partial(attend_back_kernel, blocks=tokens // (2...]
    pallas_call x1, Pallas kernels: 61.8 us -> 41.6 us  [attention_forward(): pl.pallas_call(functools.partial(attend_kernel, blocks=tokens // (2 * spa...]
    reduce_scatter x1, waiting for transfers between devices: 0.01 us -> 14.6 us  [shards_sequences(): lax.psum_scatter(rest_grads, ('dp', 'seq'), scatter_dimension=0, tiled=True)]
    ppermute x3, waiting for transfers between devices: 0.01 us -> 9.28 us  [gather_rows(): held.append(lax.ppermute(array, 'dp', [(i, i ^ mask) for i in range(dp)]))]
    pallas_call x1, Pallas kernels: 67.1 us -> 73.1 us  [finish(): pl.pallas_call(functools.partial(finish_kernel, dp=dp, seq=seq, kv_width=...]
  transfers between devices with their start and end apart: 6 -> 6, of which waited for: 0 -> 2; matrix products, arithmetic and copies ran while one was open for 3% -> 3% of each run, Pallas kernels for 55% -> 46%
where the time goes in v4:
time: 406 us; the launch traced here: 405 us
  Pallas kernels  325 us (80%)
  waiting for transfers between devices  23.9 us (6%)
  local copies, waits for them, and re-layouts  17.5 us (4%)
  between operations  14.2 us (3%)
  other arithmetic  12.4 us (3%)
  starting transfers between devices  11.4 us (3%)
    pallas_call x1, Pallas kernels, bring(): pl.pallas_call(functools.partial(bring_kernel, dp=dp, seq=seq), in_specs=...  73.6 us
    pallas_call x1, Pallas kernels, finish(): pl.pallas_call(functools.partial(finish_kernel, dp=dp, seq=seq, kv_width=...  73.1 us
    pallas_call x1, Pallas kernels, mlp_both(): pl.pallas_call(functools.partial(mlp_kernel, chunk=chunk, dp=dp, seq=seq)...  64.9 us
    pallas_call x1, Pallas kernels, attention_backward(): pl.pallas_call(functools.partial(attend_back_kernel, blocks=tokens // (2...  60.9 us
    pallas_call x1, Pallas kernels, attention_forward(): pl.pallas_call(functools.partial(attend_kernel, blocks=tokens // (2 * spa...  41.6 us
    reduce_scatter x1, waiting for transfers between devices, shards_sequences(): lax.psum_scatter(rest_grads, ('dp', 'seq'), scatter_dimension=0, tiled=True)  14.6 us
    pallas_call x1, Pallas kernels, project_qkv(): pl.pallas_call(functools.partial(qkv_kernel, heads=heads, kv_heads=kv_hea...  11.2 us
    unnamed x23, local copies, waits for them, and re-layouts  10.3 us
  transfers between devices with their start and end apart: 6, of which 2 were waited for; matrix products, arithmetic and copies ran while one was open for 3% of the time, Pallas kernels for 46%

profile of v4, /device:TPU:0, one launch (start us, length us, event | category | flops | bytes accessed | tf_op | source)
XLA Modules:
  0.0 404.8 jit_solution(4166016194886916604)
XLA Ops:
  7.2 0.8 copy.34
  8.0 0.8 copy.35
  15.0 1.5 fusion.5.first_ref
  16.5 73.6 %bring.1 = (bf16[8,576,256]{2,1,0:T(8,128)(2,1)}, bf16[32,144,128]{2,1,0:T(8,128)(2,1)}, bf16[8,816,128]{2,1,0:T(8,128)(2,1)}) custom-call(bf16[8,576,256]{2,1,0:T(8,128)(2,1)} %bitcast.26, bf16[1,144,128]{2,1,0:T(8,128)(2,1)} %fusion.5.first_ref, bf16[1,816,128]{2,1,0:T(8,128)(2,1)} %bitcast.31), custom_call_target="tpu_custom_call" | custom-call | tf_op jit(solution)/shard_map/bring/pallas_call | solution.py:755
  90.7 1.1 collective-permute-start.1
  92.3 4.7 %all-to-all-start = ((bf16[8,576,256]{2,1,0:T(8,128)(2,1)}), bf16[8,576,256]{2,1,0:T(8,128)(2,1)S(1)}, u32[]{:S(2)}, u32[]{:S(2)}) async-start(bf16[8,576,256]{2,1,0:T(8,128)(2,1)} %bitcast.4), calls=%async_computation | async-start | bytes 4718592 | tf_op jit(solution)/shard_map/all_to_all | solution.py:1235
  97.1 1.3 sort.17
  98.5 0.9 reshape.65.gain_ref
  99.9 1.8 multiply_sine_fusion
  101.6 11.2 %project_qkv.1 = (bf16[576,2048]{1,0:T(8,128)(2,1)}, bf16[192,2048]{1,0:T(8,128)(2,1)}, bf16[192,2048]{1,0:T(8,128)(2,1)}, bf16[3,2048,64]{2,1,0:T(8,128)(2,1)},...) custom-call(s32[32]{0:T(128)} %fusion.26.where_ref, bf16[8,576,256]{2,1,0:T(8,128)(2,1)} %get-tuple-element.37.x_ref, ...), custom_call_target="tpu_custom_call" | custom-call | flops 4529848320 | bytes 10240000 | tf_op jit(solution)/shard_map/project_qkv/pallas_call | solution.py:826
  112.9 41.6 %attention_forward.1 = (bf16[576,2048]{1,0:T(8,128)(2,1)}, f32[3,8,2048]{2,1,0:T(8,128)}) custom-call(s32[16]{0:T(128)} %get-tuple-element.38.inv_ref, bf16[576,2048]{1,0:T(8,128)(2,1)} %get-tuple-element.40.q_ref, bf16[3,2048,64]{2,1,0:T(8,128)(2,1)} %get-tuple-element.41.k_ref, bf16[192,2048]{1,0:T(8,128)(2,1)} %get-tuple-element.42.v_ref), custom_call_target="tpu_custom_call" | custom-call | flops 38654705664 | bytes 12288000 | tf_op jit(solution)/shard_map/attention_forward/pallas_call | solution.py:470
  154.5 0.9 reshape.66.gain_ref
  155.9 9.3 %collective-permute-done.more_1_ = bf16[8,816,128]{2,1,0:T(8,128)(2,1)} collective-permute-done((bf16[8,816,128]{2,1,0:T(8,128)(2,1)}, bf16[8,816,128]{2,1,0:T(8,128)(2,1)}, u32[]{:S(2)}, u32[]{:S(2)}) %collective-permute-start) | collective-permute-done | bytes 1671200 | tf_op jit(solution)/shard_map/ppermute | solution.py:993
  165.1 1.4 copy-done
  166.6 64.9 %mlp_both.1 = (bf16[8,576,256]{2,1,0:T(8,128)(2,1)}, f32[8,576,256]{2,1,0:T(8,128)}, bf16[576,2048]{1,0:T(8,128)(2,1)}, bf16[32,816,128]{2,1,0:T(8,128)(2,1)}, f32[1,576]{1,0:T(1,128)}) custom-call(s32[8]{0:T(128)} %bitcast.32, bf16[8,576,256]{2,1,0:T(8,128)(2,1)} %get-tuple-element.37.x_ref, bf16[576,2048]{1,0:T(8,128)(2,1)} %get-tuple-element.43.mixed_ref.o_ref, ...), custom_call_target="tpu_custom_call" | custom-call | flops 36691771392 | bytes 16515072 | tf_op jit(solution)/shard_map/mlp_both/pallas_call | solution.py:1008
  231.5 4.5 %all-to-all-start.1 = ((bf16[8,576,256]{2,1,0:T(8,128)(2,1)}), bf16[8,576,256]{2,1,0:T(8,128)(2,1)S(1)}, u32[]{:S(2)}, u32[]{:S(2)}) async-start(bf16[8,576,256]{2,1,0:T(8,128)(2,1)} %get-tuple-element.46), calls=%async_computation.1 | async-start | bytes 4718592 | tf_op jit(solution)/shard_map/all_to_all | solution.py:1235
  236.0 60.9 %attention_backward.1 = (bf16[576,2048]{1,0:T(8,128)(2,1)}, bf16[192,2048]{1,0:T(8,128)(2,1)}, bf16[192,2048]{1,0:T(8,128)(2,1)}) custom-call(s32[16]{0:T(128)} %get-tuple-element.38.inv_ref, bf16[576,2048]{1,0:T(8,128)(2,1)} %get-tuple-element.40.q_ref, bf16[192,2048]{1,0:T(8,128)(2,1)} %get-tuple-element.48.kt_ref, ...), custom_call_target="tpu_custom_call" | custom-call | flops 77309411328 | bytes 18432000 | tf_op jit(solution)/shard_map/attention_backward/pallas_call | solution.py:613
  296.9 73.1 %finish.1 = (bf16[8,576,256]{2,1,0:T(8,128)(2,1)}, f32[144,128]{1,0:T(8,128)}, f32[8,576]{1,0:T(8,128)}) custom-call(bf16[8,576,256]{2,1,0:T(8,128)(2,1)} %get-tuple-element.37.x_ref, f32[8,576,256]{2,1,0:T(8,128)} %get-tuple-element.47.dmid_ref, bf16[576,2048]{1,0:T(8,128)(2,1)} %get-tuple-element.52.dq_ref, bf16[192,2048]{1,0:T(8,128)(2,1)} %get-tuple-element.53.dk_ref, ...), custom_call_target="tpu_custom_call" | custom-call | flops 4529848320 | bytes 14155776 | tf_op jit(solution)/shard_map/finish/pallas_call | solution.py:1194
  370.0 1.1 fusion.33
  372.4 1.4 slice_reduce_fusion
  373.9 4.3 %convert_bitcast_fusion = f32[8,256,576]{1,2,0:T(8,128)} fusion(bf16[8,576,256]{2,1,0:T(8,128)(2,1)} %get-tuple-element.57), kind=kLoop, calls=%fused_computation | loop fusion | flops 1179648 | bytes 7077888 | tf_op jit(solution)/shard_map/transpose | solution.py:1301
  378.1 14.6 %reduce-scatter.2.cloned.1.call-done = bf16[1,816,128]{2,1,0:T(8,128)(2,1)} async-done(((bf16[32,816,128]{2,1,0:T(8,128)(2,1)}), bf16[1,816,128]{2,1,0:T(8,128)(2,1)}) %reduce-scatter.2.cloned.1.call-update) | async-done | bytes 208912 | tf_op jit(solution)/shard_map/reduce_scatter | solution.py:1295
  392.7 1.0 fusion.32
  395.9 1.4 copy.49
  (44 shorter events, 12.6 us)
Async XLA Ops:
  15.0 1.5 copy-start.2
  90.1 65.7 %collective-permute-start.2 = (bf16[8,816,128]{2,1,0:T(8,128)(2,1)}, bf16[8,816,128]{2,1,0:T(8,128)(2,1)}, u32[]{:S(2)}, u32[]{:S(2)}) collective-permute-start(bf16[8,816,128]{2,1,0:T(8,128)(2,1)} %get-tuple-element.45.more_0_), channel_id=1, source_target_pairs={{0,24},{8,16},{16,8},{24,0},{1,25},{9,17},{17,9},{25,1},{2,26},{10... | collective-permute-start | bytes 5013512 | tf_op jit(solution)/shard_map/ppermute | solution.py:993
  90.7 65.2 %collective-permute-start.1 = (bf16[8,816,128]{2,1,0:T(8,128)(2,1)}, bf16[8,816,128]{2,1,0:T(8,128)(2,1)}, u32[]{:S(2)}, u32[]{:S(2)}) collective-permute-start(bf16[8,816,128]{2,1,0:T(8,128)(2,1)} %get-tuple-element.45.more_0_), channel_id=1, source_target_pairs={{0,8},{8,0},{16,24},{24,16},{1,9},{9,1},{17,25},{25,17},{2,10},{10... | collective-permute-start | bytes 5013512 | tf_op jit(solution)/shard_map/ppermute | solution.py:993
  91.8 73.3 %collective-permute-start = (bf16[8,816,128]{2,1,0:T(8,128)(2,1)}, bf16[8,816,128]{2,1,0:T(8,128)(2,1)}, u32[]{:S(2)}, u32[]{:S(2)}) collective-permute-start(bf16[8,816,128]{2,1,0:T(8,128)(2,1)} %get-tuple-element.45.more_0_), channel_id=1, source_target_pairs={{0,16},{8,24},{16,0},{24,8},{1,17},{9,25},{17,1},{25,9},{2,18},{10... | collective-permute-start | bytes 5013512 | tf_op jit(solution)/shard_map/ppermute | solution.py:993
  92.3 4.8 %copy-start.5 = (s32[16]{0:T(128)S(1)}, s32[16]{0:T(128)}, u32[]{:S(2)}) copy-start(s32[16]{0:T(128)} %param.13) | copy-start | bytes 196
  92.3 6.1 %copy-start.3 = (bf16[576]{0:T(1024)(128)(2,1)S(1)}, bf16[576]{0:T(1024)(128)(2,1)}, u32[]{:S(2)}) copy-start(bf16[576]{0:T(1024)(128)(2,1)} %param.14) | copy-start | bytes 3460
  92.3 72.8 %all-to-all-start = ((bf16[8,576,256]{2,1,0:T(8,128)(2,1)}), bf16[8,576,256]{2,1,0:T(8,128)(2,1)S(1)}, u32[]{:S(2)}, u32[]{:S(2)}) async-start(bf16[8,576,256]{2,1,0:T(8,128)(2,1)} %bitcast.4), calls=%async_computation | async-start | bytes 4718592 | tf_op jit(solution)/shard_map/all_to_all | solution.py:1235
  97.0 295.7 %reduce-scatter.2.cloned.1.call-start = ((), (), s32[]{:S(2)}) async-start(), calls=%async_computation.3 | async-start | bytes 6893568 | tf_op jit(solution)/shard_map/reduce_scatter | solution.py:1295
  112.9 41.6 %copy-start.4 = (bf16[576]{0:T(1024)(128)(2,1)S(1)}, bf16[576]{0:T(1024)(128)(2,1)}, u32[]{:S(2)}) copy-start(bf16[576]{0:T(1024)(128)(2,1)} %param.19) | copy-start | bytes 3460
  165.1 1.4 copy-start
  231.5 146.6 %all-to-all-start.1 = ((bf16[8,576,256]{2,1,0:T(8,128)(2,1)}), bf16[8,576,256]{2,1,0:T(8,128)(2,1)S(1)}, u32[]{:S(2)}, u32[]{:S(2)}) async-start(bf16[8,576,256]{2,1,0:T(8,128)(2,1)} %get-tuple-element.46), calls=%async_computation.1 | async-start | bytes 4718592 | tf_op jit(solution)/shard_map/all_to_all | solution.py:1235
  395.9 1.4 copy-start.1
Sparse Core Ops, SparseCore 0:
  231.7 161.0 reduce-scatter.1

commit v5 on v4

--- a/solution.py
+++ b/solution.py
@@ -657,6 +657,21 @@
     return seq_stages(seq) + [("dp", b) for b in reversed(bits_of(dp))]
 
 
+def rest_chains(dp, seq):
+    near, far = [("seq", b) for b in bits_of(seq)[:1]], [("seq", b) for b in reversed(bits_of(seq)[1:])]
+    chip = [("dp", b) for b in reversed(bits_of(dp)[1:])]
+    return far + near + chip, far + chip + near
+
+
+def away_place(stages, d, s, my_dp, my_seq):
+    place = 0
+    for at, (axis, bit) in enumerate(stages):
+        mine = ((my_dp if axis == "dp" else my_seq) // bit) % 2
+        theirs = ((d if axis == "dp" else s) // bit) % 2
+        place = place + (1 << at) * (1 - mine if theirs else mine)
+    return place
+
+
 def arrival_order(stages, dp, seq, my_dp, my_seq):
     ids = jnp.arange(dp * seq, dtype=jnp.int32)
     away = {"dp": (ids // seq) ^ my_dp, "seq": (ids % seq) ^ my_seq}
@@ -865,9 +880,10 @@
     where_ref, x_ref, mixed_ref, dy_ref, gain_ref, *more, chunk, dp, seq,
 ):
     packs = more[:dp]
-    out_ref, dmid_ref, dmixed_ref, grads_ref, gain_grad_ref = more[dp : dp + 5]
+    out_ref, dmid_ref, dmixed_ref = more[dp : dp + 3]
+    one_refs, two_refs, gain_grad_ref = more[dp + 3 : dp + 5], more[dp + 5 : dp + 7], more[dp + 7]
     (o_w, o_t, gate_w, gate_t, up_w, up_t, down_w, down_t, o_sum, gate_sum, up_sum, down_sum, gain_sum,
-     pack, pack_sem) = more[dp + 5 :]
+     pack, pack_sem) = more[dp + 8 :]
     step, steps = pl.program_id(0), pl.num_programs(0)
     width, ff = gate_w.shape
     lanes = pack.shape[3]
@@ -960,26 +976,39 @@
     @pl.when(step == steps - 1)
     def _():
         gain_grad_ref[...] = jnp.sum(gain_sum[...].T, axis=0, keepdims=True)
+        my_dp, my_seq = lax.axis_index("dp"), lax.axis_index("seq")
+        upper = my_dp % 2 == 1
+
+        def put(refs, place, first, even, odd):
+            keep_ref, give_ref = refs
+            span = slice(first, first + even.shape[0])
+            keep_ref[place, span, :] = jnp.where(upper, odd, even).astype(BF16)
+            give_ref[place, span, :] = jnp.where(upper, even, odd).astype(BF16)
+
+        blank = jnp.zeros((lanes - o_cols, width), F32)
+        edge = jnp.zeros((padded - o_cols, lanes), F32)
         for s in range(seq):
             tall = lambda total, first, count: total[first : first + count, :]
-            blank = jnp.zeros((lanes - o_cols, width), F32)
-            o_piece = jnp.concatenate([tall(o_sum, o_cols * s, o_cols), blank], axis=0).T.astype(BF16)
-            gate_piece = tall(gate_sum, ff_cols * s, lanes).T.astype(BF16)
-            up_piece = tall(up_sum, ff_cols * s, lanes).T.astype(BF16)
+            o_piece = jnp.concatenate([tall(o_sum, o_cols * s, o_cols), blank], axis=0).T
+            gate_piece = tall(gate_sum, ff_cols * s, lanes).T
+            up_piece = tall(up_sum, ff_cols * s, lanes).T
             both = jnp.concatenate(
                 [tall(gate_sum, ff_cols * s + lanes, spare), tall(up_sum, ff_cols * s + lanes, spare)], axis=0
-            ).T.astype(BF16)
-            for d in range(dp):
-                at = d * seq + s
-                band = slice(rows * d, rows * (d + 1))
-                for i, piece in enumerate((o_piece, gate_piece, up_piece, both)):
-                    grads_ref[at, rows * i : rows * (i + 1), :] = piece[band]
+            ).T
+            for d in range(0, dp, 2):
+                bands = slice(rows * d, rows * (d + 1)), slice(rows * (d + 1), rows * (d + 2))
+                one, two = [away_place(c, d, s, my_dp, my_seq) for c in rest_chains(dp, seq)]
+                for i, piece in enumerate((o_piece, gate_piece, up_piece)):
+                    put(one_refs, one, rows * i, piece[bands[0]], piece[bands[1]])
+                put(two_refs, two, 0, both[bands[0]], both[bands[1]])
                 for t in range(ff_rows // lanes):
-                    first = 4 * rows + padded * t
-                    cols = slice(ff_rows * d + lanes * t, ff_rows * d + lanes * (t + 1))
-                    piece = down_sum[o_cols * s : o_cols * (s + 1), cols]
-                    piece = jnp.concatenate([piece, jnp.zeros((padded - o_cols, lanes), F32)], axis=0)
-                    grads_ref[at, first : first + padded, :] = piece.astype(BF16)
+                    pair = []
+                    for at in (d, d + 1):
+                        cols = slice(ff_rows * at + lanes * t, ff_rows * at + lanes * (t + 1))
+                        pair.append(
+                            jnp.concatenate([down_sum[o_cols * s : o_cols * (s + 1), cols], edge], axis=0)
+                        )
+                    put(two_refs, two, rows + padded * t, *pair)
 
 
 def row_bits(at, dp):
@@ -999,6 +1028,9 @@
     tokens = blocks * block
     dp, seq = lax.axis_size("dp"), lax.axis_size("seq")
     grad_rows, lanes = packs[0].shape[1:]
+    first_rows = 3 * (width // dp)
+    one = dp * seq // 2, first_rows, lanes
+    two = dp * seq // 2, grad_rows - first_rows, lanes
     tok = pl.BlockSpec((batch, width, block), lambda i, w: (i, 0, 0))
     col = pl.BlockSpec((width, batch * block), lambda i, w: (0, i))
     once = lambda shape: pl.BlockSpec(
@@ -1011,7 +1043,7 @@
             num_scalar_prefetch=1,
             grid=(blocks // batch,),
             in_specs=[tok, col, tok, once((width, 1))] + [hbm] * dp,
-            out_specs=[tok, tok, col, once((dp * seq, grad_rows, lanes)), once((1, width))],
+            out_specs=[tok, tok, col, once(one), once(one), once(two), once(two), once((1, width))],
             scratch_shapes=[
                 pltpu.VMEM((width, width), BF16),
                 pltpu.VMEM((width, width), BF16),
@@ -1034,7 +1066,10 @@
             jax.ShapeDtypeStruct(x.shape, BF16),
             jax.ShapeDtypeStruct(x.shape, F32),
             jax.ShapeDtypeStruct((width, tokens), BF16),
-            jax.ShapeDtypeStruct((dp * seq, grad_rows, lanes), BF16),
+            jax.ShapeDtypeStruct(one, BF16),
+            jax.ShapeDtypeStruct(one, BF16),
+            jax.ShapeDtypeStruct(two, BF16),
+            jax.ShapeDtypeStruct(two, BF16),
             jax.ShapeDtypeStruct((1, width), F32),
         ],
         compiler_params=pltpu.CompilerParams(vmem_limit_bytes=60 * 2**20),
@@ -1053,22 +1088,65 @@
     return index
 
 
+def add_blocks(total_ref, term_ref, count, total_first=0, term_first=0):
+    def one(i, _):
+        total = total_ref[total_first + i].astype(F32) + term_ref[term_first + i].astype(F32)
+        total_ref[total_first + i] = total.astype(BF16)
+        return 0
+
+    lax.fori_loop(0, count, one, 0)
+
+
 def finish_kernel(
     x_ref, dmid_ref, dq_ref, dk_ref, dv_ref, gain_ref, w_t_ref, other_gain_ref,
-    out_ref, grads_ref, gains_ref,
-    w_nat, w_sum, gain_sum, din, packed, landed, gain_held, gain_landed,
-    own_sem, d_send, d_recv, r_send, r_recv, g_send, g_recv, *, dp, seq, kv_width,
+    keep_one, keep_two, came_one, came_two,
+    out_ref, gains_ref, q_ref, k_ref, v_ref, o_ref, gate_ref, up_ref, down_ref,
+    w_nat, w_sum, gain_sum, din, packed, landed, one, one_came, one_landed, two, two_came, two_landed,
+    gain_held, gain_landed,
+    own_sem, d_send, d_recv, r_send, r_recv, g_send, g_recv, fetch_sem, *, dp, seq, kv_width,
 ):
     step, steps = pl.program_id(0), seq // 2
     my_dp, my_seq = lax.axis_index("dp"), lax.axis_index("seq")
     width = w_nat.shape[0]
-    lanes = grads_ref.shape[1]
+    lanes = packed.shape[2]
     rows = width // dp
     q_cols, kv_cols = width // seq, kv_width // seq
-    stages = all_stages(dp, seq)
+    orders = [all_stages(dp, seq), *rest_chains(dp, seq)]
+    held = [packed, one, two]
+    arrived = [landed, one_landed, two_landed]
+    fetches = [
+        pltpu.make_async_copy(source, target, fetch_sem.at[i])
+        for i, (source, target) in enumerate(
+            ((keep_one, one), (keep_two, two), (came_one, one_came), (came_two, two_came))
+        )
+    ]
+
+    def halve(chain, turn):
+        at = len(orders[chain]) - 1 - turn
+        half = 1 << at
+        return pltpu.make_async_remote_copy(
+            src_ref=held[chain].at[pl.ds(half, half)],
+            dst_ref=arrived[chain].at[pl.ds(half, half)],
+            send_sem=r_send.at[chain, turn],
+            recv_sem=r_recv.at[chain, turn],
+            device_id=stage_peer(my_dp, my_seq, orders[chain][at]),
+            device_id_type=pl.DeviceIdType.MESH,
+        )
+
+    def take(chain, turn):
+        halve(chain, turn).wait_recv()
+        half = 1 << (len(orders[chain]) - 1 - turn)
+        if half > 1:
+            add_blocks(held[chain], arrived[chain], half, 0, half)
+            halve(chain, turn + 1).start()
+
+    def result(chain):
+        return held[chain][0].astype(F32) + arrived[chain][1].astype(F32)
 
     @pl.when(step == 0)
     def _():
+        for fetch in fetches:
+            fetch.start()
         greet(all_peers(my_dp, my_seq, dp, seq))
         w_sum[...] = jnp.zeros_like(w_sum)
         gain_sum[...] = jnp.zeros_like(gain_sum)
@@ -1109,6 +1187,14 @@
         def _():
             move(2 * back).start()
             move(2 * back + 1).start()
+
+    @pl.when(step == 0)
+    def _():
+        for fetch in fetches:
+            fetch.wait()
+        for chain, came in ((1, one_came), (2, two_came)):
+            add_blocks(held[chain], came, came.shape[0])
+            halve(chain, 0).start()
 
     @pl.when(step == steps - 1)
     def _():
@@ -1128,59 +1214,65 @@
                 axis=0,
             ).T.astype(BF16)
             for d in range(dp):
-                place = 0
-                for at, (axis, bit) in enumerate(stages):
-                    mine = ((my_dp if axis == "dp" else my_seq) // bit) % 2
-                    theirs = ((d if axis == "dp" else s) // bit) % 2
-                    place = place + (1 << at) * (1 - mine if theirs else mine)
-                packed[place] = piece[rows * d : rows * (d + 1)]
+                packed[away_place(orders[0], d, s, my_dp, my_seq)] = piece[rows * d : rows * (d + 1)]
         gain_row = jnp.sum(gain_sum[...].T, axis=0, keepdims=True)
         gain_held[0] = jnp.concatenate(
             [gain_row, other_gain_ref[...], jnp.zeros((6, width), F32)], axis=0
         )
-        sent = []
-        for turn, at in enumerate(reversed(range(len(stages)))):
-            half = 1 << at
-            peer = stage_peer(my_dp, my_seq, stages[at])
-            send = pltpu.make_async_remote_copy(
-                src_ref=packed.at[pl.ds(half, half)],
-                dst_ref=landed.at[pl.ds(half, half)],
-                send_sem=r_send.at[at],
-                recv_sem=r_recv.at[at],
-                device_id=peer,
-                device_id_type=pl.DeviceIdType.MESH,
-            )
-            gain_copy = pltpu.make_async_remote_copy(
+        turns = len(orders[0])
+        gain_copies = [
+            pltpu.make_async_remote_copy(
                 src_ref=gain_held.at[turn],
                 dst_ref=gain_landed.at[turn],
                 send_sem=g_send.at[turn],
                 recv_sem=g_recv.at[turn],
-                device_id=peer,
+                device_id=stage_peer(my_dp, my_seq, orders[0][turns - 1 - turn]),
                 device_id_type=pl.DeviceIdType.MESH,
             )
-            send.start()
-            gain_copy.start()
-            sent += [send, gain_copy]
-            gain_copy.wait_recv()
+            for turn in range(turns)
+        ]
+        halve(0, 0).start()
+        gain_copies[0].start()
+        for turn in range(turns):
+            gain_copies[turn].wait_recv()
             gain_held[turn + 1] = gain_held[turn] + gain_landed[turn]
-            send.wait_recv()
-            both = packed[0:half].astype(F32) + landed[half : 2 * half].astype(F32)
-            if at == 0:
-                grads_ref[...] = both[0]
-            else:
-                packed[0:half] = both.astype(BF16)
-        gains_ref[...] = gain_held[len(stages)]
-        for copy in sent:
+            if turn + 1 < turns:
+                gain_copies[turn + 1].start()
+            take(0, turn)
+            if turn > 0:
+                for chain in (1, 2):
+                    take(chain, turn - 1)
+        gains_ref[...] = gain_held[turns]
+        qkv = result(0)
+        q_ref[...] = qkv[:, :q_cols]
+        turned = qkv.T
+        k_ref[...] = turned[q_cols : q_cols + kv_cols]
+        v_ref[...] = turned[q_cols + kv_cols : q_cols + 2 * kv_cols]
+        first, second = result(1), result(2)
+        spare = gate_ref.shape[1] - lanes
+        padded = -(-q_cols // 16) * 16
+        o_ref[...] = first[:rows, :q_cols]
+        gate_ref[...] = jnp.concatenate([first[rows : 2 * rows], second[:rows, :spare]], axis=1)
+        up_ref[...] = jnp.concatenate([first[2 * rows :], second[:rows, spare : 2 * spare]], axis=1)
+        for t in range(down_ref.shape[1] // lanes):
+            at = rows + padded * t
+            down_ref[:, lanes * t : lanes * (t + 1)] = second[at : at + q_cols]
+        for copy in gain_copies:
             copy.wait_send()
+        for chain in range(3):
+            for turn in range(len(orders[chain])):
+                halve(chain, turn).wait_send()
         for away in range(1, seq):
             move(away).wait()
         own.wait()
 
 
-def finish(x, dmid, dq_t, dk_t, dv_t, gain, w_t, other_gain, lanes):
+def finish(x, dmid, dq_t, dk_t, dv_t, gain, w_t, other_gain, keep_one, keep_two, came_one, came_two, ff):
     blocks, width, block = x.shape
     tokens = blocks * block
     feats = w_t.shape[0]
+    kv_width = dk_t.shape[0]
+    lanes = keep_one.shape[2]
     dp, seq = lax.axis_size("dp"), lax.axis_size("seq")
     rows = width // dp
     stages = len(all_stages(dp, seq))
@@ -1191,19 +1283,26 @@
     tok = pl.BlockSpec((2, width, block), lambda i: (pair(i), 0, 0))
     col = lambda rows: pl.BlockSpec((rows, 2 * block), lambda i: (0, pair(i)))
     once = lambda shape: pl.BlockSpec(shape, lambda i: (0,) * len(shape), pipeline_mode=pl.Buffered(1))
+    hbm = pl.BlockSpec(memory_space=pl.ANY)
+    small = [
+        (8, width),
+        (rows, width // seq),
+        (kv_width // seq, rows),
+        (kv_width // seq, rows),
+        (rows, width // seq),
+        (rows, ff // seq),
+        (rows, ff // seq),
+        (width // seq, ff // dp),
+    ]
     return pl.pallas_call(
-        functools.partial(finish_kernel, dp=dp, seq=seq, kv_width=dk_t.shape[0]),
+        functools.partial(finish_kernel, dp=dp, seq=seq, kv_width=kv_width),
         grid=(blocks // 2,),
         in_specs=[
-            tok, tok, col(dq_t.shape[0]), col(dk_t.shape[0]), col(dv_t.shape[0]),
-            once((width, 1)), once((feats, width)), once((1, width)),
+            tok, tok, col(dq_t.shape[0]), col(kv_width), col(kv_width),
+            once((width, 1)), once((feats, width)), once((1, width)), hbm, hbm, hbm, hbm,
         ],
-        out_specs=[pl.BlockSpec(memory_space=pl.ANY), once((rows, lanes)), once((8, width))],
-        out_shape=[
-            jax.ShapeDtypeStruct(x.shape, BF16),
-            jax.ShapeDtypeStruct((rows, lanes), F32),
-            jax.ShapeDtypeStruct((8, width), F32),
-        ],
+        out_specs=[hbm] + [once(shape) for shape in small],
+        out_shape=[jax.ShapeDtypeStruct(x.shape, BF16)] + [jax.ShapeDtypeStruct(shape, F32) for shape in small],
         scratch_shapes=[
             pltpu.VMEM((width, feats), BF16),
             pltpu.VMEM((feats, width), F32),
@@ -1211,15 +1310,18 @@
             pltpu.VMEM(x.shape, BF16),
             pltpu.VMEM((dp * seq, rows, lanes), BF16),
             pltpu.VMEM((dp * seq, rows, lanes), BF16),
+            *[pltpu.VMEM(keep_one.shape, BF16)] * 3,
+            *[pltpu.VMEM(keep_two.shape, BF16)] * 3,
             pltpu.VMEM((stages + 1, 8, width), F32),
             pltpu.VMEM((stages, 8, width), F32),
             pltpu.SemaphoreType.DMA,
             pltpu.SemaphoreType.DMA((seq - 1,)),
             pltpu.SemaphoreType.DMA((seq - 1,)),
+            pltpu.SemaphoreType.DMA((3, stages)),
+            pltpu.SemaphoreType.DMA((3, stages)),
             pltpu.SemaphoreType.DMA((stages,)),
             pltpu.SemaphoreType.DMA((stages,)),
-            pltpu.SemaphoreType.DMA((stages,)),
-            pltpu.SemaphoreType.DMA((stages,)),
+            pltpu.SemaphoreType.DMA((4,)),
         ],
         compiler_params=pltpu.CompilerParams(
             collective_id=2, has_side_effects=True, vmem_limit_bytes=VMEM_BYTES
@@ -1228,7 +1330,7 @@
             flops=4 * tokens * width * feats, bytes_accessed=tokens * width * 12, transcendentals=0
         ),
         name="finish",
-    )(x, dmid, dq_t, dk_t, dv_t, gain, w_t, other_gain)
+    )(x, dmid, dq_t, dk_t, dv_t, gain, w_t, other_gain, keep_one, keep_two, came_one, came_two)
 
 
 def exchange(blocks):
@@ -1288,38 +1390,31 @@
         where_first, x, gain_one, first_all, cos_t, sin_t, heads, kv_heads, rows
     )
     o_t, logs = attention_forward(inv, q_t, k_nat, v_t, span)
-    out, dmid, do_t, rest_grads, gain_two_term = mlp_both(
+    out, dmid, do_t, keep_one, give_one, keep_two, give_two, gain_two_term = mlp_both(
         where_second, x, o_t, dy, gain_two, second_all, ff
     )
+    sibling = [(i, i ^ 1) for i in range(dp)]
+    came_one, came_two = lax.ppermute(give_one, "dp", sibling), lax.ppermute(give_two, "dp", sibling)
     hidden_out = exchange(out).transpose(0, 2, 1)
-    rest_sum = lax.psum_scatter(rest_grads, ("dp", "seq"), scatter_dimension=0, tiled=True)[0].astype(F32)
 
     dq_t, dk_t, dv_t = attention_backward(
         inv, q_t, k_t, k_nat, v_nat, o_t, do_t, logs, cos_t, sin_t, span
     )
-    din, qkv_sum, gains = finish(x, dmid, dq_t, dk_t, dv_t, gain_one, w_t, gain_two_term, lanes)
-    grad_in = din.astype(F32).transpose(0, 2, 1)
-    o_sum, gate_sum, up_sum, both_sum = [rest_sum[rows * i : rows * (i + 1)] for i in range(4)]
-    spare = gate_weight.shape[1] - lanes
-    down_sum = jnp.concatenate(
-        [
-            rest_sum[4 * rows + padded * t : 4 * rows + padded * t + q_cols]
-            for t in range(ff_rows // lanes)
-        ],
-        axis=1,
+    din, gains, q_grad, k_grad, v_grad, o_grad, gate_grad, up_grad, down_grad = finish(
+        x, dmid, dq_t, dk_t, dv_t, gain_one, w_t, gain_two_term, keep_one, keep_two, came_one, came_two, ff
     )
     return (
         hidden_out,
-        grad_in,
+        din.astype(F32).transpose(0, 2, 1),
         gains[0],
-        qkv_sum[:, :q_cols],
-        qkv_sum[:, q_cols : q_cols + kv_cols],
-        qkv_sum[:, q_cols + kv_cols : q_cols + 2 * kv_cols],
-        o_sum[:, :q_cols],
+        q_grad,
+        k_grad.T,
+        v_grad.T,
+        o_grad,
         gains[1],
-        jnp.concatenate([gate_sum, both_sum[:, :spare]], axis=1),
-        jnp.concatenate([up_sum, both_sum[:, spare:]], axis=1),
-        down_sum.T,
+        gate_grad,
+        up_grad,
+        down_grad.T,
     )
 
 

time: 406 us -> 392 us (0.966)
  waiting for transfers between devices: 23.9 us -> 9.11 us
  Pallas kernels: 325 us -> 339 us
  between operations: 14.2 us -> 0.83 us
    reduce_scatter x1 -> x0, waiting for transfers between devices: 14.6 us -> none  [shards_sequences(): lax.psum_scatter(rest_grads, ('dp', 'seq'), scatter_dimension=0, tiled=True)]
    pallas_call x1, Pallas kernels: 73.1 us -> 86.2 us  [finish(): pl.pallas_call(functools.partial(finish_kernel, dp=dp, seq=seq, kv_width=...]
    unnamed x23 -> x43, local copies, waits for them, and re-layouts: 10.3 us -> 14.5 us
  transfers between devices with their start and end apart: 6 -> 7, of which waited for: 2 -> 1; matrix products, arithmetic and copies ran while one was open for 3% -> 3% of each run, Pallas kernels for 46% -> 51%
where the time goes in v5:
time: 392 us; the launch traced here: 390 us
  Pallas kernels  339 us (86%)
  local copies, waits for them, and re-layouts  19.9 us (5%)
  starting transfers between devices  11.9 us (3%)
  other arithmetic  10.1 us (3%)
  waiting for transfers between devices  9.11 us (2%)
    pallas_call x1, Pallas kernels, finish(): pl.pallas_call(functools.partial(finish_kernel, dp=dp, seq=seq, kv_width=...  86.2 us
    pallas_call x1, Pallas kernels, bring(): pl.pallas_call(functools.partial(bring_kernel, dp=dp, seq=seq), in_specs=...  73.6 us
    pallas_call x1, Pallas kernels, mlp_both(): pl.pallas_call(functools.partial(mlp_kernel, chunk=chunk, dp=dp, seq=seq)...  65.1 us
    pallas_call x1, Pallas kernels, attention_backward(): pl.pallas_call(functools.partial(attend_back_kernel, blocks=tokens // (2...  60.6 us
    pallas_call x1, Pallas kernels, attention_forward(): pl.pallas_call(functools.partial(attend_kernel, blocks=tokens // (2 * spa...  41.8 us
    unnamed x43, local copies, waits for them, and re-layouts  14.5 us
    pallas_call x1, Pallas kernels, project_qkv(): pl.pallas_call(functools.partial(qkv_kernel, heads=heads, kv_heads=kv_hea...  11.2 us
    all_to_all x2, starting transfers between devices, exchange(): return lax.all_to_all(blocks, 'seq', 0, 0, tiled=True)  9.18 us
  transfers between devices with their start and end apart: 7, of which 1 were waited for; matrix products, arithmetic and copies ran while one was open for 3% of the time, Pallas kernels for 51%

profile of v5, /device:TPU:0, one launch (start us, length us, event | category | flops | bytes accessed | tf_op | source)
XLA Modules:
  0.0 390.4 jit_solution(1686460601926061159)
XLA Ops:
  0.6 0.8 copy.30
  1.5 0.8 copy.31
  3.8 0.8 pad_dynamic-update-slice_fusion
  4.6 0.8 slice_dynamic-update-slice_fusion.1
  8.5 1.5 fusion.5.first_ref
  9.9 73.6 %bring.1 = (bf16[8,576,256]{2,1,0:T(8,128)(2,1)}, bf16[32,144,128]{2,1,0:T(8,128)(2,1)}, bf16[8,816,128]{2,1,0:T(8,128)(2,1)}) custom-call(bf16[8,576,256]{2,1,0:T(8,128)(2,1)} %bitcast.14, bf16[1,144,128]{2,1,0:T(8,128)(2,1)} %fusion.5.first_ref, bf16[1,816,128]{2,1,0:T(8,128)(2,1)} %bitcast.18), custom_call_target="tpu_custom_call" | custom-call | tf_op jit(solution)/shard_map/bring/pallas_call | solution.py:770
  84.1 1.1 collective-permute-start.1
  85.8 4.7 %all-to-all-start = ((bf16[8,576,256]{2,1,0:T(8,128)(2,1)}), bf16[8,576,256]{2,1,0:T(8,128)(2,1)S(1)}, u32[]{:S(2)}, u32[]{:S(2)}) async-start(bf16[8,576,256]{2,1,0:T(8,128)(2,1)} %bitcast.4), calls=%async_computation | async-start | bytes 4718592 | tf_op jit(solution)/shard_map/all_to_all | solution.py:1337
  90.5 1.3 sort.17
  91.9 0.9 reshape.59.gain_ref
  93.3 1.8 multiply_sine_fusion
  95.1 11.2 %project_qkv.1 = (bf16[576,2048]{1,0:T(8,128)(2,1)}, bf16[192,2048]{1,0:T(8,128)(2,1)}, bf16[192,2048]{1,0:T(8,128)(2,1)}, bf16[3,2048,64]{2,1,0:T(8,128)(2,1)},...) custom-call(s32[32]{0:T(128)} %fusion.26.where_ref, bf16[8,576,256]{2,1,0:T(8,128)(2,1)} %get-tuple-element.46.x_ref, ...), custom_call_target="tpu_custom_call" | custom-call | flops 4529848320 | bytes 10240000 | tf_op jit(solution)/shard_map/project_qkv/pallas_call | solution.py:841
  106.3 41.8 %attention_forward.1 = (bf16[576,2048]{1,0:T(8,128)(2,1)}, f32[3,8,2048]{2,1,0:T(8,128)}) custom-call(s32[16]{0:T(128)} %get-tuple-element.47.inv_ref, bf16[576,2048]{1,0:T(8,128)(2,1)} %get-tuple-element.49.q_ref, bf16[3,2048,64]{2,1,0:T(8,128)(2,1)} %get-tuple-element.50.k_ref, bf16[192,2048]{1,0:T(8,128)(2,1)} %get-tuple-element.51.v_ref), custom_call_target="tpu_custom_call" | custom-call | flops 38654705664 | bytes 12288000 | tf_op jit(solution)/shard_map/attention_forward/pallas_call | solution.py:470
  148.1 0.9 reshape.60.gain_ref
  149.5 9.1 %collective-permute-done.more_1_ = bf16[8,816,128]{2,1,0:T(8,128)(2,1)} collective-permute-done((bf16[8,816,128]{2,1,0:T(8,128)(2,1)}, bf16[8,816,128]{2,1,0:T(8,128)(2,1)}, u32[]{:S(2)}, u32[]{:S(2)}) %collective-permute-start) | collective-permute-done | bytes 1671200 | tf_op jit(solution)/shard_map/ppermute | solution.py:1022
  158.6 1.4 copy-done
  160.0 65.1 %mlp_both.1 = (bf16[8,576,256]{2,1,0:T(8,128)(2,1)}, f32[8,576,256]{2,1,0:T(8,128)}, bf16[576,2048]{1,0:T(8,128)(2,1)}, bf16[16,432,128]{2,1,0:T(8,128)(2,1)}, b...) custom-call(s32[8]{0:T(128)} %bitcast.22, ...), custom_call_target="tpu_custom_call" | custom-call | flops 36691771392 | bytes 16515072 | tf_op jit(solution)/shard_map/mlp_both/pallas_call | solution.py:1040
  225.2 4.5 %all-to-all-start.1 = ((bf16[8,576,256]{2,1,0:T(8,128)(2,1)}), bf16[8,576,256]{2,1,0:T(8,128)(2,1)S(1)}, u32[]{:S(2)}, u32[]{:S(2)}) async-start(bf16[8,576,256]{2,1,0:T(8,128)(2,1)} %get-tuple-element.55), calls=%async_computation.1 | async-start | bytes 4718592 | tf_op jit(solution)/shard_map/all_to_all | solution.py:1337
  230.2 60.6 %attention_backward.1 = (bf16[576,2048]{1,0:T(8,128)(2,1)}, bf16[192,2048]{1,0:T(8,128)(2,1)}, bf16[192,2048]{1,0:T(8,128)(2,1)}) custom-call(s32[16]{0:T(128)} %get-tuple-element.47.inv_ref, bf16[576,2048]{1,0:T(8,128)(2,1)} %get-tuple-element.49.q_ref, bf16[192,2048]{1,0:T(8,128)(2,1)} %get-tuple-element.57.kt_ref, ...), custom_call_target="tpu_custom_call" | custom-call | flops 77309411328 | bytes 18432000 | tf_op jit(solution)/shard_map/attention_backward/pallas_call | solution.py:613
  290.9 1.1 copy-done.2
  292.6 86.2 %finish.1 = (bf16[8,576,256]{2,1,0:T(8,128)(2,1)}, f32[8,576]{1,0:T(8,128)}, f32[144,72]{1,0:T(8,128)}, f32[24,144]{1,0:T(8,128)}, f32[24,144]{1,0:T(8,128)}, /*...) custom-call(bf16[8,576,256]{2,1,0:T(8,128)(2,1)} %get-tuple-element.46.x_ref, ...), custom_call_target="tpu_custom_call" | custom-call | flops 4529848320 | bytes 14155776 | tf_op jit(solution)/shard_map/finish/pallas_call | solution.py:1297
  378.8 1.4 slice_reduce_fusion
  380.2 4.3 %convert_bitcast_fusion = f32[8,256,576]{1,2,0:T(8,128)} fusion(bf16[8,576,256]{2,1,0:T(8,128)(2,1)} %get-tuple-element.70), kind=kLoop, calls=%fused_computation | loop fusion | flops 1179648 | bytes 7077888 | tf_op jit(solution)/shard_map/transpose | solution.py:1408
  384.6 1.4 copy.49
  (57 shorter events, 12.5 us)
Async XLA Ops:
  8.5 1.5 copy-start.3
  83.6 65.9 %collective-permute-start.2 = (bf16[8,816,128]{2,1,0:T(8,128)(2,1)}, bf16[8,816,128]{2,1,0:T(8,128)(2,1)}, u32[]{:S(2)}, u32[]{:S(2)}) collective-permute-start(bf16[8,816,128]{2,1,0:T(8,128)(2,1)} %get-tuple-element.54.more_0_), channel_id=1, source_target_pairs={{0,24},{8,16},{16,8},{24,0},{1,25},{9,17},{17,9},{25,1},{2,26},{10... | collective-permute-start | bytes 5013512 | tf_op jit(solution)/shard_map/ppermute | solution.py:1022
  84.1 65.4 %collective-permute-start.1 = (bf16[8,816,128]{2,1,0:T(8,128)(2,1)}, bf16[8,816,128]{2,1,0:T(8,128)(2,1)}, u32[]{:S(2)}, u32[]{:S(2)}) collective-permute-start(bf16[8,816,128]{2,1,0:T(8,128)(2,1)} %get-tuple-element.54.more_0_), channel_id=1, source_target_pairs={{0,8},{8,0},{16,24},{24,16},{1,9},{9,1},{17,25},{25,17},{2,10},{10... | collective-permute-start | bytes 5013512 | tf_op jit(solution)/shard_map/ppermute | solution.py:1022
  85.3 73.3 %collective-permute-start = (bf16[8,816,128]{2,1,0:T(8,128)(2,1)}, bf16[8,816,128]{2,1,0:T(8,128)(2,1)}, u32[]{:S(2)}, u32[]{:S(2)}) collective-permute-start(bf16[8,816,128]{2,1,0:T(8,128)(2,1)} %get-tuple-element.54.more_0_), channel_id=1, source_target_pairs={{0,16},{8,24},{16,0},{24,8},{1,17},{9,25},{17,1},{25,9},{2,18},{10... | collective-permute-start | bytes 5013512 | tf_op jit(solution)/shard_map/ppermute | solution.py:1022
  85.8 4.7 %copy-start.13 = (s32[16]{0:T(128)S(1)}, s32[16]{0:T(128)}, u32[]{:S(2)}) copy-start(s32[16]{0:T(128)} %param.13) | copy-start | bytes 196
  85.8 6.1 %copy-start.11 = (bf16[576]{0:T(1024)(128)(2,1)S(1)}, bf16[576]{0:T(1024)(128)(2,1)}, u32[]{:S(2)}) copy-start(bf16[576]{0:T(1024)(128)(2,1)} %param.14) | copy-start | bytes 3460
  85.8 72.8 %all-to-all-start = ((bf16[8,576,256]{2,1,0:T(8,128)(2,1)}), bf16[8,576,256]{2,1,0:T(8,128)(2,1)S(1)}, u32[]{:S(2)}, u32[]{:S(2)}) async-start(bf16[8,576,256]{2,1,0:T(8,128)(2,1)} %bitcast.4), calls=%async_computation | async-start | bytes 4718592 | tf_op jit(solution)/shard_map/all_to_all | solution.py:1337
  106.3 41.8 %copy-start.12 = (bf16[576]{0:T(1024)(128)(2,1)S(1)}, bf16[576]{0:T(1024)(128)(2,1)}, u32[]{:S(2)}) copy-start(bf16[576]{0:T(1024)(128)(2,1)} %param.19) | copy-start | bytes 3460
  158.6 1.4 copy-start
  225.2 159.3 %all-to-all-start.1 = ((bf16[8,576,256]{2,1,0:T(8,128)(2,1)}), bf16[8,576,256]{2,1,0:T(8,128)(2,1)S(1)}, u32[]{:S(2)}, u32[]{:S(2)}) async-start(bf16[8,576,256]{2,1,0:T(8,128)(2,1)} %get-tuple-element.55), calls=%async_computation.1 | async-start | bytes 4718592 | tf_op jit(solution)/shard_map/all_to_all | solution.py:1337
  229.7 61.2 %collective-permute-start.4 = (bf16[16,384,128]{2,1,0:T(8,128)(2,1)}, bf16[16,384,128]{2,1,0:T(8,128)(2,1)S(1)}, u32[]{:S(2)}, u32[]{:S(2)}) collective-permute-start(bf16[16,384,128]{2,1,0:T(8,128)(2,1)} %get-tuple-element.69), channel_id=1, source_target_pairs={{0,8},{8,0},{16,24},{24,16},{1,9},{9,1},{17,25},{25,17},{2,10},{10... | collective-permute-start | bytes 4718600 | tf_op jit(solution)/shard_map/ppermute | solution.py:1397
  229.7 61.2 %collective-permute-start.3 = (bf16[16,432,128]{2,1,0:T(8,128)(2,1)}, bf16[16,432,128]{2,1,0:T(8,128)(2,1)S(1)}, u32[]{:S(2)}, u32[]{:S(2)}) collective-permute-start(bf16[16,432,128]{2,1,0:T(8,128)(2,1)} %get-tuple-element.68), channel_id=1, source_target_pairs={{0,8},{8,0},{16,24},{24,16},{1,9},{9,1},{17,25},{25,17},{2,10},{10... | collective-permute-start | bytes 5308424 | tf_op jit(solution)/shard_map/ppermute | solution.py:1397
  290.8 1.1 copy-start.2
  290.9 1.7 copy-start.1
  384.5 1.5 copy-start.8
  384.5 2.1 copy-start.10
  384.5 2.7 copy-start.9
  384.5 3.3 copy-start.7
  384.5 3.9 %copy-start.5 = (f32[144,192]{1,0:T(8,128)S(1)}, f32[144,192]{1,0:T(8,128)}, u32[]{:S(2)}) copy-start(f32[144,192]{1,0:T(8,128)} %get-tuple-element.102) | copy-start | bytes 331780
  384.5 4.6 %copy-start.4 = (f32[144,192]{1,0:T(8,128)S(1)}, f32[144,192]{1,0:T(8,128)}, u32[]{:S(2)}) copy-start(f32[144,192]{1,0:T(8,128)} %get-tuple-element.103) | copy-start | bytes 331780
  384.5 5.2 %copy-start.6 = (f32[72,384]{1,0:T(8,128)S(1)}, f32[72,384]{1,0:T(8,128)}, u32[]{:S(2)}) copy-start(f32[72,384]{1,0:T(8,128)} %get-tuple-element.78) | copy-start | bytes 331780

commit v6 on v5

--- a/solution.py
+++ b/solution.py
@@ -601,25 +601,29 @@
     lax.fori_loop(0, blocks // 2, two_blocks, 0)
 
 
-def attention_backward(inv, q_t, k_t, k_nat, v_nat, o_t, do_t, logs, cos_t, sin_t, span):
+def attention_backward(inv, q_t, k_t, k_nat, v_nat, o_t, do_t, logs, cos_t, sin_t, span, first, count):
     tokens = q_t.shape[1]
     kv_heads = k_nat.shape[0]
     group = q_t.shape[0] // (kv_heads * HD)
-    pairs = kv_heads * group * tokens * tokens
-    wide_spec = pl.BlockSpec((group * HD, tokens), lambda g, i: (g, 0))
-    kv_spec = pl.BlockSpec((HD, tokens), lambda g, i: (g, 0))
-    nat_spec = pl.BlockSpec((1, tokens, HD), lambda g, i: (g, 0, 0))
+    pairs = count * group * tokens * tokens
+    wide_spec = pl.BlockSpec((group * HD, tokens), lambda g, i: (g + first, 0))
+    kv_spec = pl.BlockSpec((HD, tokens), lambda g, i: (g + first, 0))
+    nat_spec = pl.BlockSpec((1, tokens, HD), lambda g, i: (g + first, 0, 0))
     tab_spec = pl.BlockSpec((HD // 2, tokens), lambda g, i: (0, 0))
     return pl.pallas_call(
         functools.partial(attend_back_kernel, blocks=tokens // (2 * span), span=span, group=group),
         grid_spec=pltpu.PrefetchScalarGridSpec(
             num_scalar_prefetch=1,
-            grid=(kv_heads,),
+            grid=(count,),
             in_specs=[
                 wide_spec, kv_spec, nat_spec, nat_spec, wide_spec, wide_spec,
-                pl.BlockSpec((1, 8, tokens), lambda g, i: (g, 0, 0)), tab_spec, tab_spec,
+                pl.BlockSpec((1, 8, tokens), lambda g, i: (g + first, 0, 0)), tab_spec, tab_spec,
             ],
-            out_specs=[wide_spec, kv_spec, kv_spec],
+            out_specs=[
+                pl.BlockSpec((group * HD, tokens), lambda g, i: (g, 0)),
+                pl.BlockSpec((HD, tokens), lambda g, i: (g, 0)),
+                pl.BlockSpec((HD, tokens), lambda g, i: (g, 0)),
+            ],
             scratch_shapes=[
                 pltpu.VMEM((HD, tokens), F32),
                 pltpu.VMEM((HD, tokens), F32),
@@ -627,9 +631,9 @@
             ],
         ),
         out_shape=[
-            jax.ShapeDtypeStruct(q_t.shape, BF16),
-            jax.ShapeDtypeStruct(k_t.shape, BF16),
-            jax.ShapeDtypeStruct(k_t.shape, BF16),
+            jax.ShapeDtypeStruct((count * group * HD, tokens), BF16),
+            jax.ShapeDtypeStruct((count * HD, tokens), BF16),
+            jax.ShapeDtypeStruct((count * HD, tokens), BF16),
         ],
         compiler_params=pltpu.CompilerParams(vmem_limit_bytes=VMEM_BYTES),
         cost_estimate=pl.CostEstimate(
@@ -702,13 +706,14 @@
     return peers + [(flip(my_dp, [b]), my_seq) for b in bits_of(dp)]
 
 
-def bring_kernel(x_ref, first_ref, second_ref, out_ref, all_one_ref, all_two_ref,
+def bring_kernel(x_ref, first_ref, second_ref, third_ref, out_ref, all_first, all_second, all_third,
                  local_sem, x_send, x_recv, w_send, w_recv, *, dp, seq):
     my_dp, my_seq = lax.axis_index("dp"), lax.axis_index("seq")
-    orders = all_stages(dp, seq), seq_stages(seq)
+    orders = all_stages(dp, seq), seq_stages(seq), seq_stages(seq)
+    chains = range(len(orders))
     greet(all_peers(my_dp, my_seq, dp, seq))
-    shards_in = (first_ref, second_ref)
-    gathered = (all_one_ref, all_two_ref)
+    shards_in = first_ref, second_ref, third_ref
+    gathered = all_first, all_second, all_third
 
     def weight_copy(chain, stage):
         held = 1 << stage
@@ -722,13 +727,13 @@
             device_id_type=pl.DeviceIdType.MESH,
         )
 
-    copies = [[weight_copy(c, s) for s in range(len(orders[c]))] for c in range(2)]
-    for c in range(2):
+    copies = [[weight_copy(c, s) for s in range(len(orders[c]))] for c in chains]
+    for c in chains:
         copies[c][0].start()
     own = [
-        pltpu.make_async_copy(shards_in[c], gathered[c].at[pl.ds(0, 1)], local_sem.at[c]) for c in range(2)
+        pltpu.make_async_copy(shards_in[c], gathered[c].at[pl.ds(0, 1)], local_sem.at[c]) for c in chains
     ]
-    own.append(pltpu.make_async_copy(x_ref.at[my_seq], out_ref.at[my_seq], local_sem.at[2]))
+    own.append(pltpu.make_async_copy(x_ref.at[my_seq], out_ref.at[my_seq], local_sem.at[len(orders)]))
     for copy in own:
         copy.start()
     moves = []
@@ -744,50 +749,51 @@
                 device_id_type=pl.DeviceIdType.MESH,
             )
         )
-    for c in range(2):
+    for c in chains:
         own[c].wait()
     for stage in range(1, len(orders[0])):
-        for c in range(2):
+        for c in chains:
             if stage < len(orders[c]):
                 copies[c][stage - 1].wait_recv()
                 copies[c][stage].start()
         if stage == 1:
             for move in moves:
                 move.start()
-    for c in range(2):
+    for c in chains:
         copies[c][-1].wait_recv()
         for copy in copies[c]:
             copy.wait_send()
     for move in moves:
         move.wait()
-    own[2].wait()
-
-
-def bring(x, first, second):
+    own[-1].wait()
+
+
+def bring(x, first, second, third):
     dp, seq = lax.axis_size("dp"), lax.axis_size("seq")
     stages = len(all_stages(dp, seq))
     hbm = pl.BlockSpec(memory_space=pl.ANY)
     return pl.pallas_call(
         functools.partial(bring_kernel, dp=dp, seq=seq),
-        in_specs=[hbm] * 3,
-        out_specs=[hbm] * 3,
+        in_specs=[hbm] * 4,
+        out_specs=[hbm] * 4,
         out_shape=[
             jax.ShapeDtypeStruct(x.shape, x.dtype),
             jax.ShapeDtypeStruct((dp * seq, *first.shape[1:]), first.dtype),
             jax.ShapeDtypeStruct((seq, *second.shape[1:]), second.dtype),
+            jax.ShapeDtypeStruct((seq, *third.shape[1:]), third.dtype),
         ],
         scratch_shapes=[
-            pltpu.SemaphoreType.DMA((3,)),
+            pltpu.SemaphoreType.DMA((4,)),
             pltpu.SemaphoreType.DMA((seq - 1,)),
             pltpu.SemaphoreType.DMA((seq - 1,)),
-            pltpu.SemaphoreType.DMA((2, stages)),
-            pltpu.SemaphoreType.DMA((2, stages)),
+            pltpu.SemaphoreType.DMA((3, stages)),
+            pltpu.SemaphoreType.DMA((3, stages)),
         ],
         compiler_params=pltpu.CompilerParams(
             collective_id=1, has_side_effects=True, vmem_limit_bytes=VMEM_BYTES
         ),
         name="bring",
-    )(x, first, second)
+    )(x, first, second, third)
 
 
 def qkv_kernel(where_ref, x_ref, gain_ref, packed_ref, cos_ref, sin_ref,
@@ -879,11 +885,11 @@
 def mlp_kernel(
     where_ref, x_ref, mixed_ref, dy_ref, gain_ref, *more, chunk, dp, seq,
 ):
-    packs = more[:dp]
-    out_ref, dmid_ref, dmixed_ref = more[dp : dp + 3]
-    one_refs, two_refs, gain_grad_ref = more[dp + 3 : dp + 5], more[dp + 5 : dp + 7], more[dp + 7]
+    packs, more = more[: 2 * dp], more[2 * dp :]
+    out_ref, dmid_ref, dmixed_ref = more[:3]
+    one_refs, two_refs, gain_grad_ref = more[3:5], more[5:7], more[7]
     (o_w, o_t, gate_w, gate_t, up_w, up_t, down_w, down_t, o_sum, gate_sum, up_sum, down_sum, gain_sum,
-     pack, pack_sem) = more[dp + 8 :]
+     pack, pack_sem) = more[8:]
     step, steps = pl.program_id(0), pl.num_programs(0)
     width, ff = gate_w.shape
     lanes = pack.shape[3]
@@ -896,12 +902,14 @@
     def _():
         for total in (o_sum, gate_sum, up_sum, down_sum, gain_sum):
             total[...] = jnp.zeros_like(total)
-        fetches = [
-            pltpu.make_async_copy(
-                packs[i], pack.at[flip(lax.axis_index("dp"), row_bits(i, dp))], pack_sem.at[i]
-            )
-            for i in range(dp)
-        ]
+        fetches = []
+        for i in range(dp):
+            owner = flip(lax.axis_index("dp"), row_bits(i, dp))
+            first = 0
+            for source, sem in ((packs[2 * i], pack_sem.at[2 * i]), (packs[2 * i + 1], pack_sem.at[2 * i + 1])):
+                span = pl.ds(first, source.shape[1])
+                fetches.append(pltpu.make_async_copy(source, pack.at[owner, :, span, :], sem))
+                first += source.shape[1]
         for fetch in fetches:
             fetch.start()
         for fetch in fetches:
@@ -1015,19 +1023,15 @@
     return [b for i, b in enumerate(reversed(bits_of(dp))) if (at >> i) & 1]
 
 
-def gather_rows(array, dp):
-    held = [array]
-    for at in range(1, dp):
-        mask = sum(row_bits(at, dp))
-        held.append(lax.ppermute(array, "dp", [(i, i ^ mask) for i in range(dp)]))
-    return held
+def over_rows(array, mask):
+    return lax.ppermute(array, "dp", [(i, i ^ mask) for i in range(lax.axis_size("dp"))])
 
 
 def mlp_both(where, x, mixed, dy, gain, packs, ff, batch=2, chunk=512):
     blocks, width, block = x.shape
     tokens = blocks * block
     dp, seq = lax.axis_size("dp"), lax.axis_size("seq")
-    grad_rows, lanes = packs[0].shape[1:]
+    grad_rows, lanes = packs[0].shape[1] + packs[1].shape[1], packs[0].shape[2]
     first_rows = 3 * (width // dp)
     one = dp * seq // 2, first_rows, lanes
     two = dp * seq // 2, grad_rows - first_rows, lanes
@@ -1042,7 +1046,7 @@
         grid_spec=pltpu.PrefetchScalarGridSpec(
             num_scalar_prefetch=1,
             grid=(blocks // batch,),
-            in_specs=[tok, col, tok, once((width, 1))] + [hbm] * dp,
+            in_specs=[tok, col, tok, once((width, 1))] + [hbm] * (2 * dp),
             out_specs=[tok, tok, col, once(one), once(one), once(two), once(two), once((1, width))],
             scratch_shapes=[
                 pltpu.VMEM((width, width), BF16),
@@ -1058,8 +1062,8 @@
                 pltpu.VMEM((ff, width), F32),
                 pltpu.VMEM((width, ff), F32),
                 pltpu.VMEM((width, lanes), F32),
-                pltpu.VMEM((dp, *packs[0].shape), BF16),
-                pltpu.SemaphoreType.DMA((dp,)),
+                pltpu.VMEM((dp, packs[0].shape[0], grad_rows, lanes), BF16),
+                pltpu.SemaphoreType.DMA((2 * dp,)),
             ],
         ),
         out_shape=[
@@ -1098,9 +1102,8 @@
 
 
 def finish_kernel(
-    x_ref, dmid_ref, dq_ref, dk_ref, dv_ref, gain_ref, w_t_ref, other_gain_ref,
-    keep_one, keep_two, came_one, came_two,
-    out_ref, gains_ref, q_ref, k_ref, v_ref, o_ref, gate_ref, up_ref, down_ref,
+    x_ref, dmid_ref, dq_one, dq_two, dk_one, dk_two, dv_one, dv_two, gain_ref, w_t_ref, other_gain_ref,
+    keep_one, keep_two, came_one, came_two, out_ref, gains_ref, qkv_ref, one_ref, two_ref,
     w_nat, w_sum, gain_sum, din, packed, landed, one, one_came, one_landed, two, two_came, two_landed,
     gain_held, gain_landed,
     own_sem, d_send, d_recv, r_send, r_recv, g_send, g_recv, fetch_sem, *, dp, seq, kv_width,
@@ -1111,7 +1114,7 @@
     lanes = packed.shape[2]
     rows = width // dp
     q_cols, kv_cols = width // seq, kv_width // seq
-    orders = [all_stages(dp, seq), *rest_chains(dp, seq)]
+    orders = [all_stages(dp, seq), *[chain[:-1] for chain in rest_chains(dp, seq)]]
     held = [packed, one, two]
     arrived = [landed, one_landed, two_landed]
     fetches = [
@@ -1148,6 +1151,11 @@
         for fetch in fetches:
             fetch.start()
         greet(all_peers(my_dp, my_seq, dp, seq))
+        for fetch in fetches:
+            fetch.wait()
+        for chain, came in ((1, one_came), (2, two_came)):
+            add_blocks(held[chain], came, came.shape[0])
+            halve(chain, 0).start()
         w_sum[...] = jnp.zeros_like(w_sum)
         gain_sum[...] = jnp.zeros_like(gain_sum)
         w_nat[...] = w_t_ref[...].T
@@ -1157,7 +1165,8 @@
     rstd = lax.rsqrt(jnp.mean(x * x, axis=0, keepdims=True) + eps_norm)
     scaled_x = x * rstd
     normed = (scaled_x * gain).astype(BF16)
-    dlin = jnp.concatenate([dq_ref[...], dk_ref[...], dv_ref[...]], axis=0)
+    dlins = dq_one, dq_two, dk_one, dk_two, dv_one, dv_two
+    dlin = jnp.concatenate([ref[...] for ref in dlins], axis=0)
     w_sum[...] += dot(dlin, normed, 1, 1)
     dnormed = dot(w_nat[...], dlin, 1, 0)
     product = dnormed * scaled_x
@@ -1181,20 +1190,15 @@
             device_id_type=pl.DeviceIdType.MESH,
         )
 
-    for back in range(1, steps):
-
-        @pl.when(step == steps - 1 - back)
-        def _():
-            move(2 * back).start()
-            move(2 * back + 1).start()
-
     @pl.when(step == 0)
     def _():
-        for fetch in fetches:
-            fetch.wait()
-        for chain, came in ((1, one_came), (2, two_came)):
-            add_blocks(held[chain], came, came.shape[0])
-            halve(chain, 0).start()
+        for away in range(seq - 2, seq):
+            move(away).start()
+
+    @pl.when(step == max(steps - 2, 0))
+    def _():
+        for chain in (1, 2):
+            take(chain, 0)
 
     @pl.when(step == steps - 1)
     def _():
@@ -1239,24 +1243,18 @@
             if turn + 1 < turns:
                 gain_copies[turn + 1].start()
             take(0, turn)
-            if turn > 0:
+            if turn == turns - 3:
                 for chain in (1, 2):
-                    take(chain, turn - 1)
+                    take(chain, 1)
+                for away in range(seq // 2, seq - 2):
+                    move(away).start()
+            if turn == turns - 2:
+                for chain in (1, 2):
+                    take(chain, 2)
+                for away in range(2, seq // 2):
+                    move(away).start()
         gains_ref[...] = gain_held[turns]
-        qkv = result(0)
-        q_ref[...] = qkv[:, :q_cols]
-        turned = qkv.T
-        k_ref[...] = turned[q_cols : q_cols + kv_cols]
-        v_ref[...] = turned[q_cols + kv_cols : q_cols + 2 * kv_cols]
-        first, second = result(1), result(2)
-        spare = gate_ref.shape[1] - lanes
-        padded = -(-q_cols // 16) * 16
-        o_ref[...] = first[:rows, :q_cols]
-        gate_ref[...] = jnp.concatenate([first[rows : 2 * rows], second[:rows, :spare]], axis=1)
-        up_ref[...] = jnp.concatenate([first[2 * rows :], second[:rows, spare : 2 * spare]], axis=1)
-        for t in range(down_ref.shape[1] // lanes):
-            at = rows + padded * t
-            down_ref[:, lanes * t : lanes * (t + 1)] = second[at : at + q_cols]
+        qkv_ref[...], one_ref[...], two_ref[...] = result(0), result(1), result(2)
         for copy in gain_copies:
             copy.wait_send()
         for chain in range(3):
@@ -1267,11 +1265,11 @@
         own.wait()
 
 
-def finish(x, dmid, dq_t, dk_t, dv_t, gain, w_t, other_gain, keep_one, keep_two, came_one, came_two, ff):
+def finish(x, dmid, dlins, gain, w_t, other_gain, keep_one, keep_two, came_one, came_two):
     blocks, width, block = x.shape
     tokens = blocks * block
     feats = w_t.shape[0]
-    kv_width = dk_t.shape[0]
+    kv_width = (feats - width) // 2
     lanes = keep_one.shape[2]
     dp, seq = lax.axis_size("dp"), lax.axis_size("seq")
     rows = width // dp
@@ -1284,21 +1282,12 @@
     col = lambda rows: pl.BlockSpec((rows, 2 * block), lambda i: (0, pair(i)))
     once = lambda shape: pl.BlockSpec(shape, lambda i: (0,) * len(shape), pipeline_mode=pl.Buffered(1))
     hbm = pl.BlockSpec(memory_space=pl.ANY)
-    small = [
-        (8, width),
-        (rows, width // seq),
-        (kv_width // seq, rows),
-        (kv_width // seq, rows),
-        (rows, width // seq),
-        (rows, ff // seq),
-        (rows, ff // seq),
-        (width // seq, ff // dp),
-    ]
+    small = [(8, width), (rows, lanes), keep_one.shape[1:], keep_two.shape[1:]]
     return pl.pallas_call(
         functools.partial(finish_kernel, dp=dp, seq=seq, kv_width=kv_width),
         grid=(blocks // 2,),
         in_specs=[
-            tok, tok, col(dq_t.shape[0]), col(kv_width), col(kv_width),
+            tok, tok, *[col(d.shape[0]) for d in dlins],
             once((width, 1)), once((feats, width)), once((1, width)), hbm, hbm, hbm, hbm,
         ],
         out_specs=[hbm] + [once(shape) for shape in small],
@@ -1330,7 +1319,63 @@
             flops=4 * tokens * width * feats, bytes_accessed=tokens * width * 12, transcendentals=0
         ),
         name="finish",
-    )(x, dmid, dq_t, dk_t, dv_t, gain, w_t, other_gain, keep_one, keep_two, came_one, came_two)
+    )(x, dmid, *dlins, gain, w_t, other_gain, keep_one, keep_two, came_one, came_two)
+
+
+def deliver_kernel(
+    din_ref, gains_ref, qkv_ref, one_ref, two_ref,
+    out_ref, gain_one, gain_two, q_ref, k_ref, v_ref, o_ref, gate_ref, up_ref, down_ref,
+):
+    out_ref[...] = din_ref[...].astype(F32)
+
+    @pl.when(pl.program_id(0) == 0)
+    def _():
+        rows, q_cols = q_ref.shape
+        kv_cols, lanes = k_ref.shape[0], qkv_ref.shape[1]
+        spare = gate_ref.shape[1] - lanes
+        padded = -(-q_cols // 16) * 16
+        gain_one[...] = gains_ref[0]
+        gain_two[...] = gains_ref[1]
+        qkv = qkv_ref[...]
+        turned = qkv.T
+        q_ref[...] = qkv[:, :q_cols]
+        k_ref[...] = turned[q_cols : q_cols + kv_cols]
+        v_ref[...] = turned[q_cols + kv_cols : q_cols + 2 * kv_cols]
+        o_ref[...] = one_ref[:rows, :q_cols]
+        both = two_ref[:rows]
+        gate_ref[...] = jnp.concatenate([one_ref[rows : 2 * rows], both[:, :spare]], axis=1)
+        up_ref[...] = jnp.concatenate([one_ref[2 * rows : 3 * rows], both[:, spare : 2 * spare]], axis=1)
+        for t in range(down_ref.shape[1] // lanes):
+            at = rows + padded * t
+            down_ref[:, lanes * t : lanes * (t + 1)] = two_ref[at : at + q_cols]
+
+
+def deliver(din, gains, qkv, one, two, kv_cols, ff):
+    blocks, width, block = din.shape
+    rows = qkv.shape[0]
+    dp, seq = lax.axis_size("dp"), lax.axis_size("seq")
+    tok = pl.BlockSpec((2, width, block), lambda i: (i, 0, 0))
+    once = lambda shape: pl.BlockSpec(shape, lambda i: (0,) * len(shape), pipeline_mode=pl.Buffered(1))
+    small = [
+        (width,),
+        (width,),
+        (rows, width // seq),
+        (kv_cols, rows),
+        (kv_cols, rows),
+        (rows, width // seq),
+        (rows, ff // seq),
+        (rows, ff // seq),
+        (width // seq, ff // dp),
+    ]
+    return pl.pallas_call(
+        deliver_kernel,
+        grid=(blocks // 2,),
+        in_specs=[tok] + [once(a.shape) for a in (gains, qkv, one, two)],
+        out_specs=[tok] + [once(shape) for shape in small],
+        out_shape=[jax.ShapeDtypeStruct(shape, F32) for shape in [din.shape] + small],
+        compiler_params=pltpu.CompilerParams(vmem_limit_bytes=VMEM_BYTES),
+        name="deliver",
+    )(din, gains, qkv, one, two)
 
 
 def exchange(blocks):
@@ -1370,10 +1415,15 @@
         + [down_turned[:, c : c + lanes] for c in range(0, ff_rows, lanes)],
         axis=0,
     )
-    x, first_all, second_row = bring(hidden_in.transpose(0, 2, 1), first[None], second[None])
+    at = second.shape[0] * 5 // 8 // 16 * 16
+    x, first_all, straight, hopping = bring(
+        hidden_in.transpose(0, 2, 1), first[None], second[None, :at], second[None, at:]
+    )
     out_grad, x = lax.optimization_barrier((out_grad, x))
+    masks = [sum(row_bits(i, dp)) for i in range(dp)]
+    straight_all = [straight] + [over_rows(straight, m) for m in masks[1:]]
+    hopping_all = [hopping if m == 0 else over_rows(hopping, m) if m & (m - 1) == 0 else None for m in masks]
     dy = exchange(out_grad.transpose(0, 2, 1))
-    second_all = gather_rows(second_row, dp)
 
     my_dp, my_seq = lax.axis_index("dp"), lax.axis_index("seq")
     where_first = arrival_order(all_stages(dp, seq), dp, seq, my_dp, my_seq)
@@ -1390,31 +1440,56 @@
         where_first, x, gain_one, first_all, cos_t, sin_t, heads, kv_heads, rows
     )
     o_t, logs = attention_forward(inv, q_t, k_nat, v_t, span)
+    hopping_all, o_t = lax.optimization_barrier((hopping_all, o_t))
+    for i, mask in enumerate(masks):
+        if hopping_all[i] is None:
+            low = mask & -mask
+            hopping_all[i] = over_rows(hopping_all[masks.index(mask - low)], low)
+    packs = [part for pair in zip(straight_all, hopping_all) for part in pair]
     out, dmid, do_t, keep_one, give_one, keep_two, give_two, gain_two_term = mlp_both(
-        where_second, x, o_t, dy, gain_two, second_all, ff
+        where_second, x, o_t, dy, gain_two, packs, ff
     )
-    sibling = [(i, i ^ 1) for i in range(dp)]
-    came_one, came_two = lax.ppermute(give_one, "dp", sibling), lax.ppermute(give_two, "dp", sibling)
+    came_one, came_two = over_rows(give_one, 1), over_rows(give_two, 1)
     hidden_out = exchange(out).transpose(0, 2, 1)
 
-    dq_t, dk_t, dv_t = attention_backward(
-        inv, q_t, k_t, k_nat, v_nat, o_t, do_t, logs, cos_t, sin_t, span
+    def back(queries, *heads):
+        return attention_backward(
+            inv, queries, k_t, k_nat, v_nat, o_t, do_t, logs, cos_t, sin_t, span, *heads
+        )
+
+    parts = [back(q_t, 0, 1)]
+    came_one, came_two, parts[0] = lax.optimization_barrier((came_one, came_two, parts[0]))
+    half = dp * seq // 4
+    add = lambda a, b: (a.astype(F32) + b.astype(F32)).astype(BF16)
+    sums = [
+        (add(keep[:half], came[:half]), add(keep[half:], came[half:]))
+        for keep, came in ((keep_one, came_one), (keep_two, came_two))
+    ]
+    sums, q_t = lax.optimization_barrier((sums, q_t))
+    crossed = [
+        lax.ppermute(high, axis, [(i, i ^ bit) for i in range(lax.axis_size(axis))])
+        for (_, high), (axis, bit) in zip(sums, [chain[-1] for chain in rest_chains(dp, seq)])
+    ]
+    parts.append(back(q_t, 1, kv_heads - 1))
+    dlins = [part[i] for i in range(3) for part in parts]
+    din, gains, qkv_sum, one_sum, two_sum = finish(
+        x, dmid, dlins, gain_one, w_t, gain_two_term, sums[0][0], sums[1][0], *crossed
     )
-    din, gains, q_grad, k_grad, v_grad, o_grad, gate_grad, up_grad, down_grad = finish(
-        x, dmid, dq_t, dk_t, dv_t, gain_one, w_t, gain_two_term, keep_one, keep_two, came_one, came_two, ff
+    grad_in, gain_one_sum, gain_two_sum, q_sum, k_sum, v_sum, o_sum, gate_sum, up_sum, down_sum = deliver(
+        din, gains, qkv_sum, one_sum, two_sum, kv_cols, ff
     )
     return (
         hidden_out,
-        din.astype(F32).transpose(0, 2, 1),
-        gains[0],
-        q_grad,
-        k_grad.T,
-        v_grad.T,
-        o_grad,
-        gains[1],
-        gate_grad,
-        up_grad,
-        down_grad.T,
+        grad_in.transpose(0, 2, 1),
+        gain_one_sum,
+        q_sum,
+        k_sum.T,
+        v_sum.T,
+        o_sum,
+        gain_two_sum,
+        gate_sum,
+        up_sum,
+        down_sum.T,
     )
 
 

time: 392 us -> 378 us (0.964)
  local copies, waits for them, and re-layouts: 19.9 us -> 11.2 us
  waiting for transfers between devices: 9.11 us -> 1.05 us
  starting transfers between devices: 11.9 us -> 17.6 us
  Pallas kernels: 339 us -> 335 us
    unnamed x43 -> x21, local copies, waits for them, and re-layouts: 14.5 us -> 5.64 us
    pallas_call x1, Pallas kernels: 86.2 us -> 77.4 us  [finish(): pl.pallas_call(functools.partial(finish_kernel, dp=dp, seq=seq, kv_width=...]
    ppermute x5 -> x10, waiting for transfers between devices: 9.11 us -> 1.04 us  [the longest x8 1.04 us: over_rows(): lax.ppermute(array, 'dp', [(i, i ^ mask) for i in range(lax.axis_size('dp...]
    pallas_call x0 -> x1, Pallas kernels: none -> 4.85 us  [deliver(): pl.pallas_call(deliver_kernel, grid=(blocks // 2,), in_specs=[tok] + [onc...]
    transpose x1 -> x0, other arithmetic: 4.28 us -> none  [shards_sequences(): din.astype(F32).transpose(0, 2, 1)]
    ppermute x5 -> x10, starting transfers between devices: 2.71 us -> 6.91 us  [the longest x8 4.34 us: over_rows(): lax.ppermute(array, 'dp', [(i, i ^ mask) for i in range(lax.axis_size('dp...]
    convert_element_type x0 -> x2, other arithmetic: none -> 4.08 us  [shards_sequences(): add = lambda a, b: (a.astype(F32) + b.astype(F32)).astype(BF16)]
    pallas_call x1 -> x2, Pallas kernels: 60.6 us -> 64.2 us  [attention_backward(): pl.pallas_call(functools.partial(attend_back_kernel, blocks=tokens // (2...]
  transfers between devices with their start and end apart: 7 -> 12, of which waited for: 1 -> 1; matrix products, arithmetic and copies ran while one was open for 3% -> 3% of each run, Pallas kernels for 51% -> 53%
where the time goes in v6:
time: 378 us; the launch traced here: 377 us
  Pallas kernels  335 us (89%)
  starting transfers between devices  17.6 us (5%)
  other arithmetic  12 us (3%)
  local copies, waits for them, and re-layouts  11.2 us (3%)
    pallas_call x1, Pallas kernels, finish(): pl.pallas_call(functools.partial(finish_kernel, dp=dp, seq=seq, kv_width=...  77.4 us
    pallas_call x1, Pallas kernels, bring(): pl.pallas_call(functools.partial(bring_kernel, dp=dp, seq=seq), in_specs=...  70.2 us
    pallas_call x1, Pallas kernels, mlp_both(): pl.pallas_call(functools.partial(mlp_kernel, chunk=chunk, dp=dp, seq=seq)...  65 us
    pallas_call x2, Pallas kernels, attention_backward(): pl.pallas_call(functools.partial(attend_back_kernel, blocks=tokens // (2...  64.2 us
    pallas_call x1, Pallas kernels, attention_forward(): pl.pallas_call(functools.partial(attend_kernel, blocks=tokens // (2 * spa...  41.7 us
    pallas_call x1, Pallas kernels, project_qkv(): pl.pallas_call(functools.partial(qkv_kernel, heads=heads, kv_heads=kv_hea...  11.2 us
    all_to_all x2, starting transfers between devices, exchange(): return lax.all_to_all(blocks, 'seq', 0, 0, tiled=True)  10.7 us
  transfers between devices with their start and end apart: 12, of which 1 were waited for; matrix products, arithmetic and copies ran while one was open for 3% of the time, Pallas kernels for 53%

profile of v6, /device:TPU:0, one launch (start us, length us, event | category | flops | bytes accessed | tf_op | source)
XLA Modules:
  0.0 377.3 jit_solution(9077671534982368346)
XLA Ops:
  6.1 1.5 fusion.11.first_ref
  7.6 1.5 fusion.4.second_ref
  9.8 70.2 %bring.1 = (bf16[8,576,256]{2,1,0:T(8,128)(2,1)}, bf16[32,144,128]{2,1,0:T(8,128)(2,1)}, bf16[8,496,128]{2,1,0:T(8,128)(2,1)}, bf16[8,320,128]{2,1,0:T(8,128)(2,1)}) custom-call(bf16[8,576,256]{2,1,0:T(8,128)(2,1)} %bitcast.16, bf16[1,144,128]{2,1,0:T(8,128)(2,1)} %fusion.11.first_ref, bf16[1,496,128]{2,1,0:T(8,128)(2,1)} %fusion.4.second_ref, ...), custom_call_target="tpu_custom_call" | custom-call | tf_op jit(solution)/shard_map/bring/pallas_call | solution.py:775
  80.2 1.6 collective-permute-start
  82.4 1.5 collective-permute-start.2
  83.9 4.7 %all-to-all-start = ((bf16[8,576,256]{2,1,0:T(8,128)(2,1)}), bf16[8,576,256]{2,1,0:T(8,128)(2,1)S(1)}, u32[]{:S(2)}, u32[]{:S(2)}) async-start(bf16[8,576,256]{2,1,0:T(8,128)(2,1)} %bitcast.5), calls=%async_computation | async-start | bytes 4718592 | tf_op jit(solution)/shard_map/all_to_all | solution.py:1382
  88.6 1.3 sort.17
  89.9 0.9 reshape.59.gain_ref
  91.3 1.8 multiply_sine_fusion
  93.1 11.2 %project_qkv.1 = (bf16[576,2048]{1,0:T(8,128)(2,1)}, bf16[192,2048]{1,0:T(8,128)(2,1)}, bf16[192,2048]{1,0:T(8,128)(2,1)}, bf16[3,2048,64]{2,1,0:T(8,128)(2,1)},...) custom-call(s32[32]{0:T(128)} %fusion.29.where_ref, bf16[8,576,256]{2,1,0:T(8,128)(2,1)} %get-tuple-element.70.x_ref, ...), custom_call_target="tpu_custom_call" | custom-call | flops 4529848320 | bytes 10240000 | tf_op jit(solution)/shard_map/project_qkv/pallas_call | solution.py:847
  104.4 41.7 %attention_forward.1 = (bf16[576,2048]{1,0:T(8,128)(2,1)}, f32[3,8,2048]{2,1,0:T(8,128)}) custom-call(s32[16]{0:T(128)} %get-tuple-element.72.inv_ref, bf16[576,2048]{1,0:T(8,128)(2,1)} %get-tuple-element.100.q_ref, bf16[3,2048,64]{2,1,0:T(8,128)(2,1)} %get-tuple-element.75.k_ref, bf16[192,2048]{1,0:T(8,128)(2,1)} %get-tuple-element.76.v_ref), custom_call_target="tpu_custom_call" | custom-call | flops 38654705664 | bytes 12288000 | tf_op jit(solution)/shard_map/attention_forward/pallas_call | solution.py:470
  147.5 1.0 collective-permute-done.5.more_7_
  148.6 1.4 copy-done
  150.0 65.0 %mlp_both.1 = (bf16[8,576,256]{2,1,0:T(8,128)(2,1)}, f32[8,576,256]{2,1,0:T(8,128)}, bf16[576,2048]{1,0:T(8,128)(2,1)}, bf16[16,432,128]{2,1,0:T(8,128)(2,1)}, b...) custom-call(s32[8]{0:T(128)} %bitcast.22, ...), custom_call_target="tpu_custom_call" | custom-call | flops 36691771392 | bytes 16515072 | tf_op jit(solution)/shard_map/mlp_both/pallas_call | solution.py:1044
  215.0 6.0 %all-to-all-start.1 = ((bf16[8,576,256]{2,1,0:T(8,128)(2,1)}), bf16[8,576,256]{2,1,0:T(8,128)(2,1)S(1)}, u32[]{:S(2)}, u32[]{:S(2)}) async-start(bf16[8,576,256]{2,1,0:T(8,128)(2,1)} %get-tuple-element.84), calls=%async_computation.1 | async-start | bytes 4718592 | tf_op jit(solution)/shard_map/all_to_all | solution.py:1382
  221.5 22.5 %attention_backward.2 = (bf16[192,2048]{1,0:T(8,128)(2,1)}, bf16[64,2048]{1,0:T(8,128)(2,1)}, bf16[64,2048]{1,0:T(8,128)(2,1)}) custom-call(s32[16]{0:T(128)} %get-tuple-element.72.inv_ref, bf16[576,2048]{1,0:T(8,128)(2,1)} %get-tuple-element.100.q_ref, bf16[192,2048]{1,0:T(8,128)(2,1)} %get-tuple-element.88.kt_ref, ...), custom_call_target="tpu_custom_call" | custom-call | flops 25769803776 | bytes 18432000 | tf_op jit(solution)/shard_map/attention_backward/pallas_call | solution.py:613
  244.1 1.4 add_convert_fusion
  245.5 2.7 add_convert_fusion.2
  248.2 2.0 collective-permute-start.9
  250.8 41.7 %attention_backward.3 = (bf16[384,2048]{1,0:T(8,128)(2,1)}, bf16[128,2048]{1,0:T(8,128)(2,1)}, bf16[128,2048]{1,0:T(8,128)(2,1)}) custom-call(s32[16]{0:T(128)} %get-tuple-element.72.inv_ref, bf16[576,2048]{1,0:T(8,128)(2,1)} %get-tuple-element.100.q_ref, bf16[192,2048]{1,0:T(8,128)(2,1)} %get-tuple-element.88.kt_ref, ...), custom_call_target="tpu_custom_call" | custom-call | flops 51539607552 | bytes 18432000 | tf_op jit(solution)/shard_map/attention_backward/pallas_call | solution.py:613
  292.5 0.8 copy-done.8
  293.6 77.4 %finish.1 = (bf16[8,576,256]{2,1,0:T(8,128)(2,1)}, f32[8,576]{1,0:T(8,128)}, f32[144,128]{1,0:T(8,128)}, f32[432,128]{1,0:T(8,128)}, f32[384,128]{1,0:T(8,128)}) custom-call(bf16[8,576,256]{2,1,0:T(8,128)(2,1)} %get-tuple-element.70.x_ref, f32[8,576,256]{2,1,0:T(8,128)} %get-tuple-element.85.dmid_ref, bf16[192,2048]{1,0:T(8,128)(2,1)} %get-tuple-element.95.dq_one, ...), custom_call_target="tpu_custom_call" | custom-call | flops 4529848320 | bytes 14155776 | tf_op jit(solution)/shard_map/finish/pallas_call | solution.py:1286
  371.0 4.9 %deliver.1 = (f32[8,576,256]{2,1,0:T(8,128)}, f32[576]{0:T(1024)}, f32[576]{0:T(1024)}, f32[144,72]{1,0:T(8,128)}, f32[24,144]{1,0:T(8,128)}, /*index=5*/f32[24,...) custom-call(bf16[8,576,256]{2,1,0:T(8,128)(2,1)} %get-tuple-element.112.din_ref, ...), custom_call_target="tpu_custom_call" | custom-call | tf_op jit(solution)/shard_map/deliver/pallas_call | solution.py:1370
  375.9 1.4 copy.36
  (50 shorter events, 10.4 us)
Async XLA Ops:
  80.1 66.0 %collective-permute-start.1 = (bf16[8,320,128]{2,1,0:T(8,128)(2,1)}, bf16[8,320,128]{2,1,0:T(8,128)(2,1)}, u32[]{:S(2)}, u32[]{:S(2)}) collective-permute-start(bf16[8,320,128]{2,1,0:T(8,128)(2,1)} %get-tuple-element.81.more_1_), channel_id=1, source_target_pairs={{0,8},{8,0},{16,24},{24,16},{1,9},{9,1},{17,25},{25,17},{2,10},{10... | collective-permute-start | bytes 1966088 | tf_op jit(solution)/shard_map/ppermute | solution.py:1027
  80.2 65.9 %collective-permute-start = (bf16[8,320,128]{2,1,0:T(8,128)(2,1)}, bf16[8,320,128]{2,1,0:T(8,128)(2,1)}, u32[]{:S(2)}, u32[]{:S(2)}) collective-permute-start(bf16[8,320,128]{2,1,0:T(8,128)(2,1)} %get-tuple-element.81.more_1_), channel_id=1, source_target_pairs={{0,16},{8,24},{16,0},{24,8},{1,17},{9,25},{17,1},{25,9},{2,18},{10... | collective-permute-start | bytes 1966088 | tf_op jit(solution)/shard_map/ppermute | solution.py:1027
  81.7 65.8 %collective-permute-start.4 = (bf16[8,496,128]{2,1,0:T(8,128)(2,1)}, bf16[8,496,128]{2,1,0:T(8,128)(2,1)S(1)}, u32[]{:S(2)}, u32[]{:S(2)}) collective-permute-start(bf16[8,496,128]{2,1,0:T(8,128)(2,1)} %get-tuple-element.80.more_0_), channel_id=1, source_target_pairs={{0,24},{8,16},{16,8},{24,0},{1,25},{9,17},{17,9},{25,1},{2,26},{10... | collective-permute-start | bytes 3047432 | tf_op jit(solution)/shard_map/ppermute | solution.py:1027
  82.0 65.5 %collective-permute-start.3 = (bf16[8,496,128]{2,1,0:T(8,128)(2,1)}, bf16[8,496,128]{2,1,0:T(8,128)(2,1)}, u32[]{:S(2)}, u32[]{:S(2)}) collective-permute-start(bf16[8,496,128]{2,1,0:T(8,128)(2,1)} %get-tuple-element.80.more_0_), channel_id=1, source_target_pairs={{0,8},{8,0},{16,24},{24,16},{1,9},{9,1},{17,25},{25,17},{2,10},{10... | collective-permute-start | bytes 3047432 | tf_op jit(solution)/shard_map/ppermute | solution.py:1027
  82.4 65.2 %collective-permute-start.2 = (bf16[8,496,128]{2,1,0:T(8,128)(2,1)}, bf16[8,496,128]{2,1,0:T(8,128)(2,1)}, u32[]{:S(2)}, u32[]{:S(2)}) collective-permute-start(bf16[8,496,128]{2,1,0:T(8,128)(2,1)} %get-tuple-element.80.more_0_), channel_id=1, source_target_pairs={{0,16},{8,24},{16,0},{24,8},{1,17},{9,25},{17,1},{25,9},{2,18},{10... | collective-permute-start | bytes 3047432 | tf_op jit(solution)/shard_map/ppermute | solution.py:1027
  83.9 4.7 %copy-start.5 = (s32[16]{0:T(128)S(1)}, s32[16]{0:T(128)}, u32[]{:S(2)}) copy-start(s32[16]{0:T(128)} %param.13) | copy-start | bytes 196
  83.9 6.1 %copy-start.3 = (bf16[576]{0:T(1024)(128)(2,1)S(1)}, bf16[576]{0:T(1024)(128)(2,1)}, u32[]{:S(2)}) copy-start(bf16[576]{0:T(1024)(128)(2,1)} %param.14) | copy-start | bytes 3460
  83.9 64.7 %all-to-all-start = ((bf16[8,576,256]{2,1,0:T(8,128)(2,1)}), bf16[8,576,256]{2,1,0:T(8,128)(2,1)S(1)}, u32[]{:S(2)}, u32[]{:S(2)}) async-start(bf16[8,576,256]{2,1,0:T(8,128)(2,1)} %bitcast.5), calls=%async_computation | async-start | bytes 4718592 | tf_op jit(solution)/shard_map/all_to_all | solution.py:1382
  104.3 41.8 %copy-start.4 = (bf16[576]{0:T(1024)(128)(2,1)S(1)}, bf16[576]{0:T(1024)(128)(2,1)}, u32[]{:S(2)}) copy-start(bf16[576]{0:T(1024)(128)(2,1)} %param.19) | copy-start | bytes 3460
  146.0 2.5 collective-permute-start.5
  147.5 1.0 copy-start.6
  148.6 1.4 copy-start
  215.0 160.9 %all-to-all-start.1 = ((bf16[8,576,256]{2,1,0:T(8,128)(2,1)}), bf16[8,576,256]{2,1,0:T(8,128)(2,1)S(1)}, u32[]{:S(2)}, u32[]{:S(2)}) async-start(bf16[8,576,256]{2,1,0:T(8,128)(2,1)} %get-tuple-element.84), calls=%async_computation.1 | async-start | bytes 4718592 | tf_op jit(solution)/shard_map/all_to_all | solution.py:1382
  221.0 23.0 %collective-permute-start.7 = (bf16[16,384,128]{2,1,0:T(8,128)(2,1)}, bf16[16,384,128]{2,1,0:T(8,128)(2,1)}, u32[]{:S(2)}, u32[]{:S(2)}) collective-permute-start(bf16[16,384,128]{2,1,0:T(8,128)(2,1)} %get-tuple-element.87), channel_id=1, source_target_pairs={{0,8},{8,0},{16,24},{24,16},{1,9},{9,1},{17,25},{25,17},{2,10},{10... | collective-permute-start | bytes 4718600 | tf_op jit(solution)/shard_map/ppermute | solution.py:1027
  221.0 23.0 %collective-permute-start.6 = (bf16[16,432,128]{2,1,0:T(8,128)(2,1)}, bf16[16,432,128]{2,1,0:T(8,128)(2,1)S(1)}, u32[]{:S(2)}, u32[]{:S(2)}) collective-permute-start(bf16[16,432,128]{2,1,0:T(8,128)(2,1)} %get-tuple-element.86), channel_id=1, source_target_pairs={{0,8},{8,0},{16,24},{24,16},{1,9},{9,1},{17,25},{25,17},{2,10},{10... | collective-permute-start | bytes 5308424 | tf_op jit(solution)/shard_map/ppermute | solution.py:1027
  221.5 22.5 %copy-start.1 = (bf16[16,432,128]{2,1,0:T(8,128)(2,1)S(1)}, bf16[16,432,128]{2,1,0:T(8,128)(2,1)}, u32[]{:S(2)}) copy-start(bf16[16,432,128]{2,1,0:T(8,128)(2,1)} %get-tuple-element.96) | copy-start | bytes 5308420
  244.1 1.4 copy-start.2
  248.2 44.3 %collective-permute-start.9 = (bf16[8,384,128]{2,1,0:T(8,128)(2,1)S(1)}, bf16[8,384,128]{2,1,0:T(8,128)(2,1)S(1)}, u32[]{:S(2)}, u32[]{:S(2)}) collective-permute-start(bf16[8,384,128]{2,1,0:T(8,128)(2,1)S(1)} %get-tuple-element.111), channel_id=1, source_target_pairs={{0,1},{1,0},{2,3},{3,2},{4,5},{5,4},{6,7},{7,6},{8,9},{9,8},{10,11... | collective-permute-start | bytes 2359304 | tf_op jit(solution)/shard_map/ppermute | solution.py:1470
  250.2 42.2 %collective-permute-start.8 = (bf16[8,432,128]{2,1,0:T(8,128)(2,1)S(1)}, bf16[8,432,128]{2,1,0:T(8,128)(2,1)S(1)}, u32[]{:S(2)}, u32[]{:S(2)}) collective-permute-start(bf16[8,432,128]{2,1,0:T(8,128)(2,1)S(1)} %get-tuple-element.110), channel_id=1, source_target_pairs={{0,16},{8,24},{16,0},{24,8},{1,17},{9,25},{17,1},{25,9},{2,18},{10... | collective-permute-start | bytes 2654216 | tf_op jit(solution)/shard_map/ppermute | solution.py:1470
  292.5 0.9 copy-start.8
  292.5 1.1 copy-start.7

commit v7 on v6

--- a/solution.py
+++ b/solution.py
@@ -2,6 +2,7 @@
 
 import jax
 import jax.numpy as jnp
+import numpy as np
 from jax import lax
 from jax.experimental import pallas as pl
 from jax.experimental.pallas import tpu as pltpu
@@ -706,13 +707,33 @@
     return peers + [(flip(my_dp, [b]), my_seq) for b in bits_of(dp)]
 
 
-def bring_kernel(x_ref, first_ref, second_ref, third_ref, out_ref, all_first, all_second, all_third,
-                 local_sem, x_send, x_recv, w_send, w_recv, *, dp, seq):
+def bring_kernel(order_ref, freq_ref, gain_one, gain_two, q_ref, k_ref, v_ref, o_ref, gate_ref, up_ref,
+                 down_ref, x_ref, inv_ref, cos_ref, sin_ref, one_ref, two_ref, out_ref,
+                 all_first, all_second, all_third, first_ref, rest_ref, local_sem, x_send, x_recv, w_send, w_recv, *, dp, seq):
     my_dp, my_seq = lax.axis_index("dp"), lax.axis_index("seq")
     orders = all_stages(dp, seq), seq_stages(seq), seq_stages(seq)
     chains = range(len(orders))
+    rows, q_cols = q_ref.shape
+    lanes = rest_ref.shape[2]
+    kv_cols = k_ref.shape[0]
+    blank = lambda cols: jnp.zeros((rows, cols), F32)
+    wide = lambda ref: ref[...].astype(F32)
+    first_ref[0] = jnp.concatenate(
+        [wide(q_ref), wide(k_ref).T, wide(v_ref).T, blank(lanes - q_cols - 2 * kv_cols)], axis=1
+    ).astype(BF16)
+    rest_ref[0, :rows] = jnp.concatenate([wide(o_ref), blank(lanes - q_cols)], axis=1).astype(BF16)
+    rest_ref[0, rows : 2 * rows] = gate_ref[:, :lanes]
+    rest_ref[0, 2 * rows : 3 * rows] = up_ref[:, :lanes]
+    rest_ref[0, 3 * rows : 4 * rows] = jnp.concatenate([gate_ref[:, lanes:], up_ref[:, lanes:]], axis=1)
+    padded = -(-q_cols // 16) * 16
+    for t in range(down_ref.shape[1] // lanes):
+        piece = down_ref[:, t * lanes : (t + 1) * lanes].astype(F32)
+        piece = jnp.concatenate([piece, jnp.zeros((padded - q_cols, lanes), F32)], axis=0).astype(BF16)
+        rest_ref[0, 4 * rows + padded * t : 4 * rows + padded * (t + 1)] = piece
+
     greet(all_peers(my_dp, my_seq, dp, seq))
-    shards_in = first_ref, second_ref, third_ref
+    at = all_second.shape[1]
+    shards_in = first_ref, rest_ref.at[:, pl.ds(0, at)], rest_ref.at[:, pl.ds(at, all_third.shape[1])]
     gathered = all_first, all_second, all_third
 
     def weight_copy(chain, stage):
@@ -759,6 +780,20 @@
         if stage == 1:
             for move in moves:
                 move.start()
+            spans = order_ref.shape[0]
+            span = cos_ref.shape[1] // spans
+            inside = lax.broadcasted_iota(jnp.int32, (1, span), 1)
+            for slot in range(spans):
+                angles = (inside + order_ref[slot] * span).astype(F32) * freq_ref[...]
+                cos_ref[:, slot * span : (slot + 1) * span] = jnp.cos(angles)
+                sin_ref[:, slot * span : (slot + 1) * span] = jnp.sin(angles)
+                found = 0
+                for other in range(spans):
+                    found = found + jnp.where(order_ref[other] == slot, other, 0)
+                inv_ref[slot] = found
+            for source, target in ((gain_one, one_ref), (gain_two, two_ref)):
+                row = source[...].astype(F32)[None]
+                target[...] = jnp.broadcast_to(row, (8, row.shape[1])).T[:, :1]
     for c in chains:
         copies[c][-1].wait_recv()
         for copy in copies[c]:
@@ -768,21 +803,36 @@
     own[-1].wait()
 
 
-def bring(x, first, second, third):
+def bring(span_order, inv_freq, gains, weights, x):
     dp, seq = lax.axis_size("dp"), lax.axis_size("seq")
     stages = len(all_stages(dp, seq))
+    lanes = 128
+    width = x.shape[1]
+    rows, q_cols = weights[0].shape
+    rest_rows = 4 * rows + -(-q_cols // 16) * 16 * (weights[-1].shape[1] // lanes)
+    cut = rest_rows * 5 // 8 // 16 * 16
     hbm = pl.BlockSpec(memory_space=pl.ANY)
+    smem = pl.BlockSpec(memory_space=pltpu.SMEM)
+    vmem = pl.BlockSpec(memory_space=pltpu.VMEM)
+    table = jax.ShapeDtypeStruct((inv_freq.shape[0], x.shape[0] * x.shape[2]), F32)
     return pl.pallas_call(
         functools.partial(bring_kernel, dp=dp, seq=seq),
-        in_specs=[hbm] * 4,
-        out_specs=[hbm] * 4,
+        in_specs=[smem] + [vmem] * (3 + len(weights)) + [hbm],
+        out_specs=[smem] + [vmem] * 4 + [hbm] * 4,
         out_shape=[
+            jax.ShapeDtypeStruct(span_order.shape, jnp.int32),
+            table,
+            table,
+            jax.ShapeDtypeStruct((width, 1), F32),
+            jax.ShapeDtypeStruct((width, 1), F32),
             jax.ShapeDtypeStruct(x.shape, x.dtype),
-            jax.ShapeDtypeStruct((dp * seq, *first.shape[1:]), first.dtype),
-            jax.ShapeDtypeStruct((seq, *second.shape[1:]), second.dtype),
-            jax.ShapeDtypeStruct((seq, *third.shape[1:]), third.dtype),
+            jax.ShapeDtypeStruct((dp * seq, rows, lanes), x.dtype),
+            jax.ShapeDtypeStruct((seq, cut, lanes), x.dtype),
+            jax.ShapeDtypeStruct((seq, rest_rows - cut, lanes), x.dtype),
         ],
         scratch_shapes=[
+            pltpu.VMEM((1, rows, lanes), BF16),
+            pltpu.VMEM((1, rest_rows, lanes), BF16),
             pltpu.SemaphoreType.DMA((4,)),
             pltpu.SemaphoreType.DMA((seq - 1,)),
             pltpu.SemaphoreType.DMA((seq - 1,)),
@@ -793,7 +843,7 @@
             collective_id=1, has_side_effects=True, vmem_limit_bytes=VMEM_BYTES
         ),
         name="bring",
-    )(x, first, second, third)
+    )(span_order, inv_freq, *gains, *weights, x)
 
 
 def qkv_kernel(where_ref, x_ref, gain_ref, packed_ref, cos_ref, sin_ref,
@@ -918,11 +968,11 @@
             at = where_ref[s]
             stack = lambda first: jnp.concatenate(
                 [pack[d, at, first : first + rows, :] for d in range(dp)], axis=0
-            ).astype(F32).T
-            o_sum[o_cols * s : o_cols * s + o_cols, :] = stack(0)[:o_cols]
-            gate_t[ff_cols * s : ff_cols * s + lanes, :] = stack(rows).astype(BF16)
-            up_t[ff_cols * s : ff_cols * s + lanes, :] = stack(2 * rows).astype(BF16)
-            both = stack(3 * rows).astype(BF16)
+            )
+            o_sum[o_cols * s : o_cols * s + o_cols, :] = stack(0).astype(F32).T[:o_cols]
+            gate_t[ff_cols * s : ff_cols * s + lanes, :] = stack(rows).T
+            up_t[ff_cols * s : ff_cols * s + lanes, :] = stack(2 * rows).T
+            both = stack(3 * rows).T
             gate_t[ff_cols * s + lanes : ff_cols * (s + 1), :] = both[:spare]
             up_t[ff_cols * s + lanes : ff_cols * (s + 1), :] = both[spare : 2 * spare]
             for d in range(dp):
@@ -931,14 +981,22 @@
                     piece = pack[d, at, first : first + padded, :].astype(F32)[:o_cols]
                     cols = slice(ff_rows * d + lanes * t, ff_rows * d + lanes * (t + 1))
                     down_sum[o_cols * s : o_cols * s + o_cols, cols] = piece
+        for s in range(0, seq, 2):
+            for d in range(dp):
+                halves = [pack[d, where_ref[s + i], 3 * rows : 4 * rows, :] for i in range(2)]
+                for matrix, first, cut in ((gate_w, rows, 0), (up_w, 2 * rows, spare)):
+                    pieces = []
+                    for i in range(2):
+                        pieces.append(pack[d, where_ref[s + i], first : first + rows, :])
+                        pieces.append(halves[i][:, cut : cut + spare])
+                    cols = slice(ff_cols * s, ff_cols * (s + 2))
+                    matrix[rows * d : rows * (d + 1), cols] = jnp.concatenate(pieces, axis=1)
         o_t[...] = o_sum[...].astype(BF16)
         o_w[...] = o_sum[...].T.astype(BF16)
         down_t[...] = down_sum[...].astype(BF16)
         for first in range(0, ff, lanes):
             part = slice(first, first + lanes)
-            down_w[part, :] = down_sum[:, part].T.astype(BF16)
-            gate_w[:, part] = gate_t[part, :].T
-            up_w[:, part] = up_t[part, :].T
+            down_w[part, :] = down_t[:, part].T
         o_sum[...] = jnp.zeros_like(o_sum)
         down_sum[...] = jnp.zeros_like(down_sum)
 
@@ -964,8 +1022,8 @@
         dnormed += dot(gate_w[:, part], dgate, 1, 0)
         dnormed += dot(up_w[:, part], dup, 1, 0)
         down_sum[:, part] += dot(dy, inner, 1, 1)
-        gate_sum[part, :] += dot(dgate, normed, 1, 1)
-        up_sum[part, :] += dot(dup, normed, 1, 1)
+        gate_sum[:, part] += dot(normed, dgate, 1, 1)
+        up_sum[:, part] += dot(normed, dup, 1, 1)
     out = (mid + added).astype(BF16)
     scaled_mid = mid * rstd
     product = dnormed * scaled_mid
@@ -996,19 +1054,19 @@
         blank = jnp.zeros((lanes - o_cols, width), F32)
         edge = jnp.zeros((padded - o_cols, lanes), F32)
         for s in range(seq):
-            tall = lambda total, first, count: total[first : first + count, :]
-            o_piece = jnp.concatenate([tall(o_sum, o_cols * s, o_cols), blank], axis=0).T
-            gate_piece = tall(gate_sum, ff_cols * s, lanes).T
-            up_piece = tall(up_sum, ff_cols * s, lanes).T
-            both = jnp.concatenate(
-                [tall(gate_sum, ff_cols * s + lanes, spare), tall(up_sum, ff_cols * s + lanes, spare)], axis=0
-            ).T
+            o_piece = jnp.concatenate([o_sum[o_cols * s : o_cols * (s + 1), :], blank], axis=0).T
+            pair_cols = slice(ff_cols * (s - s % 2), ff_cols * (s - s % 2 + 2))
+            shift = ff_cols * (s % 2)
             for d in range(0, dp, 2):
                 bands = slice(rows * d, rows * (d + 1)), slice(rows * (d + 1), rows * (d + 2))
                 one, two = [away_place(c, d, s, my_dp, my_seq) for c in rest_chains(dp, seq)]
-                for i, piece in enumerate((o_piece, gate_piece, up_piece)):
-                    put(one_refs, one, rows * i, piece[bands[0]], piece[bands[1]])
-                put(two_refs, two, 0, both[bands[0]], both[bands[1]])
+                put(one_refs, one, 0, o_piece[bands[0]], o_piece[bands[1]])
+                rests = []
+                for i, total in enumerate((gate_sum, up_sum)):
+                    wide = [total[band, pair_cols] for band in bands]
+                    put(one_refs, one, rows * (i + 1), *[w[:, shift : shift + lanes] for w in wide])
+                    rests.append([w[:, shift + lanes : shift + ff_cols] for w in wide])
+                put(two_refs, two, 0, *[jnp.concatenate([g, u], axis=1) for g, u in zip(*rests)])
                 for t in range(ff_rows // lanes):
                     pair = []
                     for at in (d, d + 1):
@@ -1027,7 +1085,7 @@
     return lax.ppermute(array, "dp", [(i, i ^ mask) for i in range(lax.axis_size("dp"))])
 
 
-def mlp_both(where, x, mixed, dy, gain, packs, ff, batch=2, chunk=512):
+def mlp_both(where, x, mixed, dy, gain, packs, ff, batch=2, chunk=768):
     blocks, width, block = x.shape
     tokens = blocks * block
     dp, seq = lax.axis_size("dp"), lax.axis_size("seq")
@@ -1058,8 +1116,8 @@
                 pltpu.VMEM((ff, width), BF16),
                 pltpu.VMEM((width, ff), BF16),
                 pltpu.VMEM((width, width), F32),
-                pltpu.VMEM((ff, width), F32),
-                pltpu.VMEM((ff, width), F32),
+                pltpu.VMEM((width, ff), F32),
+                pltpu.VMEM((width, ff), F32),
                 pltpu.VMEM((width, ff), F32),
                 pltpu.VMEM((width, lanes), F32),
                 pltpu.VMEM((dp, packs[0].shape[0], grad_rows, lanes), BF16),
@@ -1382,10 +1440,6 @@
     return lax.all_to_all(blocks, "seq", 0, 0, tiled=True)
 
 
-def pad_lanes(matrix, lanes):
-    return jnp.pad(matrix, ((0, 0), (0, lanes - matrix.shape[1])))
-
-
 def shards_sequences(
     hidden_in, span_order, attn_gain, q_weight, k_weight, v_weight, o_weight, mlp_gain,
     gate_weight, up_weight, down_weight, out_grad,
@@ -1403,21 +1457,13 @@
     ff_rows = down_weight.shape[0]
     padded = -(-q_cols // 16) * 16
 
-    first = pad_lanes(jnp.concatenate([q_weight, k_weight, v_weight], axis=1), lanes)
-    down_turned = jnp.pad(down_weight.T, ((0, padded - q_cols), (0, 0)))
-    second = jnp.concatenate(
-        [
-            pad_lanes(o_weight, lanes),
-            gate_weight[:, :lanes],
-            up_weight[:, :lanes],
-            jnp.concatenate([gate_weight[:, lanes:], up_weight[:, lanes:]], axis=1),
-        ]
-        + [down_turned[:, c : c + lanes] for c in range(0, ff_rows, lanes)],
-        axis=0,
-    )
-    at = second.shape[0] * 5 // 8 // 16 * 16
-    x, first_all, straight, hopping = bring(
-        hidden_in.transpose(0, 2, 1), first[None], second[None, :at], second[None, at:]
+    inv_freq = np.float32(rope_base ** (-2.0 * np.arange(HD // 2) / HD))
+    inv, cos_t, sin_t, gain_one, gain_two, x, first_all, straight, hopping = bring(
+        span_order,
+        inv_freq[:, None],
+        (attn_gain, mlp_gain),
+        (q_weight, k_weight.T, v_weight.T, o_weight, gate_weight, up_weight, down_weight.T),
+        hidden_in.transpose(0, 2, 1),
     )
     out_grad, x = lax.optimization_barrier((out_grad, x))
     masks = [sum(row_bits(i, dp)) for i in range(dp)]
@@ -1428,14 +1474,6 @@
     my_dp, my_seq = lax.axis_index("dp"), lax.axis_index("seq")
     where_first = arrival_order(all_stages(dp, seq), dp, seq, my_dp, my_seq)
     where_second = arrival_order(seq_stages(seq), dp, seq, my_dp, my_seq)[:seq]
-    inv = jnp.argsort(span_order).astype(jnp.int32)
-    slot_pos = slot_positions(jnp.arange(tokens, dtype=jnp.int32), span_order, span)
-    inv_freq = rope_base ** (-(jnp.arange(HD // 2, dtype=F32) * 2.0) / HD)
-    angles = slot_pos.astype(F32)[None, :] * inv_freq[:, None]
-    cos_t, sin_t = jnp.cos(angles), jnp.sin(angles)
-    gain_one = attn_gain.astype(F32)[:, None]
-    gain_two = mlp_gain.astype(F32)[:, None]
-
     q_t, k_t, v_t, k_nat, v_nat, w_t = project_qkv(
         where_first, x, gain_one, first_all, cos_t, sin_t, heads, kv_heads, rows
     )

time: 378 us -> 363 us (0.960)
  local copies, waits for them, and re-layouts: 11.2 us -> 3.99 us
  other arithmetic: 12 us -> 5.11 us
  Pallas kernels: 335 us -> 331 us
    slice x5 -> x0, local copies, waits for them, and re-layouts: 3.85 us -> none  [the longest x1 0.77 us: shards_sequences(): gate_weight[:, lanes:]]
  transfers between devices with their start and end apart: 12 -> 12, of which waited for: 1 -> 1; matrix products, arithmetic and copies ran while one was open for 3% -> 1% of each run, Pallas kernels for 53% -> 55%
where the time goes in v7:
time: 363 us; the launch traced here: 362 us
  Pallas kernels  331 us (91%)
  starting transfers between devices  19.3 us (5%)
  other arithmetic  5.11 us (1%)
  local copies, waits for them, and re-layouts  3.99 us (1%)
    pallas_call x1, Pallas kernels, finish(): pl.pallas_call(functools.partial(finish_kernel, dp=dp, seq=seq, kv_width=...  77.4 us
    pallas_call x1, Pallas kernels, bring(): pl.pallas_call(functools.partial(bring_kernel, dp=dp, seq=seq), in_specs=...  69.8 us
    pallas_call x2, Pallas kernels, attention_backward(): pl.pallas_call(functools.partial(attend_back_kernel, blocks=tokens // (2...  64.2 us
    pallas_call x1, Pallas kernels, mlp_both(): pl.pallas_call(functools.partial(mlp_kernel, chunk=chunk, dp=dp, seq=seq)...  62.1 us
    pallas_call x1, Pallas kernels, attention_forward(): pl.pallas_call(functools.partial(attend_kernel, blocks=tokens // (2 * spa...  41.7 us
    all_to_all x2, starting transfers between devices, exchange(): return lax.all_to_all(blocks, 'seq', 0, 0, tiled=True)  12.5 us
    pallas_call x1, Pallas kernels, project_qkv(): pl.pallas_call(functools.partial(qkv_kernel, heads=heads, kv_heads=kv_hea...  11.2 us
  transfers between devices with their start and end apart: 12, of which 1 were waited for; matrix products, arithmetic and copies ran while one was open for 1% of the time, Pallas kernels for 55%

profile of v7, /device:TPU:0, one launch (start us, length us, event | category | flops | bytes accessed | tf_op | source)
XLA Modules:
  0.0 362.4 jit_solution(2391918022355324524)
XLA Ops:
  0.6 69.8 %bring.1 = (s32[16]{0:T(128)}, f32[32,2048]{1,0:T(8,128)}, f32[32,2048]{1,0:T(8,128)}, f32[576,1]{1,0:T(8,128)}, f32[576,1]{1,0:T(8,128)}, /*index=5*/bf16[8,576...) custom-call(s32[16]{0:T(128)} %order_ref.1, ...), custom_call_target="tpu_custom_call" | custom-call | tf_op jit(solution)/shard_map/bring/pallas_call | solution.py:818
  70.5 1.6 collective-permute-start
  72.4 0.3 collective-permute-start.3
  72.8 1.5 collective-permute-start.2
  74.2 6.4 %all-to-all-start = ((bf16[8,576,256]{2,1,0:T(8,128)(2,1)}), bf16[8,576,256]{2,1,0:T(8,128)(2,1)S(1)}, u32[]{:S(2)}, u32[]{:S(2)}) async-start(bf16[8,576,256]{2,1,0:T(8,128)(2,1)} %bitcast.4), calls=%async_computation | async-start | bytes 4718592 | tf_op jit(solution)/shard_map/all_to_all | solution.py:1440
  80.7 0.5 fusion.8.where_ref
  81.2 11.2 %project_qkv.1 = (bf16[576,2048]{1,0:T(8,128)(2,1)}, bf16[192,2048]{1,0:T(8,128)(2,1)}, bf16[192,2048]{1,0:T(8,128)(2,1)}, bf16[3,2048,64]{2,1,0:T(8,128)(2,1)},...) custom-call(s32[32]{0:T(128)} %fusion.8.where_ref, bf16[8,576,256]{2,1,0:T(8,128)(2,1)} %get-tuple-element.74.x_ref, ...), custom_call_target="tpu_custom_call" | custom-call | flops 4529848320 | bytes 10240000 | tf_op jit(solution)/shard_map/project_qkv/pallas_call | solution.py:897
  92.5 41.7 %attention_forward.1 = (bf16[576,2048]{1,0:T(8,128)(2,1)}, f32[3,8,2048]{2,1,0:T(8,128)}) custom-call(s32[16]{0:T(128)} %get-tuple-element.76.inv_ref, bf16[576,2048]{1,0:T(8,128)(2,1)} %get-tuple-element.108.q_ref, bf16[3,2048,64]{2,1,0:T(8,128)(2,1)} %get-tuple-element.82.k_ref, bf16[192,2048]{1,0:T(8,128)(2,1)} %get-tuple-element.83.v_ref), custom_call_target="tpu_custom_call" | custom-call | flops 38654705664 | bytes 12288000 | tf_op jit(solution)/shard_map/attention_forward/pallas_call | solution.py:471
  134.2 0.5 fusion.1
  134.8 1.9 collective-permute-done.5.more_7_
  136.6 1.4 copy-done
  138.0 62.1 %mlp_both.1 = (bf16[8,576,256]{2,1,0:T(8,128)(2,1)}, f32[8,576,256]{2,1,0:T(8,128)}, bf16[576,2048]{1,0:T(8,128)(2,1)}, bf16[16,432,128]{2,1,0:T(8,128)(2,1)}, b...) custom-call(s32[8]{0:T(128)} %bitcast.20, ...), custom_call_target="tpu_custom_call" | custom-call | flops 36691771392 | bytes 16515072 | tf_op jit(solution)/shard_map/mlp_both/pallas_call | solution.py:1102
  200.1 6.0 %all-to-all-start.1 = ((bf16[8,576,256]{2,1,0:T(8,128)(2,1)}), bf16[8,576,256]{2,1,0:T(8,128)(2,1)S(1)}, u32[]{:S(2)}, u32[]{:S(2)}) async-start(bf16[8,576,256]{2,1,0:T(8,128)(2,1)} %get-tuple-element.92), calls=%async_computation.1 | async-start | bytes 4718592 | tf_op jit(solution)/shard_map/all_to_all | solution.py:1440
  206.1 0.5 collective-permute-start.6
  206.6 22.5 %attention_backward.2 = (bf16[192,2048]{1,0:T(8,128)(2,1)}, bf16[64,2048]{1,0:T(8,128)(2,1)}, bf16[64,2048]{1,0:T(8,128)(2,1)}) custom-call(s32[16]{0:T(128)} %get-tuple-element.76.inv_ref, bf16[576,2048]{1,0:T(8,128)(2,1)} %get-tuple-element.108.q_ref, bf16[192,2048]{1,0:T(8,128)(2,1)} %get-tuple-element.96.kt_ref, ...), custom_call_target="tpu_custom_call" | custom-call | flops 25769803776 | bytes 18432000 | tf_op jit(solution)/shard_map/attention_backward/pallas_call | solution.py:614
  229.2 1.4 add_convert_fusion
  230.6 2.7 add_convert_fusion.2
  233.3 2.0 collective-permute-start.9
  235.3 0.5 collective-permute-start.8
  235.8 41.7 %attention_backward.3 = (bf16[384,2048]{1,0:T(8,128)(2,1)}, bf16[128,2048]{1,0:T(8,128)(2,1)}, bf16[128,2048]{1,0:T(8,128)(2,1)}) custom-call(s32[16]{0:T(128)} %get-tuple-element.76.inv_ref, bf16[576,2048]{1,0:T(8,128)(2,1)} %get-tuple-element.108.q_ref, bf16[192,2048]{1,0:T(8,128)(2,1)} %get-tuple-element.96.kt_ref, ...), custom_call_target="tpu_custom_call" | custom-call | flops 51539607552 | bytes 18432000 | tf_op jit(solution)/shard_map/attention_backward/pallas_call | solution.py:614
  277.5 0.9 copy-done.5
  278.6 77.4 %finish.1 = (bf16[8,576,256]{2,1,0:T(8,128)(2,1)}, f32[8,576]{1,0:T(8,128)}, f32[144,128]{1,0:T(8,128)}, f32[432,128]{1,0:T(8,128)}, f32[384,128]{1,0:T(8,128)}) custom-call(bf16[8,576,256]{2,1,0:T(8,128)(2,1)} %get-tuple-element.74.x_ref, f32[8,576,256]{2,1,0:T(8,128)} %get-tuple-element.93.dmid_ref, bf16[192,2048]{1,0:T(8,128)(2,1)} %get-tuple-element.103.dq_one, ...), custom_call_target="tpu_custom_call" | custom-call | flops 4529848320 | bytes 14155776 | tf_op jit(solution)/shard_map/finish/pallas_call | solution.py:1344
  356.1 4.9 %deliver.1 = (f32[8,576,256]{2,1,0:T(8,128)}, f32[576]{0:T(1024)}, f32[576]{0:T(1024)}, f32[144,72]{1,0:T(8,128)}, f32[24,144]{1,0:T(8,128)}, /*index=5*/f32[24,...) custom-call(bf16[8,576,256]{2,1,0:T(8,128)(2,1)} %get-tuple-element.120.din_ref, ...), custom_call_target="tpu_custom_call" | custom-call | tf_op jit(solution)/shard_map/deliver/pallas_call | solution.py:1428
  361.0 1.4 copy.25
  (25 shorter events, 0.8 us)
Async XLA Ops:
  70.5 63.6 %collective-permute-start.1 = (bf16[8,320,128]{2,1,0:T(8,128)(2,1)}, bf16[8,320,128]{2,1,0:T(8,128)(2,1)}, u32[]{:S(2)}, u32[]{:S(2)}) collective-permute-start(bf16[8,320,128]{2,1,0:T(8,128)(2,1)} %get-tuple-element.89.more_1_), channel_id=1, source_target_pairs={{0,8},{8,0},{16,24},{24,16},{1,9},{9,1},{17,25},{25,17},{2,10},{10... | collective-permute-start | bytes 1966088 | tf_op jit(solution)/shard_map/ppermute | solution.py:1085
  70.5 63.6 %collective-permute-start = (bf16[8,320,128]{2,1,0:T(8,128)(2,1)}, bf16[8,320,128]{2,1,0:T(8,128)(2,1)}, u32[]{:S(2)}, u32[]{:S(2)}) collective-permute-start(bf16[8,320,128]{2,1,0:T(8,128)(2,1)} %get-tuple-element.89.more_1_), channel_id=1, source_target_pairs={{0,16},{8,24},{16,0},{24,8},{1,17},{9,25},{17,1},{25,9},{2,18},{10... | collective-permute-start | bytes 1966088 | tf_op jit(solution)/shard_map/ppermute | solution.py:1085
  72.1 62.6 %collective-permute-start.4 = (bf16[8,496,128]{2,1,0:T(8,128)(2,1)}, bf16[8,496,128]{2,1,0:T(8,128)(2,1)S(1)}, u32[]{:S(2)}, u32[]{:S(2)}) collective-permute-start(bf16[8,496,128]{2,1,0:T(8,128)(2,1)} %get-tuple-element.88.more_0_), channel_id=1, source_target_pairs={{0,24},{8,16},{16,8},{24,0},{1,25},{9,17},{17,9},{25,1},{2,26},{10... | collective-permute-start | bytes 3047432 | tf_op jit(solution)/shard_map/ppermute | solution.py:1085
  72.4 62.3 %collective-permute-start.3 = (bf16[8,496,128]{2,1,0:T(8,128)(2,1)}, bf16[8,496,128]{2,1,0:T(8,128)(2,1)}, u32[]{:S(2)}, u32[]{:S(2)}) collective-permute-start(bf16[8,496,128]{2,1,0:T(8,128)(2,1)} %get-tuple-element.88.more_0_), channel_id=1, source_target_pairs={{0,8},{8,0},{16,24},{24,16},{1,9},{9,1},{17,25},{25,17},{2,10},{10... | collective-permute-start | bytes 3047432 | tf_op jit(solution)/shard_map/ppermute | solution.py:1085
  72.8 62.0 %collective-permute-start.2 = (bf16[8,496,128]{2,1,0:T(8,128)(2,1)}, bf16[8,496,128]{2,1,0:T(8,128)(2,1)}, u32[]{:S(2)}, u32[]{:S(2)}) collective-permute-start(bf16[8,496,128]{2,1,0:T(8,128)(2,1)} %get-tuple-element.88.more_0_), channel_id=1, source_target_pairs={{0,16},{8,24},{16,0},{24,8},{1,17},{9,25},{17,1},{25,9},{2,18},{10... | collective-permute-start | bytes 3047432 | tf_op jit(solution)/shard_map/ppermute | solution.py:1085
  74.2 62.4 %all-to-all-start = ((bf16[8,576,256]{2,1,0:T(8,128)(2,1)}), bf16[8,576,256]{2,1,0:T(8,128)(2,1)S(1)}, u32[]{:S(2)}, u32[]{:S(2)}) async-start(bf16[8,576,256]{2,1,0:T(8,128)(2,1)} %bitcast.4), calls=%async_computation | async-start | bytes 4718592 | tf_op jit(solution)/shard_map/all_to_all | solution.py:1440
  134.1 2.5 collective-permute-start.5
  134.7 1.9 copy-start.3
  136.6 1.4 copy-start
  200.1 160.8 %all-to-all-start.1 = ((bf16[8,576,256]{2,1,0:T(8,128)(2,1)}), bf16[8,576,256]{2,1,0:T(8,128)(2,1)S(1)}, u32[]{:S(2)}, u32[]{:S(2)}) async-start(bf16[8,576,256]{2,1,0:T(8,128)(2,1)} %get-tuple-element.92), calls=%async_computation.1 | async-start | bytes 4718592 | tf_op jit(solution)/shard_map/all_to_all | solution.py:1440
  206.1 23.0 %collective-permute-start.7 = (bf16[16,384,128]{2,1,0:T(8,128)(2,1)}, bf16[16,384,128]{2,1,0:T(8,128)(2,1)}, u32[]{:S(2)}, u32[]{:S(2)}) collective-permute-start(bf16[16,384,128]{2,1,0:T(8,128)(2,1)} %get-tuple-element.95), channel_id=1, source_target_pairs={{0,8},{8,0},{16,24},{24,16},{1,9},{9,1},{17,25},{25,17},{2,10},{10... | collective-permute-start | bytes 4718600 | tf_op jit(solution)/shard_map/ppermute | solution.py:1085
  206.1 23.0 %collective-permute-start.6 = (bf16[16,432,128]{2,1,0:T(8,128)(2,1)}, bf16[16,432,128]{2,1,0:T(8,128)(2,1)S(1)}, u32[]{:S(2)}, u32[]{:S(2)}) collective-permute-start(bf16[16,432,128]{2,1,0:T(8,128)(2,1)} %get-tuple-element.94), channel_id=1, source_target_pairs={{0,8},{8,0},{16,24},{24,16},{1,9},{9,1},{17,25},{25,17},{2,10},{10... | collective-permute-start | bytes 5308424 | tf_op jit(solution)/shard_map/ppermute | solution.py:1085
  206.6 22.5 %copy-start.1 = (bf16[16,432,128]{2,1,0:T(8,128)(2,1)S(1)}, bf16[16,432,128]{2,1,0:T(8,128)(2,1)}, u32[]{:S(2)}) copy-start(bf16[16,432,128]{2,1,0:T(8,128)(2,1)} %get-tuple-element.104) | copy-start | bytes 5308420
  229.2 1.4 copy-start.2
  233.3 44.2 %collective-permute-start.9 = (bf16[8,384,128]{2,1,0:T(8,128)(2,1)S(1)}, bf16[8,384,128]{2,1,0:T(8,128)(2,1)S(1)}, u32[]{:S(2)}, u32[]{:S(2)}) collective-permute-start(bf16[8,384,128]{2,1,0:T(8,128)(2,1)S(1)} %get-tuple-element.119), channel_id=1, source_target_pairs={{0,1},{1,0},{2,3},{3,2},{4,5},{5,4},{6,7},{7,6},{8,9},{9,8},{10,11... | collective-permute-start | bytes 2359304 | tf_op jit(solution)/shard_map/ppermute | solution.py:1508
  235.3 42.2 %collective-permute-start.8 = (bf16[8,432,128]{2,1,0:T(8,128)(2,1)S(1)}, bf16[8,432,128]{2,1,0:T(8,128)(2,1)S(1)}, u32[]{:S(2)}, u32[]{:S(2)}) collective-permute-start(bf16[8,432,128]{2,1,0:T(8,128)(2,1)S(1)} %get-tuple-element.118), channel_id=1, source_target_pairs={{0,16},{8,24},{16,0},{24,8},{1,17},{9,25},{17,1},{25,9},{2,18},{10... | collective-permute-start | bytes 2654216 | tf_op jit(solution)/shard_map/ppermute | solution.py:1508
  277.5 0.9 copy-start.5
  277.5 1.1 copy-start.4

commit v8 on v7

--- a/solution.py
+++ b/solution.py
@@ -1260,6 +1260,8 @@
 
     @pl.when(step == steps - 1)
     def _():
+        for away in range(seq // 2, seq - 2):
+            move(away).start()
         move(1).start()
         own = pltpu.make_async_copy(din.at[my_seq], out_ref.at[my_seq], own_sem)
         own.start()
@@ -1304,13 +1306,11 @@
             if turn == turns - 3:
                 for chain in (1, 2):
                     take(chain, 1)
-                for away in range(seq // 2, seq - 2):
+                for away in range(2, seq // 2):
                     move(away).start()
             if turn == turns - 2:
                 for chain in (1, 2):
                     take(chain, 2)
-                for away in range(2, seq // 2):
-                    move(away).start()
         gains_ref[...] = gain_held[turns]
         qkv_ref[...], one_ref[...], two_ref[...] = result(0), result(1), result(2)
         for copy in gain_copies:

time: 363 us -> 359 us (0.989)
    pallas_call x1, Pallas kernels: 77.4 us -> 73.7 us  [finish(): pl.pallas_call(functools.partial(finish_kernel, dp=dp, seq=seq, kv_width=...]
where the time goes in v8:
time: 359 us
  Pallas kernels  328 us (91%)
  starting transfers between devices  19.3 us (5%)
  other arithmetic  5.11 us (1%)
  local copies, waits for them, and re-layouts  3.99 us (1%)
    pallas_call x1, Pallas kernels, finish(): pl.pallas_call(functools.partial(finish_kernel, dp=dp, seq=seq, kv_width=...  73.7 us
    pallas_call x1, Pallas kernels, bring(): pl.pallas_call(functools.partial(bring_kernel, dp=dp, seq=seq), in_specs=...  69.8 us
    pallas_call x2, Pallas kernels, attention_backward(): pl.pallas_call(functools.partial(attend_back_kernel, blocks=tokens // (2...  64.2 us
    pallas_call x1, Pallas kernels, mlp_both(): pl.pallas_call(functools.partial(mlp_kernel, chunk=chunk, dp=dp, seq=seq)...  62.1 us
    pallas_call x1, Pallas kernels, attention_forward(): pl.pallas_call(functools.partial(attend_kernel, blocks=tokens // (2 * spa...  41.7 us
    all_to_all x2, starting transfers between devices, exchange(): return lax.all_to_all(blocks, 'seq', 0, 0, tiled=True)  12.5 us
    pallas_call x1, Pallas kernels, project_qkv(): pl.pallas_call(functools.partial(qkv_kernel, heads=heads, kv_heads=kv_hea...  11.2 us
  transfers between devices with their start and end apart: 12, of which 1 were waited for; matrix products, arithmetic and copies ran while one was open for 1% of the time, Pallas kernels for 55%

profile of v8, /device:TPU:0, one launch (start us, length us, event | category | flops | bytes accessed | tf_op | source)
XLA Modules:
  0.0 358.7 jit_solution(8342841464173840530)
XLA Ops:
  0.6 69.8 %bring.1 = (s32[16]{0:T(128)}, f32[32,2048]{1,0:T(8,128)}, f32[32,2048]{1,0:T(8,128)}, f32[576,1]{1,0:T(8,128)}, f32[576,1]{1,0:T(8,128)}, /*index=5*/bf16[8,576...) custom-call(s32[16]{0:T(128)} %order_ref.1, ...), custom_call_target="tpu_custom_call" | custom-call | tf_op jit(solution)/shard_map/bring/pallas_call | solution.py:818
  70.5 1.6 collective-permute-start
  72.4 0.3 collective-permute-start.3
  72.8 1.5 collective-permute-start.2
  74.2 6.4 %all-to-all-start = ((bf16[8,576,256]{2,1,0:T(8,128)(2,1)}), bf16[8,576,256]{2,1,0:T(8,128)(2,1)S(1)}, u32[]{:S(2)}, u32[]{:S(2)}) async-start(bf16[8,576,256]{2,1,0:T(8,128)(2,1)} %bitcast.4), calls=%async_computation | async-start | bytes 4718592 | tf_op jit(solution)/shard_map/all_to_all | solution.py:1440
  80.7 0.5 fusion.8.where_ref
  81.2 11.2 %project_qkv.1 = (bf16[576,2048]{1,0:T(8,128)(2,1)}, bf16[192,2048]{1,0:T(8,128)(2,1)}, bf16[192,2048]{1,0:T(8,128)(2,1)}, bf16[3,2048,64]{2,1,0:T(8,128)(2,1)},...) custom-call(s32[32]{0:T(128)} %fusion.8.where_ref, bf16[8,576,256]{2,1,0:T(8,128)(2,1)} %get-tuple-element.74.x_ref, ...), custom_call_target="tpu_custom_call" | custom-call | flops 4529848320 | bytes 10240000 | tf_op jit(solution)/shard_map/project_qkv/pallas_call | solution.py:897
  92.5 41.7 %attention_forward.1 = (bf16[576,2048]{1,0:T(8,128)(2,1)}, f32[3,8,2048]{2,1,0:T(8,128)}) custom-call(s32[16]{0:T(128)} %get-tuple-element.76.inv_ref, bf16[576,2048]{1,0:T(8,128)(2,1)} %get-tuple-element.108.q_ref, bf16[3,2048,64]{2,1,0:T(8,128)(2,1)} %get-tuple-element.82.k_ref, bf16[192,2048]{1,0:T(8,128)(2,1)} %get-tuple-element.83.v_ref), custom_call_target="tpu_custom_call" | custom-call | flops 38654705664 | bytes 12288000 | tf_op jit(solution)/shard_map/attention_forward/pallas_call | solution.py:471
  134.2 0.5 fusion.1
  134.8 1.9 collective-permute-done.5.more_7_
  136.6 1.4 copy-done
  138.0 62.1 %mlp_both.1 = (bf16[8,576,256]{2,1,0:T(8,128)(2,1)}, f32[8,576,256]{2,1,0:T(8,128)}, bf16[576,2048]{1,0:T(8,128)(2,1)}, bf16[16,432,128]{2,1,0:T(8,128)(2,1)}, b...) custom-call(s32[8]{0:T(128)} %bitcast.20, ...), custom_call_target="tpu_custom_call" | custom-call | flops 36691771392 | bytes 16515072 | tf_op jit(solution)/shard_map/mlp_both/pallas_call | solution.py:1102
  200.1 6.0 %all-to-all-start.1 = ((bf16[8,576,256]{2,1,0:T(8,128)(2,1)}), bf16[8,576,256]{2,1,0:T(8,128)(2,1)S(1)}, u32[]{:S(2)}, u32[]{:S(2)}) async-start(bf16[8,576,256]{2,1,0:T(8,128)(2,1)} %get-tuple-element.92), calls=%async_computation.1 | async-start | bytes 4718592 | tf_op jit(solution)/shard_map/all_to_all | solution.py:1440
  206.1 0.5 collective-permute-start.6
  206.6 22.5 %attention_backward.2 = (bf16[192,2048]{1,0:T(8,128)(2,1)}, bf16[64,2048]{1,0:T(8,128)(2,1)}, bf16[64,2048]{1,0:T(8,128)(2,1)}) custom-call(s32[16]{0:T(128)} %get-tuple-element.76.inv_ref, bf16[576,2048]{1,0:T(8,128)(2,1)} %get-tuple-element.108.q_ref, bf16[192,2048]{1,0:T(8,128)(2,1)} %get-tuple-element.96.kt_ref, ...), custom_call_target="tpu_custom_call" | custom-call | flops 25769803776 | bytes 18432000 | tf_op jit(solution)/shard_map/attention_backward/pallas_call | solution.py:614
  229.2 1.4 add_convert_fusion
  230.6 2.7 add_convert_fusion.2
  233.3 2.0 collective-permute-start.9
  235.3 0.5 collective-permute-start.8
  235.8 41.7 %attention_backward.3 = (bf16[384,2048]{1,0:T(8,128)(2,1)}, bf16[128,2048]{1,0:T(8,128)(2,1)}, bf16[128,2048]{1,0:T(8,128)(2,1)}) custom-call(s32[16]{0:T(128)} %get-tuple-element.76.inv_ref, bf16[576,2048]{1,0:T(8,128)(2,1)} %get-tuple-element.108.q_ref, bf16[192,2048]{1,0:T(8,128)(2,1)} %get-tuple-element.96.kt_ref, ...), custom_call_target="tpu_custom_call" | custom-call | flops 51539607552 | bytes 18432000 | tf_op jit(solution)/shard_map/attention_backward/pallas_call | solution.py:614
  277.5 0.9 copy-done.5
  278.7 73.7 %finish.1 = (bf16[8,576,256]{2,1,0:T(8,128)(2,1)}, f32[8,576]{1,0:T(8,128)}, f32[144,128]{1,0:T(8,128)}, f32[432,128]{1,0:T(8,128)}, f32[384,128]{1,0:T(8,128)}) custom-call(bf16[8,576,256]{2,1,0:T(8,128)(2,1)} %get-tuple-element.74.x_ref, f32[8,576,256]{2,1,0:T(8,128)} %get-tuple-element.93.dmid_ref, bf16[192,2048]{1,0:T(8,128)(2,1)} %get-tuple-element.103.dq_one, ...), custom_call_target="tpu_custom_call" | custom-call | flops 4529848320 | bytes 14155776 | tf_op jit(solution)/shard_map/finish/pallas_call | solution.py:1344
  352.4 4.9 %deliver.1 = (f32[8,576,256]{2,1,0:T(8,128)}, f32[576]{0:T(1024)}, f32[576]{0:T(1024)}, f32[144,72]{1,0:T(8,128)}, f32[24,144]{1,0:T(8,128)}, /*index=5*/f32[24,...) custom-call(bf16[8,576,256]{2,1,0:T(8,128)(2,1)} %get-tuple-element.120.din_ref, ...), custom_call_target="tpu_custom_call" | custom-call | tf_op jit(solution)/shard_map/deliver/pallas_call | solution.py:1428
  357.3 1.4 copy.25
  (25 shorter events, 0.8 us)
Async XLA Ops:
  70.5 63.6 %collective-permute-start.1 = (bf16[8,320,128]{2,1,0:T(8,128)(2,1)}, bf16[8,320,128]{2,1,0:T(8,128)(2,1)}, u32[]{:S(2)}, u32[]{:S(2)}) collective-permute-start(bf16[8,320,128]{2,1,0:T(8,128)(2,1)} %get-tuple-element.89.more_1_), channel_id=1, source_target_pairs={{0,8},{8,0},{16,24},{24,16},{1,9},{9,1},{17,25},{25,17},{2,10},{10... | collective-permute-start | bytes 1966088 | tf_op jit(solution)/shard_map/ppermute | solution.py:1085
  70.5 63.6 %collective-permute-start = (bf16[8,320,128]{2,1,0:T(8,128)(2,1)}, bf16[8,320,128]{2,1,0:T(8,128)(2,1)}, u32[]{:S(2)}, u32[]{:S(2)}) collective-permute-start(bf16[8,320,128]{2,1,0:T(8,128)(2,1)} %get-tuple-element.89.more_1_), channel_id=1, source_target_pairs={{0,16},{8,24},{16,0},{24,8},{1,17},{9,25},{17,1},{25,9},{2,18},{10... | collective-permute-start | bytes 1966088 | tf_op jit(solution)/shard_map/ppermute | solution.py:1085
  72.1 62.6 %collective-permute-start.4 = (bf16[8,496,128]{2,1,0:T(8,128)(2,1)}, bf16[8,496,128]{2,1,0:T(8,128)(2,1)S(1)}, u32[]{:S(2)}, u32[]{:S(2)}) collective-permute-start(bf16[8,496,128]{2,1,0:T(8,128)(2,1)} %get-tuple-element.88.more_0_), channel_id=1, source_target_pairs={{0,24},{8,16},{16,8},{24,0},{1,25},{9,17},{17,9},{25,1},{2,26},{10... | collective-permute-start | bytes 3047432 | tf_op jit(solution)/shard_map/ppermute | solution.py:1085
  72.4 62.3 %collective-permute-start.3 = (bf16[8,496,128]{2,1,0:T(8,128)(2,1)}, bf16[8,496,128]{2,1,0:T(8,128)(2,1)}, u32[]{:S(2)}, u32[]{:S(2)}) collective-permute-start(bf16[8,496,128]{2,1,0:T(8,128)(2,1)} %get-tuple-element.88.more_0_), channel_id=1, source_target_pairs={{0,8},{8,0},{16,24},{24,16},{1,9},{9,1},{17,25},{25,17},{2,10},{10... | collective-permute-start | bytes 3047432 | tf_op jit(solution)/shard_map/ppermute | solution.py:1085
  72.8 62.0 %collective-permute-start.2 = (bf16[8,496,128]{2,1,0:T(8,128)(2,1)}, bf16[8,496,128]{2,1,0:T(8,128)(2,1)}, u32[]{:S(2)}, u32[]{:S(2)}) collective-permute-start(bf16[8,496,128]{2,1,0:T(8,128)(2,1)} %get-tuple-element.88.more_0_), channel_id=1, source_target_pairs={{0,16},{8,24},{16,0},{24,8},{1,17},{9,25},{17,1},{25,9},{2,18},{10... | collective-permute-start | bytes 3047432 | tf_op jit(solution)/shard_map/ppermute | solution.py:1085
  74.2 62.4 %all-to-all-start = ((bf16[8,576,256]{2,1,0:T(8,128)(2,1)}), bf16[8,576,256]{2,1,0:T(8,128)(2,1)S(1)}, u32[]{:S(2)}, u32[]{:S(2)}) async-start(bf16[8,576,256]{2,1,0:T(8,128)(2,1)} %bitcast.4), calls=%async_computation | async-start | bytes 4718592 | tf_op jit(solution)/shard_map/all_to_all | solution.py:1440
  134.1 2.5 collective-permute-start.5
  134.7 1.9 copy-start.3
  136.6 1.4 copy-start
  200.1 157.2 %all-to-all-start.1 = ((bf16[8,576,256]{2,1,0:T(8,128)(2,1)}), bf16[8,576,256]{2,1,0:T(8,128)(2,1)S(1)}, u32[]{:S(2)}, u32[]{:S(2)}) async-start(bf16[8,576,256]{2,1,0:T(8,128)(2,1)} %get-tuple-element.92), calls=%async_computation.1 | async-start | bytes 4718592 | tf_op jit(solution)/shard_map/all_to_all | solution.py:1440
  206.1 23.0 %collective-permute-start.7 = (bf16[16,384,128]{2,1,0:T(8,128)(2,1)}, bf16[16,384,128]{2,1,0:T(8,128)(2,1)}, u32[]{:S(2)}, u32[]{:S(2)}) collective-permute-start(bf16[16,384,128]{2,1,0:T(8,128)(2,1)} %get-tuple-element.95), channel_id=1, source_target_pairs={{0,8},{8,0},{16,24},{24,16},{1,9},{9,1},{17,25},{25,17},{2,10},{10... | collective-permute-start | bytes 4718600 | tf_op jit(solution)/shard_map/ppermute | solution.py:1085
  206.1 23.0 %collective-permute-start.6 = (bf16[16,432,128]{2,1,0:T(8,128)(2,1)}, bf16[16,432,128]{2,1,0:T(8,128)(2,1)S(1)}, u32[]{:S(2)}, u32[]{:S(2)}) collective-permute-start(bf16[16,432,128]{2,1,0:T(8,128)(2,1)} %get-tuple-element.94), channel_id=1, source_target_pairs={{0,8},{8,0},{16,24},{24,16},{1,9},{9,1},{17,25},{25,17},{2,10},{10... | collective-permute-start | bytes 5308424 | tf_op jit(solution)/shard_map/ppermute | solution.py:1085
  206.6 22.5 %copy-start.1 = (bf16[16,432,128]{2,1,0:T(8,128)(2,1)S(1)}, bf16[16,432,128]{2,1,0:T(8,128)(2,1)}, u32[]{:S(2)}) copy-start(bf16[16,432,128]{2,1,0:T(8,128)(2,1)} %get-tuple-element.104) | copy-start | bytes 5308420
  229.2 1.4 copy-start.2
  233.3 44.2 %collective-permute-start.9 = (bf16[8,384,128]{2,1,0:T(8,128)(2,1)S(1)}, bf16[8,384,128]{2,1,0:T(8,128)(2,1)S(1)}, u32[]{:S(2)}, u32[]{:S(2)}) collective-permute-start(bf16[8,384,128]{2,1,0:T(8,128)(2,1)S(1)} %get-tuple-element.119), channel_id=1, source_target_pairs={{0,1},{1,0},{2,3},{3,2},{4,5},{5,4},{6,7},{7,6},{8,9},{9,8},{10,11... | collective-permute-start | bytes 2359304 | tf_op jit(solution)/shard_map/ppermute | solution.py:1508
  235.3 42.2 %collective-permute-start.8 = (bf16[8,432,128]{2,1,0:T(8,128)(2,1)S(1)}, bf16[8,432,128]{2,1,0:T(8,128)(2,1)S(1)}, u32[]{:S(2)}, u32[]{:S(2)}) collective-permute-start(bf16[8,432,128]{2,1,0:T(8,128)(2,1)S(1)} %get-tuple-element.118), channel_id=1, source_target_pairs={{0,16},{8,24},{16,0},{24,8},{1,17},{9,25},{17,1},{25,9},{2,18},{10... | collective-permute-start | bytes 2654216 | tf_op jit(solution)/shard_map/ppermute | solution.py:1508
  277.5 0.9 copy-start.5
  277.5 1.1 copy-start.4

commit v9 on v8

--- a/solution.py
+++ b/solution.py
@@ -1303,12 +1303,12 @@
             if turn + 1 < turns:
                 gain_copies[turn + 1].start()
             take(0, turn)
-            if turn == turns - 3:
+            if turn == turns - 4:
                 for chain in (1, 2):
                     take(chain, 1)
                 for away in range(2, seq // 2):
                     move(away).start()
-            if turn == turns - 2:
+            if turn == turns - 3:
                 for chain in (1, 2):
                     take(chain, 2)
         gains_ref[...] = gain_held[turns]

time: 359 us -> 359 us (level)
  no operation moved by 1% of the time
where the time goes in v9:
time: 359 us
  Pallas kernels  327 us (91%)
  starting transfers between devices  19.3 us (5%)
  other arithmetic  5.11 us (1%)
  local copies, waits for them, and re-layouts  3.99 us (1%)
    pallas_call x1, Pallas kernels, finish(): pl.pallas_call(functools.partial(finish_kernel, dp=dp, seq=seq, kv_width=...  73.7 us
    pallas_call x1, Pallas kernels, bring(): pl.pallas_call(functools.partial(bring_kernel, dp=dp, seq=seq), in_specs=...  69.8 us
    pallas_call x2, Pallas kernels, attention_backward(): pl.pallas_call(functools.partial(attend_back_kernel, blocks=tokens // (2...  64.2 us
    pallas_call x1, Pallas kernels, mlp_both(): pl.pallas_call(functools.partial(mlp_kernel, chunk=chunk, dp=dp, seq=seq)...  62.1 us
    pallas_call x1, Pallas kernels, attention_forward(): pl.pallas_call(functools.partial(attend_kernel, blocks=tokens // (2 * spa...  41.6 us
    all_to_all x2, starting transfers between devices, exchange(): return lax.all_to_all(blocks, 'seq', 0, 0, tiled=True)  12.5 us
    pallas_call x1, Pallas kernels, project_qkv(): pl.pallas_call(functools.partial(qkv_kernel, heads=heads, kv_heads=kv_hea...  11.2 us
  transfers between devices with their start and end apart: 12, of which 1 were waited for; matrix products, arithmetic and copies ran while one was open for 1% of the time, Pallas kernels for 55%

profile of v9, /device:TPU:0, one launch (start us, length us, event | category | flops | bytes accessed | tf_op | source)
XLA Modules:
  0.0 358.6 jit_solution(13515762373105789988)
XLA Ops:
  0.6 69.8 %bring.1 = (s32[16]{0:T(128)}, f32[32,2048]{1,0:T(8,128)}, f32[32,2048]{1,0:T(8,128)}, f32[576,1]{1,0:T(8,128)}, f32[576,1]{1,0:T(8,128)}, /*index=5*/bf16[8,576...) custom-call(s32[16]{0:T(128)} %order_ref.1, ...), custom_call_target="tpu_custom_call" | custom-call | tf_op jit(solution)/shard_map/bring/pallas_call | solution.py:818
  70.5 1.6 collective-permute-start
  72.4 0.3 collective-permute-start.3
  72.8 1.5 collective-permute-start.2
  74.2 6.4 %all-to-all-start = ((bf16[8,576,256]{2,1,0:T(8,128)(2,1)}), bf16[8,576,256]{2,1,0:T(8,128)(2,1)S(1)}, u32[]{:S(2)}, u32[]{:S(2)}) async-start(bf16[8,576,256]{2,1,0:T(8,128)(2,1)} %bitcast.4), calls=%async_computation | async-start | bytes 4718592 | tf_op jit(solution)/shard_map/all_to_all | solution.py:1440
  80.7 0.5 fusion.8.where_ref
  81.2 11.2 %project_qkv.1 = (bf16[576,2048]{1,0:T(8,128)(2,1)}, bf16[192,2048]{1,0:T(8,128)(2,1)}, bf16[192,2048]{1,0:T(8,128)(2,1)}, bf16[3,2048,64]{2,1,0:T(8,128)(2,1)},...) custom-call(s32[32]{0:T(128)} %fusion.8.where_ref, bf16[8,576,256]{2,1,0:T(8,128)(2,1)} %get-tuple-element.74.x_ref, ...), custom_call_target="tpu_custom_call" | custom-call | flops 4529848320 | bytes 10240000 | tf_op jit(solution)/shard_map/project_qkv/pallas_call | solution.py:897
  92.5 41.6 %attention_forward.1 = (bf16[576,2048]{1,0:T(8,128)(2,1)}, f32[3,8,2048]{2,1,0:T(8,128)}) custom-call(s32[16]{0:T(128)} %get-tuple-element.76.inv_ref, bf16[576,2048]{1,0:T(8,128)(2,1)} %get-tuple-element.108.q_ref, bf16[3,2048,64]{2,1,0:T(8,128)(2,1)} %get-tuple-element.82.k_ref, bf16[192,2048]{1,0:T(8,128)(2,1)} %get-tuple-element.83.v_ref), custom_call_target="tpu_custom_call" | custom-call | flops 38654705664 | bytes 12288000 | tf_op jit(solution)/shard_map/attention_forward/pallas_call | solution.py:471
  134.2 0.5 fusion.1
  134.7 1.9 collective-permute-done.5.more_7_
  136.6 1.4 copy-done
  138.0 62.1 %mlp_both.1 = (bf16[8,576,256]{2,1,0:T(8,128)(2,1)}, f32[8,576,256]{2,1,0:T(8,128)}, bf16[576,2048]{1,0:T(8,128)(2,1)}, bf16[16,432,128]{2,1,0:T(8,128)(2,1)}, b...) custom-call(s32[8]{0:T(128)} %bitcast.20, ...), custom_call_target="tpu_custom_call" | custom-call | flops 36691771392 | bytes 16515072 | tf_op jit(solution)/shard_map/mlp_both/pallas_call | solution.py:1102
  200.1 6.0 %all-to-all-start.1 = ((bf16[8,576,256]{2,1,0:T(8,128)(2,1)}), bf16[8,576,256]{2,1,0:T(8,128)(2,1)S(1)}, u32[]{:S(2)}, u32[]{:S(2)}) async-start(bf16[8,576,256]{2,1,0:T(8,128)(2,1)} %get-tuple-element.92), calls=%async_computation.1 | async-start | bytes 4718592 | tf_op jit(solution)/shard_map/all_to_all | solution.py:1440
  206.1 0.5 collective-permute-start.6
  206.6 22.5 %attention_backward.2 = (bf16[192,2048]{1,0:T(8,128)(2,1)}, bf16[64,2048]{1,0:T(8,128)(2,1)}, bf16[64,2048]{1,0:T(8,128)(2,1)}) custom-call(s32[16]{0:T(128)} %get-tuple-element.76.inv_ref, bf16[576,2048]{1,0:T(8,128)(2,1)} %get-tuple-element.108.q_ref, bf16[192,2048]{1,0:T(8,128)(2,1)} %get-tuple-element.96.kt_ref, ...), custom_call_target="tpu_custom_call" | custom-call | flops 25769803776 | bytes 18432000 | tf_op jit(solution)/shard_map/attention_backward/pallas_call | solution.py:614
  229.2 1.4 add_convert_fusion
  230.6 2.7 add_convert_fusion.2
  233.2 2.0 collective-permute-start.9
  235.3 0.5 collective-permute-start.8
  235.7 41.7 %attention_backward.3 = (bf16[384,2048]{1,0:T(8,128)(2,1)}, bf16[128,2048]{1,0:T(8,128)(2,1)}, bf16[128,2048]{1,0:T(8,128)(2,1)}) custom-call(s32[16]{0:T(128)} %get-tuple-element.76.inv_ref, bf16[576,2048]{1,0:T(8,128)(2,1)} %get-tuple-element.108.q_ref, bf16[192,2048]{1,0:T(8,128)(2,1)} %get-tuple-element.96.kt_ref, ...), custom_call_target="tpu_custom_call" | custom-call | flops 51539607552 | bytes 18432000 | tf_op jit(solution)/shard_map/attention_backward/pallas_call | solution.py:614
  277.5 0.9 copy-done.5
  278.6 73.7 %finish.1 = (bf16[8,576,256]{2,1,0:T(8,128)(2,1)}, f32[8,576]{1,0:T(8,128)}, f32[144,128]{1,0:T(8,128)}, f32[432,128]{1,0:T(8,128)}, f32[384,128]{1,0:T(8,128)}) custom-call(bf16[8,576,256]{2,1,0:T(8,128)(2,1)} %get-tuple-element.74.x_ref, f32[8,576,256]{2,1,0:T(8,128)} %get-tuple-element.93.dmid_ref, bf16[192,2048]{1,0:T(8,128)(2,1)} %get-tuple-element.103.dq_one, ...), custom_call_target="tpu_custom_call" | custom-call | flops 4529848320 | bytes 14155776 | tf_op jit(solution)/shard_map/finish/pallas_call | solution.py:1344
  352.3 4.9 %deliver.1 = (f32[8,576,256]{2,1,0:T(8,128)}, f32[576]{0:T(1024)}, f32[576]{0:T(1024)}, f32[144,72]{1,0:T(8,128)}, f32[24,144]{1,0:T(8,128)}, /*index=5*/f32[24,...) custom-call(bf16[8,576,256]{2,1,0:T(8,128)(2,1)} %get-tuple-element.120.din_ref, ...), custom_call_target="tpu_custom_call" | custom-call | tf_op jit(solution)/shard_map/deliver/pallas_call | solution.py:1428
  357.2 1.4 copy.25
  (25 shorter events, 0.8 us)
Async XLA Ops:
  70.5 63.6 %collective-permute-start.1 = (bf16[8,320,128]{2,1,0:T(8,128)(2,1)}, bf16[8,320,128]{2,1,0:T(8,128)(2,1)}, u32[]{:S(2)}, u32[]{:S(2)}) collective-permute-start(bf16[8,320,128]{2,1,0:T(8,128)(2,1)} %get-tuple-element.89.more_1_), channel_id=1, source_target_pairs={{0,8},{8,0},{16,24},{24,16},{1,9},{9,1},{17,25},{25,17},{2,10},{10... | collective-permute-start | bytes 1966088 | tf_op jit(solution)/shard_map/ppermute | solution.py:1085
  70.5 63.5 %collective-permute-start = (bf16[8,320,128]{2,1,0:T(8,128)(2,1)}, bf16[8,320,128]{2,1,0:T(8,128)(2,1)}, u32[]{:S(2)}, u32[]{:S(2)}) collective-permute-start(bf16[8,320,128]{2,1,0:T(8,128)(2,1)} %get-tuple-element.89.more_1_), channel_id=1, source_target_pairs={{0,16},{8,24},{16,0},{24,8},{1,17},{9,25},{17,1},{25,9},{2,18},{10... | collective-permute-start | bytes 1966088 | tf_op jit(solution)/shard_map/ppermute | solution.py:1085
  72.1 62.6 %collective-permute-start.4 = (bf16[8,496,128]{2,1,0:T(8,128)(2,1)}, bf16[8,496,128]{2,1,0:T(8,128)(2,1)S(1)}, u32[]{:S(2)}, u32[]{:S(2)}) collective-permute-start(bf16[8,496,128]{2,1,0:T(8,128)(2,1)} %get-tuple-element.88.more_0_), channel_id=1, source_target_pairs={{0,24},{8,16},{16,8},{24,0},{1,25},{9,17},{17,9},{25,1},{2,26},{10... | collective-permute-start | bytes 3047432 | tf_op jit(solution)/shard_map/ppermute | solution.py:1085
  72.4 62.3 %collective-permute-start.3 = (bf16[8,496,128]{2,1,0:T(8,128)(2,1)}, bf16[8,496,128]{2,1,0:T(8,128)(2,1)}, u32[]{:S(2)}, u32[]{:S(2)}) collective-permute-start(bf16[8,496,128]{2,1,0:T(8,128)(2,1)} %get-tuple-element.88.more_0_), channel_id=1, source_target_pairs={{0,8},{8,0},{16,24},{24,16},{1,9},{9,1},{17,25},{25,17},{2,10},{10... | collective-permute-start | bytes 3047432 | tf_op jit(solution)/shard_map/ppermute | solution.py:1085
  72.8 62.0 %collective-permute-start.2 = (bf16[8,496,128]{2,1,0:T(8,128)(2,1)}, bf16[8,496,128]{2,1,0:T(8,128)(2,1)}, u32[]{:S(2)}, u32[]{:S(2)}) collective-permute-start(bf16[8,496,128]{2,1,0:T(8,128)(2,1)} %get-tuple-element.88.more_0_), channel_id=1, source_target_pairs={{0,16},{8,24},{16,0},{24,8},{1,17},{9,25},{17,1},{25,9},{2,18},{10... | collective-permute-start | bytes 3047432 | tf_op jit(solution)/shard_map/ppermute | solution.py:1085
  74.2 62.3 %all-to-all-start = ((bf16[8,576,256]{2,1,0:T(8,128)(2,1)}), bf16[8,576,256]{2,1,0:T(8,128)(2,1)S(1)}, u32[]{:S(2)}, u32[]{:S(2)}) async-start(bf16[8,576,256]{2,1,0:T(8,128)(2,1)} %bitcast.4), calls=%async_computation | async-start | bytes 4718592 | tf_op jit(solution)/shard_map/all_to_all | solution.py:1440
  134.1 2.5 collective-permute-start.5
  134.7 1.9 copy-start.3
  136.6 1.4 copy-start
  200.1 157.1 %all-to-all-start.1 = ((bf16[8,576,256]{2,1,0:T(8,128)(2,1)}), bf16[8,576,256]{2,1,0:T(8,128)(2,1)S(1)}, u32[]{:S(2)}, u32[]{:S(2)}) async-start(bf16[8,576,256]{2,1,0:T(8,128)(2,1)} %get-tuple-element.92), calls=%async_computation.1 | async-start | bytes 4718592 | tf_op jit(solution)/shard_map/all_to_all | solution.py:1440
  206.1 23.0 %collective-permute-start.7 = (bf16[16,384,128]{2,1,0:T(8,128)(2,1)}, bf16[16,384,128]{2,1,0:T(8,128)(2,1)}, u32[]{:S(2)}, u32[]{:S(2)}) collective-permute-start(bf16[16,384,128]{2,1,0:T(8,128)(2,1)} %get-tuple-element.95), channel_id=1, source_target_pairs={{0,8},{8,0},{16,24},{24,16},{1,9},{9,1},{17,25},{25,17},{2,10},{10... | collective-permute-start | bytes 4718600 | tf_op jit(solution)/shard_map/ppermute | solution.py:1085
  206.1 23.0 %collective-permute-start.6 = (bf16[16,432,128]{2,1,0:T(8,128)(2,1)}, bf16[16,432,128]{2,1,0:T(8,128)(2,1)S(1)}, u32[]{:S(2)}, u32[]{:S(2)}) collective-permute-start(bf16[16,432,128]{2,1,0:T(8,128)(2,1)} %get-tuple-element.94), channel_id=1, source_target_pairs={{0,8},{8,0},{16,24},{24,16},{1,9},{9,1},{17,25},{25,17},{2,10},{10... | collective-permute-start | bytes 5308424 | tf_op jit(solution)/shard_map/ppermute | solution.py:1085
  206.6 22.5 %copy-start.1 = (bf16[16,432,128]{2,1,0:T(8,128)(2,1)S(1)}, bf16[16,432,128]{2,1,0:T(8,128)(2,1)}, u32[]{:S(2)}) copy-start(bf16[16,432,128]{2,1,0:T(8,128)(2,1)} %get-tuple-element.104) | copy-start | bytes 5308420
  229.1 1.4 copy-start.2
  233.2 44.2 %collective-permute-start.9 = (bf16[8,384,128]{2,1,0:T(8,128)(2,1)S(1)}, bf16[8,384,128]{2,1,0:T(8,128)(2,1)S(1)}, u32[]{:S(2)}, u32[]{:S(2)}) collective-permute-start(bf16[8,384,128]{2,1,0:T(8,128)(2,1)S(1)} %get-tuple-element.119), channel_id=1, source_target_pairs={{0,1},{1,0},{2,3},{3,2},{4,5},{5,4},{6,7},{7,6},{8,9},{9,8},{10,11... | collective-permute-start | bytes 2359304 | tf_op jit(solution)/shard_map/ppermute | solution.py:1508
  235.3 42.2 %collective-permute-start.8 = (bf16[8,432,128]{2,1,0:T(8,128)(2,1)S(1)}, bf16[8,432,128]{2,1,0:T(8,128)(2,1)S(1)}, u32[]{:S(2)}, u32[]{:S(2)}) collective-permute-start(bf16[8,432,128]{2,1,0:T(8,128)(2,1)S(1)} %get-tuple-element.118), channel_id=1, source_target_pairs={{0,16},{8,24},{16,0},{24,8},{1,17},{9,25},{17,1},{25,9},{2,18},{10... | collective-permute-start | bytes 2654216 | tf_op jit(solution)/shard_map/ppermute | solution.py:1508
  277.5 0.9 copy-start.5
  277.5 1.1 copy-start.4
